TPU v7x, 32 devices: a whole 2x2x4 slice. The times are simulated.
32 devices in a mesh: runs: 2 (over x), gx: 16 (over z, y, core).
Axes of the slice: x: 2, y: 2, z: 4, core: 2. Of those that a mesh axis runs over, the one named last changes fastest.
Arguments:
- initial: float32 [8, 512, 2048], P('runs', 'gx'), parts along dimension 0, may hold values from -3 to 3
- kappa: float32 [8, 512, 2048], P('runs', 'gx'), parts along dimension 0, may hold values from 0.3 to 1.3
- rate: float32 [8, 512, 2048], P('runs', 'gx'), parts along dimension 0, may hold values from 0.1 to 1
- writer: int32 [4, 2048, 1], P('runs', 'gx'), parts along dimension 0, may hold values from 0 to 15; in each aligned block of 128 rows (0 to 127, 128 to 255, ..., all dimensions but the last counted through in order) at most 16 rows name the same one
Outputs:
- final_state: float32 [8, 512, 2048], P('runs', 'gx'), parts along dimension 0
- snapshots: bfloat16 [4, 4096, 2048], P('runs', 'gx'), parts along dimension 0
There are 2 independent parts, one for each index of `runs`. A program takes and returns all parts, laid end to end along the dimension named above; each array names one. Nothing has to cross between parts.
Inputs may be any that keep to these rules, and one draw needn't show every extreme that they name: `writer`: in each aligned block of 128 rows (one device's rows of one step) no destination is named more than 16 times, and one is named exactly 16 times.
All inputs are finite; a program needn't handle non-finite values.
Results may differ from a plain program's by a relative error of at most 0.001.
Values may be sent and summed in bfloat16 or wider, within the bound.
No kernel may reach another device: no remote copies, remote signals or barrier semaphores. Data moves between devices by JAX's collectives and lax.ppermute only.
A program may use at most 64 MiB of HBM per device.

v0:
```python
import jax
import jax.numpy as jnp
from jax import lax
from jax.sharding import PartitionSpec as P

STEPS = 2


DT = 0.15


def padded(x, sides, width):
    for axis, dim in sides:
        size, length = (lax.axis_size(axis), x.shape[dim])
        up = [(i, (i + 1) % size) for i in range(size - 1)]
        down = [(j, i) for i, j in up]
        last = lax.slice_in_dim(x, length - width, length, axis=dim)
        initial = lax.slice_in_dim(x, 0, width, axis=dim)
        before = lax.ppermute(last, axis, up)
        after = lax.ppermute(initial, axis, down)
        x = jnp.concatenate([before, x, after], axis=dim)
    return x


def tendency(field, conduct, growth):
    centre = field[:, 1:-1]
    cond_mid = conduct[:, 1:-1]
    cond_left = 0.5 * (conduct[:, :-2] + cond_mid)
    cond_right = 0.5 * (conduct[:, 2:] + cond_mid)
    laplace = cond_left * (field[:, :-2] - centre) + cond_right * (field[:, 2:] - centre)
    cond_y = 0.5 * (cond_mid + jnp.roll(cond_mid, -1, 2))
    flux_y = cond_y * (jnp.roll(centre, -1, 2) - centre)
    laplace = laplace + flux_y - jnp.roll(flux_y, 1, 2)
    flux_z = 0.5 * (cond_mid[1:] + cond_mid[:-1]) * (centre[1:] - centre[:-1])
    zero_row = jnp.zeros_like(flux_z[:1])
    laplace = (
        laplace + jnp.concatenate([flux_z, zero_row], 0) - jnp.concatenate([zero_row, flux_z], 0)
    )
    return laplace + growth * centre * (1.0 - centre)


def with_faces(field):
    return padded(field, (("gx", 1),), 1)


def pack_rows(state, dest, writers):
    levels, width, cells = state.shape
    per_dev = levels * width
    capacity = 2 * per_dev // writers
    snap_rows = state.astype(jnp.bfloat16).reshape(per_dev, cells)
    onehot = (dest == jnp.arange(writers, dtype=jnp.int32)[None, :]).astype(jnp.float32)
    row_ids = jnp.arange(per_dev, dtype=jnp.int32)
    lower = (row_ids[:, None] > row_ids[None, :]).astype(jnp.float32)
    before = jnp.dot(lower, onehot, preferred_element_type=jnp.float32)
    ranks = jnp.sum(before * onehot, axis=1).astype(jnp.int32)
    slots = dest[:, 0] * capacity + ranks
    placing = (jnp.arange(writers * capacity, dtype=jnp.int32)[:, None] == slots[None, :]).astype(
        jnp.bfloat16
    )
    return jnp.dot(placing, snap_rows, preferred_element_type=jnp.float32).astype(jnp.bfloat16)


def shards(initial, kappa, rate, writer):
    writers = lax.axis_size("gx")
    cond_pad = padded(kappa, (("gx", 1),), 1)
    state = initial
    frames = []
    for step_index in range(STEPS):
        section_one = state + DT * tendency(with_faces(state), cond_pad, rate)
        section_two = 0.75 * state + 0.25 * (
            section_one + DT * tendency(with_faces(section_one), cond_pad, rate)
        )
        state = state / 3.0 + 2.0 / 3.0 * (
            section_two + DT * tendency(with_faces(section_two), cond_pad, rate)
        )
        outgoing = pack_rows(state, writer[step_index], writers)
        frames.append(lax.all_to_all(outgoing, "gx", split_axis=0, concat_axis=0, tiled=True))
    result = jnp.stack(frames)
    return (state, result)


def solution(mesh):
    return jax.shard_map(
        shards,
        mesh=mesh,
        in_specs=(
            P("runs", "gx", None),
            P("runs", "gx", None),
            P("runs", "gx", None),
            P("runs", "gx", None),
        ),
        out_specs=(P("runs", "gx", None), P("runs", "gx", None)),
        check_vma=False,
    )
```

profile of v0, /device:TPU:10, one launch (start us, length us, event | category | flops | bytes accessed | tf_op | source)
XLA Modules:
  0.0 123.3 jit_solution(9366074368359582174)
XLA Ops:
  0.6 1.2 fusion.113
  1.8 2.8 %collective-permute-start.3 = (f32[4,1,2048]{2,1,0:T(1,128)S(1)}, f32[4,1,2048]{2,1,0:T(1,128)S(1)}, u32[]{:S(2)}, u32[]{:S(2)}) collective-permute-start(f32[4,1,2048]{2,1,0:T(1,128)S(1)} %get-tuple-element.23), channel_id=1, source_target_pairs={{1,0},{2,1},{3,2},{4,3},{5,4},{6,5},{7,6},{8,7},{9,8},{10,9},{11,1... | collective-permute-start | bytes 98312 | tf_op jit(solution)/shard_map/ppermute | solution.py:20
  4.6 1.9 %collective-permute-start.1 = (f32[4,1,2048]{2,1,0:T(1,128)S(1)}, f32[4,1,2048]{2,1,0:T(1,128)S(1)}, u32[]{:S(2)}, u32[]{:S(2)}) collective-permute-start(f32[4,1,2048]{2,1,0:T(1,128)S(1)} %get-tuple-element.22), channel_id=1, source_target_pairs={{0,1},{1,2},{2,3},{3,4},{4,5},{5,6},{6,7},{7,8},{8,9},{9,10},{10,1... | collective-permute-start | bytes 98312 | tf_op jit(solution)/shard_map/ppermute | solution.py:19
  6.5 1.1 fusion.112
  7.6 2.7 %collective-permute-start = (f32[4,1,2048]{2,1,0:T(1,128)S(1)}, f32[4,1,2048]{2,1,0:T(1,128)S(1)}, u32[]{:S(2)}, u32[]{:S(2)}) collective-permute-start(f32[4,1,2048]{2,1,0:T(1,128)S(1)} %get-tuple-element.21), channel_id=1, source_target_pairs={{0,1},{1,2},{2,3},{3,4},{4,5},{5,6},{6,7},{7,8},{8,9},{9,10},{10,1... | collective-permute-start | bytes 98312 | tf_op jit(solution)/shard_map/ppermute | solution.py:19
  10.3 3.8 %collective-permute-start.2 = (f32[4,1,2048]{2,1,0:T(1,128)S(1)}, f32[4,1,2048]{2,1,0:T(1,128)S(1)}, u32[]{:S(2)}, u32[]{:S(2)}) collective-permute-start(f32[4,1,2048]{2,1,0:T(1,128)S(1)} %get-tuple-element.20), channel_id=1, source_target_pairs={{1,0},{2,1},{3,2},{4,3},{5,4},{6,5},{7,6},{8,7},{9,8},{10,9},{11,1... | collective-permute-start | bytes 98312 | tf_op jit(solution)/shard_map/ppermute | solution.py:20
  14.1 1.6 %slice.268 = f32[4,32,2047]{2,1,0:T(8,128)S(1)} slice(f32[4,32,2048]{2,1,0:T(8,128)} %param.4), slice={[0:4], [0:32], [1:2048]} | slice | bytes 2096128 | tf_op jit(solution)/shard_map/jit(_roll_static)/slice | solution.py:32
  15.7 0.3 slice.266
  16.3 0.5 copy-done.8
  17.1 0.4 fusion.87
  17.7 0.7 copy-done.2
  18.3 1.1 fusion.79
  19.4 0.3 slice.332
  19.8 2.4 %collective-permute-start.5 = (f32[4,1,2048]{2,1,0:T(1,128)S(1)}, f32[4,1,2048]{2,1,0:T(1,128)S(1)}, u32[]{:S(2)}, u32[]{:S(2)}) collective-permute-start(f32[4,1,2048]{2,1,0:T(1,128)S(1)} %get-tuple-element.19), channel_id=1, source_target_pairs={{1,0},{2,1},{3,2},{4,3},{5,4},{6,5},{7,6},{8,7},{9,8},{10,9},{11,1... | collective-permute-start | bytes 98312 | tf_op jit(solution)/shard_map/ppermute | solution.py:20
  22.2 1.9 %collective-permute-start.4 = (f32[4,1,2048]{2,1,0:T(1,128)S(1)}, f32[4,1,2048]{2,1,0:T(1,128)S(1)}, u32[]{:S(2)}, u32[]{:S(2)}) collective-permute-start(f32[4,1,2048]{2,1,0:T(1,128)S(1)} %get-tuple-element.18), channel_id=1, source_target_pairs={{0,1},{1,2},{2,3},{3,4},{4,5},{5,6},{6,7},{7,8},{8,9},{9,10},{10,1... | collective-permute-start | bytes 98312 | tf_op jit(solution)/shard_map/ppermute | solution.py:19
  24.2 0.2 fusion.88
  24.6 3.8 %collective-permute-done.4 = f32[4,1,2048]{2,1,0:T(1,128)S(1)} collective-permute-done((f32[4,1,2048]{2,1,0:T(1,128)S(1)}, f32[4,1,2048]{2,1,0:T(1,128)S(1)}, u32[]{:S(2)}, u32[]{:S(2)}) %collective-permute-start.4) | collective-permute-done | bytes 32800 | tf_op jit(solution)/shard_map/ppermute | solution.py:19
  28.4 1.3 %fusion.67 = f32[4,32,2048]{2,1,0:T(8,128)S(1)} fusion(f32[4,32,2048]{2,1,0:T(8,128)S(1)} %fusion.79, f32[4,32,2048]{2,1,0:T(8,128)S(1)} %fusion.88, f32[4,1,2048]{2,1,0:T(1,128)S(1)} %collective-permute-done.5, f32[4,1,2048]{2,1,0:T(1,128)S(1)} %collective-permute-done.4, f32[4,32,2047]{2,1,0:T(8,128)S(1)} %bitcast.26, f32[4,32,1]{2,1,0:T(8,128)S(1)} %slice.334, ...), kind=kLoop, calls=%fused_computation.81 | loop fusion | flops 7077888 | bytes 8257536 | tf_op jit(solution)/shard_map/add | solution.py:70
  29.6 0.3 slice.340
  30.0 1.9 %collective-permute-start.7 = (f32[4,1,2048]{2,1,0:T(1,128)S(1)}, f32[4,1,2048]{2,1,0:T(1,128)S(1)}, u32[]{:S(2)}, u32[]{:S(2)}) collective-permute-start(f32[4,1,2048]{2,1,0:T(1,128)S(1)} %get-tuple-element.17), channel_id=1, source_target_pairs={{1,0},{2,1},{3,2},{4,3},{5,4},{6,5},{7,6},{8,7},{9,8},{10,9},{11,1... | collective-permute-start | bytes 98312 | tf_op jit(solution)/shard_map/ppermute | solution.py:20
  32.0 2.4 %collective-permute-start.6 = (f32[4,1,2048]{2,1,0:T(1,128)S(1)}, f32[4,1,2048]{2,1,0:T(1,128)S(1)}, u32[]{:S(2)}, u32[]{:S(2)}) collective-permute-start(f32[4,1,2048]{2,1,0:T(1,128)S(1)} %get-tuple-element.16), channel_id=1, source_target_pairs={{0,1},{1,2},{2,3},{3,4},{4,5},{5,6},{6,7},{7,8},{8,9},{9,10},{10,1... | collective-permute-start | bytes 98312 | tf_op jit(solution)/shard_map/ppermute | solution.py:19
  34.4 0.2 fusion.89
  34.8 3.3 %collective-permute-done.6 = f32[4,1,2048]{2,1,0:T(1,128)S(1)} collective-permute-done((f32[4,1,2048]{2,1,0:T(1,128)S(1)}, f32[4,1,2048]{2,1,0:T(1,128)S(1)}, u32[]{:S(2)}, u32[]{:S(2)}) %collective-permute-start.6) | collective-permute-done | bytes 32800 | tf_op jit(solution)/shard_map/ppermute | solution.py:19
  38.1 1.4 %fusion.102 = (bf16[4,32,2048]{2,1,0:T(8,128)(2,1)S(1)}, f32[4,32,2048]{2,1,0:T(8,128)S(1)}) fusion(f32[4,32,2048]{2,1,0:T(8,128)S(1)} %fusion.67, f32[4,32,2048]{2,1,0:T(8,128)S(1)} %copy-done.2, f32[3,32,2048]{2,1,0:T(8,128)S(1)} %fusion.96, f32[4,32,2047]{2,1,0:T(8,128)S(1)} %bitcast.25, f32[4,32,1]{2,1,0:T(8,128)S(1)} %slice.342, ...), kind=kLoop, calls=%fused_computation.144 | loop fusion | flops 7340032 | bytes 8781824 | tf_op jit(solution)/shard_map/convert_element_type | solution.py:50
  39.5 0.3 slice.348
  39.9 1.0 fusion.95
  40.9 1.9 %collective-permute-start.9 = (f32[4,1,2048]{2,1,0:T(1,128)S(1)}, f32[4,1,2048]{2,1,0:T(1,128)S(1)}, u32[]{:S(2)}, u32[]{:S(2)}) collective-permute-start(f32[4,1,2048]{2,1,0:T(1,128)S(1)} %get-tuple-element.15), channel_id=1, source_target_pairs={{1,0},{2,1},{3,2},{4,3},{5,4},{6,5},{7,6},{8,7},{9,8},{10,9},{11,1... | collective-permute-start | bytes 98312 | tf_op jit(solution)/shard_map/ppermute | solution.py:20
  42.8 2.4 %collective-permute-start.8 = (f32[4,1,2048]{2,1,0:T(1,128)S(1)}, f32[4,1,2048]{2,1,0:T(1,128)S(1)}, u32[]{:S(2)}, u32[]{:S(2)}) collective-permute-start(f32[4,1,2048]{2,1,0:T(1,128)S(1)} %get-tuple-element.14), channel_id=1, source_target_pairs={{0,1},{1,2},{2,3},{3,4},{4,5},{5,6},{6,7},{7,8},{8,9},{9,10},{10,1... | collective-permute-start | bytes 98312 | tf_op jit(solution)/shard_map/ppermute | solution.py:19
  45.3 0.2 fusion.90
  45.5 1.4 %convolution_convert_fusion.1 = bf16[256,2048]{1,0:T(8,128)(2,1)} fusion(bf16[128,2048]{1,0:T(8,128)(2,1)S(1)} %bitcast.31, s32[128]{0:T(128)S(1)} %get-tuple-element.24), kind=kOutput, calls=%fused_computation.1 | convolution fusion | flops 134774784 | bytes 1573376 | tf_op jit(solution)/shard_map/dot_general | solution.py:60
  47.0 6.0 %all-to-all-start = ((bf16[16,16,2048]{2,1,0:T(8,128)(2,1)}), bf16[16,16,2048]{2,1,0:T(8,128)(2,1)}, u32[]{:S(2)}, u32[]{:S(2)}) async-start(bf16[16,16,2048]{2,1,0:T(8,128)(2,1)} %bitcast.28), calls=%async_computation | async-start | bytes 2097152 | tf_op jit(solution)/shard_map/all_to_all | solution.py:77
  53.0 3.2 %fusion.39 = f32[4,32,2048]{2,1,0:T(8,128)S(1)} fusion(f32[4,32,2048]{2,1,0:T(8,128)S(1)} %get-tuple-element.3, f32[4,32,2048]{2,1,0:T(8,128)} %copy-done.7, f32[4,1,2048]{2,1,0:T(1,128)S(1)} %collective-permute-done.9, f32[4,1,2048]{2,1,0:T(1,128)S(1)} %collective-permute-done.8, f32[4,32,2047]{2,1,0:T(8,128)} %bitcast.23, f32[4,32,1]{2,1,0:T(8,128)S(1)} %slice.350, ...), kind=kLoop, calls=%fused_computation.49 | loop fusion | flops 6291456 | bytes 7208960 | tf_op jit(solution)/shard_map/add | solution.py:69
  56.2 0.3 slice.356
  56.6 3.1 %collective-permute-start.11 = (f32[4,1,2048]{2,1,0:T(1,128)S(1)}, f32[4,1,2048]{2,1,0:T(1,128)S(1)}, u32[]{:S(2)}, u32[]{:S(2)}) collective-permute-start(f32[4,1,2048]{2,1,0:T(1,128)S(1)} %get-tuple-element.13), channel_id=1, source_target_pairs={{1,0},{2,1},{3,2},{4,3},{5,4},{6,5},{7,6},{8,7},{9,8},{10,9},{11,1... | collective-permute-start | bytes 98312 | tf_op jit(solution)/shard_map/ppermute | solution.py:20
  59.8 2.1 %collective-permute-start.10 = (f32[4,1,2048]{2,1,0:T(1,128)S(1)}, f32[4,1,2048]{2,1,0:T(1,128)S(1)}, u32[]{:S(2)}, u32[]{:S(2)}) collective-permute-start(f32[4,1,2048]{2,1,0:T(1,128)S(1)} %get-tuple-element.12), channel_id=1, source_target_pairs={{0,1},{1,2},{2,3},{3,4},{4,5},{5,6},{6,7},{7,8},{8,9},{9,10},{10,1... | collective-permute-start | bytes 98312 | tf_op jit(solution)/shard_map/ppermute | solution.py:19
  61.8 0.3 fusion.91
  62.3 5.8 %collective-permute-done.11 = f32[4,1,2048]{2,1,0:T(1,128)S(1)} collective-permute-done((f32[4,1,2048]{2,1,0:T(1,128)S(1)}, f32[4,1,2048]{2,1,0:T(1,128)S(1)}, u32[]{:S(2)}, u32[]{:S(2)}) %collective-permute-start.11) | collective-permute-done | bytes 32800 | tf_op jit(solution)/shard_map/ppermute | solution.py:20
  68.1 4.7 %collective-permute-done.10 = f32[4,1,2048]{2,1,0:T(1,128)S(1)} collective-permute-done((f32[4,1,2048]{2,1,0:T(1,128)S(1)}, f32[4,1,2048]{2,1,0:T(1,128)S(1)}, u32[]{:S(2)}, u32[]{:S(2)}) %collective-permute-start.10) | collective-permute-done | bytes 32800 | tf_op jit(solution)/shard_map/ppermute | solution.py:19
  72.9 1.2 fusion.27
  74.1 0.3 slice.364
  74.4 1.9 %collective-permute-start.13 = (f32[4,1,2048]{2,1,0:T(1,128)S(1)}, f32[4,1,2048]{2,1,0:T(1,128)S(1)}, u32[]{:S(2)}, u32[]{:S(2)}) collective-permute-start(f32[4,1,2048]{2,1,0:T(1,128)S(1)} %get-tuple-element.11), channel_id=1, source_target_pairs={{1,0},{2,1},{3,2},{4,3},{5,4},{6,5},{7,6},{8,7},{9,8},{10,9},{11,1... | collective-permute-start | bytes 98312 | tf_op jit(solution)/shard_map/ppermute | solution.py:20
  76.4 2.4 %collective-permute-start.12 = (f32[4,1,2048]{2,1,0:T(1,128)S(1)}, f32[4,1,2048]{2,1,0:T(1,128)S(1)}, u32[]{:S(2)}, u32[]{:S(2)}) collective-permute-start(f32[4,1,2048]{2,1,0:T(1,128)S(1)} %get-tuple-element.10), channel_id=1, source_target_pairs={{0,1},{1,2},{2,3},{3,4},{4,5},{5,6},{6,7},{7,8},{8,9},{9,10},{10,1... | collective-permute-start | bytes 98312 | tf_op jit(solution)/shard_map/ppermute | solution.py:19
  78.8 0.3 fusion.92
  79.3 3.2 %collective-permute-done.12 = f32[4,1,2048]{2,1,0:T(1,128)S(1)} collective-permute-done((f32[4,1,2048]{2,1,0:T(1,128)S(1)}, f32[4,1,2048]{2,1,0:T(1,128)S(1)}, u32[]{:S(2)}, u32[]{:S(2)}) %collective-permute-start.12) | collective-permute-done | bytes 32800 | tf_op jit(solution)/shard_map/ppermute | solution.py:19
  82.5 2.2 %fusion.104 = (bf16[4,32,2048]{2,1,0:T(8,128)(2,1)S(1)}, f32[4,32,2048]{2,1,0:T(8,128)}) fusion(f32[4,32,2048]{2,1,0:T(8,128)S(1)} %fusion.27, f32[4,32,2048]{2,1,0:T(8,128)S(1)} %copy-done.2, f32[3,32,2048]{2,1,0:T(8,128)S(1)} %fusion.93, f32[4,32,2047]{2,1,0:T(8,128)S(1)} %bitcast.24, f32[4,32,1]{2,1,0:T(8,128)S(1)} %slice.366, ...), kind=kLoop, calls=%fused_computation.145 | loop fusion | flops 7340032 | bytes 8781824 | tf_op jit(solution)/shard_map/convert_element_type | solution.py:50
  84.7 0.4 convolution_convert_fusion
  85.1 35.4 %all_to_all.18 = bf16[16,16,2048]{2,1,0:T(8,128)(2,1)S(1)} all-to-all(bf16[16,16,2048]{2,1,0:T(8,128)(2,1)S(1)} %bitcast.29), channel_id=1, replica_groups=mesh['runs'=2,'gx'=16] {'gx'}, dimensions={0} | all-to-all | bytes 2097152 | tf_op jit(solution)/shard_map/all_to_all | solution.py:77
  120.6 2.7 %pad_maximum_fusion = bf16[2,256,2048]{2,1,0:T(8,128)(2,1)} fusion(bf16[1,256,2048]{2,1,0:T(8,128)(2,1)S(1)} %bitcast.30, bf16[1,256,2048]{2,1,0:T(8,128)(2,1)} %bitcast.3), kind=kLoop, calls=%fused_computation.2 | loop fusion | flops 1048576 | bytes 4194304 | tf_op jit(solution)/shard_map/stack | solution.py:78
  (55 shorter events, 1.7 us)
Async XLA Ops:
  0.6 15.1 %copy-start = (f32[4,32,2048]{2,1,0:T(8,128)S(1)}, f32[4,32,2048]{2,1,0:T(8,128)}, u32[]{:S(2)}) copy-start(f32[4,32,2048]{2,1,0:T(8,128)} %param.5) | copy-start | bytes 3145732
  1.8 15.8 %collective-permute-start.3 = (f32[4,1,2048]{2,1,0:T(1,128)S(1)}, f32[4,1,2048]{2,1,0:T(1,128)S(1)}, u32[]{:S(2)}, u32[]{:S(2)}) collective-permute-start(f32[4,1,2048]{2,1,0:T(1,128)S(1)} %get-tuple-element.23), channel_id=1, source_target_pairs={{1,0},{2,1},{3,2},{4,3},{5,4},{6,5},{7,6},{8,7},{9,8},{10,9},{11,1... | collective-permute-start | bytes 98312 | tf_op jit(solution)/shard_map/ppermute | solution.py:20
  4.6 13.1 %collective-permute-start.1 = (f32[4,1,2048]{2,1,0:T(1,128)S(1)}, f32[4,1,2048]{2,1,0:T(1,128)S(1)}, u32[]{:S(2)}, u32[]{:S(2)}) collective-permute-start(f32[4,1,2048]{2,1,0:T(1,128)S(1)} %get-tuple-element.22), channel_id=1, source_target_pairs={{0,1},{1,2},{2,3},{3,4},{4,5},{5,6},{6,7},{7,8},{8,9},{9,10},{10,1... | collective-permute-start | bytes 98312 | tf_op jit(solution)/shard_map/ppermute | solution.py:19
  7.6 10.1 %collective-permute-start = (f32[4,1,2048]{2,1,0:T(1,128)S(1)}, f32[4,1,2048]{2,1,0:T(1,128)S(1)}, u32[]{:S(2)}, u32[]{:S(2)}) collective-permute-start(f32[4,1,2048]{2,1,0:T(1,128)S(1)} %get-tuple-element.21), channel_id=1, source_target_pairs={{0,1},{1,2},{2,3},{3,4},{4,5},{5,6},{6,7},{7,8},{8,9},{9,10},{10,1... | collective-permute-start | bytes 98312 | tf_op jit(solution)/shard_map/ppermute | solution.py:19
  10.3 7.4 %collective-permute-start.2 = (f32[4,1,2048]{2,1,0:T(1,128)S(1)}, f32[4,1,2048]{2,1,0:T(1,128)S(1)}, u32[]{:S(2)}, u32[]{:S(2)}) collective-permute-start(f32[4,1,2048]{2,1,0:T(1,128)S(1)} %get-tuple-element.20), channel_id=1, source_target_pairs={{1,0},{2,1},{3,2},{4,3},{5,4},{6,5},{7,6},{8,7},{9,8},{10,9},{11,1... | collective-permute-start | bytes 98312 | tf_op jit(solution)/shard_map/ppermute | solution.py:20
  14.1 2.0 %copy-start.1 = (f32[4,32,2048]{2,1,0:T(8,128)S(1)}, f32[4,32,2048]{2,1,0:T(8,128)}, u32[]{:S(2)}) copy-start(f32[4,32,2048]{2,1,0:T(8,128)} %param.4) | copy-start | bytes 3145732
  16.1 0.7 copy-start.8
  16.1 1.0 slice-start
  16.1 1.0 slice-start.1
  16.8 23.2 %copy-start.5 = (f32[3,32,2048]{2,1,0:T(8,128)}, f32[3,32,2048]{2,1,0:T(8,128)S(1)}, u32[]{:S(2)}) copy-start(f32[3,32,2048]{2,1,0:T(8,128)S(1)} %get-tuple-element.7) | copy-start | bytes 2359300
  17.1 1.2 copy-start.2
  17.5 27.7 %copy-start.3 = (f32[4,32,2048]{2,1,0:T(8,128)}, f32[4,32,2048]{2,1,0:T(8,128)S(1)}, u32[]{:S(2)}) copy-start(f32[4,32,2048]{2,1,0:T(8,128)S(1)} %get-tuple-element.9) | copy-start | bytes 3145732
  19.8 4.8 %collective-permute-start.5 = (f32[4,1,2048]{2,1,0:T(1,128)S(1)}, f32[4,1,2048]{2,1,0:T(1,128)S(1)}, u32[]{:S(2)}, u32[]{:S(2)}) collective-permute-start(f32[4,1,2048]{2,1,0:T(1,128)S(1)} %get-tuple-element.19), channel_id=1, source_target_pairs={{1,0},{2,1},{3,2},{4,3},{5,4},{6,5},{7,6},{8,7},{9,8},{10,9},{11,1... | collective-permute-start | bytes 98312 | tf_op jit(solution)/shard_map/ppermute | solution.py:20
  22.2 6.1 %collective-permute-start.4 = (f32[4,1,2048]{2,1,0:T(1,128)S(1)}, f32[4,1,2048]{2,1,0:T(1,128)S(1)}, u32[]{:S(2)}, u32[]{:S(2)}) collective-permute-start(f32[4,1,2048]{2,1,0:T(1,128)S(1)} %get-tuple-element.18), channel_id=1, source_target_pairs={{0,1},{1,2},{2,3},{3,4},{4,5},{5,6},{6,7},{7,8},{8,9},{9,10},{10,1... | collective-permute-start | bytes 98312 | tf_op jit(solution)/shard_map/ppermute | solution.py:19
  30.0 4.8 %collective-permute-start.7 = (f32[4,1,2048]{2,1,0:T(1,128)S(1)}, f32[4,1,2048]{2,1,0:T(1,128)S(1)}, u32[]{:S(2)}, u32[]{:S(2)}) collective-permute-start(f32[4,1,2048]{2,1,0:T(1,128)S(1)} %get-tuple-element.17), channel_id=1, source_target_pairs={{1,0},{2,1},{3,2},{4,3},{5,4},{6,5},{7,6},{8,7},{9,8},{10,9},{11,1... | collective-permute-start | bytes 98312 | tf_op jit(solution)/shard_map/ppermute | solution.py:20
  32.0 6.1 %collective-permute-start.6 = (f32[4,1,2048]{2,1,0:T(1,128)S(1)}, f32[4,1,2048]{2,1,0:T(1,128)S(1)}, u32[]{:S(2)}, u32[]{:S(2)}) collective-permute-start(f32[4,1,2048]{2,1,0:T(1,128)S(1)} %get-tuple-element.16), channel_id=1, source_target_pairs={{0,1},{1,2},{2,3},{3,4},{4,5},{5,6},{6,7},{7,8},{8,9},{9,10},{10,1... | collective-permute-start | bytes 98312 | tf_op jit(solution)/shard_map/ppermute | solution.py:19
  40.9 12.1 %collective-permute-start.9 = (f32[4,1,2048]{2,1,0:T(1,128)S(1)}, f32[4,1,2048]{2,1,0:T(1,128)S(1)}, u32[]{:S(2)}, u32[]{:S(2)}) collective-permute-start(f32[4,1,2048]{2,1,0:T(1,128)S(1)} %get-tuple-element.15), channel_id=1, source_target_pairs={{1,0},{2,1},{3,2},{4,3},{5,4},{6,5},{7,6},{8,7},{9,8},{10,9},{11,1... | collective-permute-start | bytes 98312 | tf_op jit(solution)/shard_map/ppermute | solution.py:20
  42.8 10.2 %collective-permute-start.8 = (f32[4,1,2048]{2,1,0:T(1,128)S(1)}, f32[4,1,2048]{2,1,0:T(1,128)S(1)}, u32[]{:S(2)}, u32[]{:S(2)}) collective-permute-start(f32[4,1,2048]{2,1,0:T(1,128)S(1)} %get-tuple-element.14), channel_id=1, source_target_pairs={{0,1},{1,2},{2,3},{3,4},{4,5},{5,6},{6,7},{7,8},{8,9},{9,10},{10,1... | collective-permute-start | bytes 98312 | tf_op jit(solution)/shard_map/ppermute | solution.py:19
  45.5 1.4 %copy-start.7 = (f32[4,32,2048]{2,1,0:T(8,128)}, f32[4,32,2048]{2,1,0:T(8,128)S(1)}, u32[]{:S(2)}) copy-start(f32[4,32,2048]{2,1,0:T(8,128)S(1)} %fusion.90) | copy-start | bytes 3145732
  47.0 38.2 %all-to-all-start = ((bf16[16,16,2048]{2,1,0:T(8,128)(2,1)}), bf16[16,16,2048]{2,1,0:T(8,128)(2,1)}, u32[]{:S(2)}, u32[]{:S(2)}) async-start(bf16[16,16,2048]{2,1,0:T(8,128)(2,1)} %bitcast.28), calls=%async_computation | async-start | bytes 2097152 | tf_op jit(solution)/shard_map/all_to_all | solution.py:77
  56.2 5.6 %copy-start.4 = (f32[4,32,2048]{2,1,0:T(8,128)S(1)}, f32[4,32,2048]{2,1,0:T(8,128)}, u32[]{:S(2)}) copy-start(f32[4,32,2048]{2,1,0:T(8,128)} %copy-done.3) | copy-start | bytes 3145732
  56.6 11.5 %collective-permute-start.11 = (f32[4,1,2048]{2,1,0:T(1,128)S(1)}, f32[4,1,2048]{2,1,0:T(1,128)S(1)}, u32[]{:S(2)}, u32[]{:S(2)}) collective-permute-start(f32[4,1,2048]{2,1,0:T(1,128)S(1)} %get-tuple-element.13), channel_id=1, source_target_pairs={{1,0},{2,1},{3,2},{4,3},{5,4},{6,5},{7,6},{8,7},{9,8},{10,9},{11,1... | collective-permute-start | bytes 98312 | tf_op jit(solution)/shard_map/ppermute | solution.py:20
  59.8 2.4 %copy-start.6 = (f32[3,32,2048]{2,1,0:T(8,128)S(1)}, f32[3,32,2048]{2,1,0:T(8,128)}, u32[]{:S(2)}) copy-start(f32[3,32,2048]{2,1,0:T(8,128)} %copy-done.5) | copy-start | bytes 2359300
  59.8 13.1 %collective-permute-start.10 = (f32[4,1,2048]{2,1,0:T(1,128)S(1)}, f32[4,1,2048]{2,1,0:T(1,128)S(1)}, u32[]{:S(2)}, u32[]{:S(2)}) collective-permute-start(f32[4,1,2048]{2,1,0:T(1,128)S(1)} %get-tuple-element.12), channel_id=1, source_target_pairs={{0,1},{1,2},{2,3},{3,4},{4,5},{5,6},{6,7},{7,8},{8,9},{9,10},{10,1... | collective-permute-start | bytes 98312 | tf_op jit(solution)/shard_map/ppermute | solution.py:19
  74.4 4.8 %collective-permute-start.13 = (f32[4,1,2048]{2,1,0:T(1,128)S(1)}, f32[4,1,2048]{2,1,0:T(1,128)S(1)}, u32[]{:S(2)}, u32[]{:S(2)}) collective-permute-start(f32[4,1,2048]{2,1,0:T(1,128)S(1)} %get-tuple-element.11), channel_id=1, source_target_pairs={{1,0},{2,1},{3,2},{4,3},{5,4},{6,5},{7,6},{8,7},{9,8},{10,9},{11,1... | collective-permute-start | bytes 98312 | tf_op jit(solution)/shard_map/ppermute | solution.py:20
  76.4 6.1 %collective-permute-start.12 = (f32[4,1,2048]{2,1,0:T(1,128)S(1)}, f32[4,1,2048]{2,1,0:T(1,128)S(1)}, u32[]{:S(2)}, u32[]{:S(2)}) collective-permute-start(f32[4,1,2048]{2,1,0:T(1,128)S(1)} %get-tuple-element.10), channel_id=1, source_target_pairs={{0,1},{1,2},{2,3},{3,4},{4,5},{5,6},{6,7},{7,8},{8,9},{9,10},{10,1... | collective-permute-start | bytes 98312 | tf_op jit(solution)/shard_map/ppermute | solution.py:19
where the time goes:
time: 125 us; the launch traced here: 123 us
  starting transfers between devices  39.6 us (32%)
  blocking collectives  35.4 us (28%)
  waiting for transfers between devices  20.9 us (17%)
  other arithmetic  16.2 us (13%)
  local copies, waits for them, and re-layouts  7.89 us (6%)
  matrix products  2.13 us (2%)
    all_to_all x1, blocking collectives, shards(): lax.all_to_all(outgoing, 'gx', split_axis=0, concat_axis=0, tiled=True)  35.4 us
    ppermute x7, starting transfers between devices, padded(): after = lax.ppermute(initial, axis, down)  17.8 us
    ppermute x7, starting transfers between devices, padded(): before = lax.ppermute(last, axis, up)  15.8 us
    ppermute x7, waiting for transfers between devices, padded(): before = lax.ppermute(last, axis, up)  15.1 us
    all_to_all x1, starting transfers between devices, shards(): lax.all_to_all(outgoing, 'gx', split_axis=0, concat_axis=0, tiled=True)  6.03 us
    ppermute x7, waiting for transfers between devices, padded(): after = lax.ppermute(initial, axis, down)  5.85 us
    add x2, other arithmetic, shards(): section_one = state + DT * tendency(with_faces(state), cond_pad, rate)  4.26 us
    convert_element_type x2, other arithmetic, pack_rows(): snap_rows = state.astype(jnp.bfloat16).reshape(per_dev, cells)  3.58 us
  transfers between devices with their start and end apart: 15, of which 5 were waited for; matrix products, arithmetic and copies ran while one was open for 12% of the time, Pallas kernels for 0%

commit v1 on v0

v1 whole, which is shorter than its diff:
```python
import functools

import jax
import jax.numpy as jnp
from jax import lax
from jax.experimental import pallas as pl
from jax.experimental.pallas import tpu as pltpu
from jax.sharding import PartitionSpec as P

STEPS = 2
DT = 0.15
LANES = 128
TILE = 8
VMEM = 48 * 1024 * 1024


def step_kernel(second, *refs):
    if second:
        where_ref, u_ref, k_ref, r_ref, core_ref, chip_ref, core2_ref, chip2_ref, place_ref = refs[:9]
        refs = refs[9:]
    else:
        where_ref, u_ref, k_ref, r_ref, core_ref, chip_ref, place_ref = refs[:7]
        core2_ref = chip2_ref = None
        refs = refs[7:]
    new_ref, pack_ref, face_ref = (refs[0], refs[1], None) if second else refs[:3]
    u0, u1, u2, xp, xm, yp, ym, zp, lin, quad = refs[-10:]
    levels, rows, cells = u_ref.shape
    ext = rows + TILE
    chunks = cells // LANES
    even = where_ref[0] == 0
    row8 = lax.broadcasted_iota(jnp.int32, (TILE, LANES), 0)
    lane = lax.broadcasted_iota(jnp.int32, (ext, LANES), 1)
    low = row8 < TILE // 2
    live = jnp.where(low, where_ref[1], where_ref[2]) > 0

    def cols(j):
        j = j % chunks
        return slice(j * LANES, (j + 1) * LANES)

    def pick(core, chip):
        below = jnp.where(even, core, chip)
        above = jnp.where(even, chip, core)
        return below, above

    kk = u2
    for j in range(chunks):
        c = cols(j)
        core, chip = core_ref[:, c].astype(jnp.float32), chip_ref[:, c].astype(jnp.float32)
        if second:
            core2, chip2 = core2_ref[:, c].astype(jnp.float32), chip2_ref[:, c].astype(jnp.float32)
        for l in range(levels):
            t = slice(l * TILE, (l + 1) * TILE)
            below, above = pick(core[t], chip[t])
            k_face = jnp.where(low, pltpu.roll(below, 3, 0), pltpu.roll(above, 5, 0))
            r_face = jnp.where(low, pltpu.roll(below, 5, 0), pltpu.roll(above, 3, 0))
            if second:
                h = slice(l // 2 * TILE, (l // 2 + 1) * TILE)
                below, above = pick(core2[h], chip2[h])
                if l % 2:
                    u_face = jnp.where(low, pltpu.roll(below, 4, 0), above)
                else:
                    u_face = jnp.where(low, below, pltpu.roll(above, 4, 0))
            else:
                u_face = jnp.where(low, below, above)
            kk[l, :rows, c] = k_ref[l, :, c]
            kk[l, rows:, c] = k_face
            u0[l, :rows, c] = u_ref[l, :, c]
            u0[l, rows:, c] = u_face
            quad[l, :rows, c] = DT * r_ref[l, :, c]
            quad[l, rows:, c] = DT * r_face

    def left_right(src, l):
        right, left, here = {}, {}, {}

        def rots(j):
            j = j % chunks
            if j not in here:
                v = src[l, :, cols(j)]
                here[j] = v
                right[j] = pltpu.roll(v, LANES - 1, 1)
                left[j] = pltpu.roll(v, 1, 1)
            return j

        def at(j):
            a, b, d = rots(j - 1), rots(j), rots(j + 1)
            return (
                here[b],
                jnp.where(lane == LANES - 1, right[d], right[b]),
                jnp.where(lane == 0, left[a], left[b]),
            )

        return at

    half = 0.5 * DT
    ats = [left_right(kk, l) for l in range(levels)]
    for j in range(chunks):
        c = cols(j)
        for l in range(levels):
            k, k_right, k_left = ats[l](j)
            a = half * (k + pltpu.roll(k, ext - 1, 0))
            b = pltpu.roll(a, 1, 0)
            d, e = half * (k + k_right), half * (k + k_left)
            xp[l, :, c], xm[l, :, c], yp[l, :, c], ym[l, :, c] = a, b, d, e
            total = a + b + d + e
            if l < levels - 1:
                f = half * (k + kk[l + 1, :, c])
                zp[l, :, c] = f
                total = total + f
            if l > 0:
                total = total + zp[l - 1, :, c]
            lin[l, :, c] = 1.0 + quad[l, :, c] - total

    def euler(src, ats, l, j):
        c = cols(j)
        u, u_right, u_left = ats[l](j)
        out = u * (lin[l, :, c] - quad[l, :, c] * u)
        out = out + xp[l, :, c] * pltpu.roll(u, ext - 1, 0) + xm[l, :, c] * pltpu.roll(u, 1, 0)
        out = out + yp[l, :, c] * u_right + ym[l, :, c] * u_left
        if l < levels - 1:
            out = out + zp[l, :, c] * src[l + 1, :, c]
        if l > 0:
            out = out + zp[l - 1, :, c] * src[l - 1, :, c]
        return out

    def masked(dst, l, c, v):
        dst[l, :rows, c] = v[:rows]
        dst[l, rows:, c] = jnp.where(live, v[rows:], 0.0)

    ats = [left_right(u0, l) for l in range(levels)]
    for j in range(chunks):
        for l in range(levels):
            masked(u1, l, cols(j), euler(u0, ats, l, j))
    ats = [left_right(u1, l) for l in range(levels)]
    for j in range(chunks):
        for l in range(levels):
            c = cols(j)
            masked(u2, l, c, 0.75 * u0[l, :, c] + 0.25 * euler(u1, ats, l, j))
    ats = [left_right(u2, l) for l in range(levels)]
    for j in range(chunks):
        for l in range(levels):
            c = cols(j)
            v = (1.0 / 3.0) * u0[l, :, c] + (2.0 / 3.0) * euler(u2, ats, l, j)
            new_ref[l, :, c] = v[:rows]
    if face_ref is not None:
        half8 = row8 < TILE // 2
        for j in range(chunks):
            c = cols(j)
            for side in range(2):
                parts = []
                for h in range(levels // 2):
                    if side == 0:
                        x = new_ref[2 * h, :TILE, c]
                        y = pltpu.roll(new_ref[2 * h + 1, :TILE, c], 4, 0)
                    else:
                        x = pltpu.roll(new_ref[2 * h, rows - TILE :, c], 4, 0)
                        y = new_ref[2 * h + 1, rows - TILE :, c]
                    parts.append(jnp.where(half8, x, y))
                face_ref[side, :, c] = jnp.concatenate(parts, 0).astype(jnp.bfloat16)
    wide = 2 * LANES
    place = place_ref[...]
    for j in range(0, cells, wide):
        v = new_ref[:, :, j : j + wide].astype(jnp.bfloat16).reshape(levels * rows, wide)
        pack_ref[:, j : j + wide] = jnp.dot(
            place, v, preferred_element_type=jnp.float32
        ).astype(jnp.bfloat16)


def step(second, where, state, kappa, rate, faces, place):
    levels, rows, cells = state.shape
    slots = place.shape[0]
    ext = (levels, rows + TILE, cells)
    out = [
        jax.ShapeDtypeStruct(state.shape, jnp.float32),
        jax.ShapeDtypeStruct((slots, cells), jnp.bfloat16),
    ]
    if not second:
        out.append(jax.ShapeDtypeStruct((2, levels * TILE // 2, cells), jnp.bfloat16))
    vmem = pl.BlockSpec(memory_space=pltpu.VMEM)
    return pl.pallas_call(
        functools.partial(step_kernel, second),
        out_shape=out,
        in_specs=[pl.BlockSpec(memory_space=pltpu.SMEM)] + [vmem] * (4 + len(faces)),
        out_specs=[vmem] * len(out),
        scratch_shapes=[pltpu.VMEM(ext, jnp.float32) for _ in range(10)],
        compiler_params=pltpu.CompilerParams(vmem_limit_bytes=VMEM),
        cost_estimate=pl.CostEstimate(
            flops=120 * levels * rows * cells, bytes_accessed=22 * levels * rows * cells, transcendentals=0
        ),
    )(where, state, kappa, rate, *faces, place)


def placing(dest, writers, per_dev):
    slots = 2 * per_dev
    capacity = slots // writers
    onehot = (dest == jnp.arange(writers, dtype=jnp.int32)[None, :]).astype(jnp.float32)
    row_ids = jnp.arange(per_dev, dtype=jnp.int32)
    lower = (row_ids[:, None] > row_ids[None, :]).astype(jnp.float32)
    before = jnp.dot(lower, onehot, preferred_element_type=jnp.float32)
    ranks = jnp.sum(before * onehot, axis=1).astype(jnp.int32)
    target = dest[:, 0] * capacity + ranks
    return (jnp.arange(slots, dtype=jnp.int32)[:, None] == target[None, :]).astype(jnp.bfloat16)


def shards(initial, kappa, rate, writer):
    n = lax.axis_size("gx")
    me = lax.axis_index("gx")
    levels, rows, cells = initial.shape
    even = me % 2 == 0
    where = jnp.stack([me % 2, (me < n - 1).astype(jnp.int32), (me > 0).astype(jnp.int32)])
    by_core = [(i, i ^ 1) for i in range(n)]
    by_chip = [(i, i + 1) for i in range(1, n - 1, 2)] + [(i + 1, i) for i in range(1, n - 1, 2)]

    def exchange(top, bottom):
        to_core = jnp.where(even, bottom, top)
        to_chip = jnp.where(even, top, bottom)
        return lax.ppermute(to_core, "gx", by_core), lax.ppermute(to_chip, "gx", by_chip)

    top = jnp.concatenate([initial[:, :3], rate[:, :2], kappa[:, :3]], 1)
    bottom = jnp.concatenate([kappa[:, -3:], rate[:, -2:], initial[:, -3:]], 1)
    flat = (levels * TILE, cells)
    faces = exchange(top.astype(jnp.bfloat16).reshape(flat), bottom.astype(jnp.bfloat16).reshape(flat))
    places = [placing(writer[s], n, levels * rows) for s in range(STEPS)]

    def route(packed):
        return lax.all_to_all(packed, "gx", split_axis=0, concat_axis=0, tiled=True)

    state, packed, edge = step(False, where, initial, kappa, rate, faces, places[0])
    first = route(packed)
    faces = faces + exchange(edge[0], edge[1])
    state, packed = step(True, where, state, kappa, rate, faces, places[1])
    return state, jnp.stack([first, route(packed)])


def solution(mesh):
    spec = P("runs", "gx", None)
    return jax.shard_map(
        shards, mesh=mesh, in_specs=(spec,) * 4, out_specs=(spec, spec), check_vma=False
    )
```

time: 125 us -> 92.3 us (0.74)
  starting transfers between devices: 39.6 us -> 13.1 us
  Pallas kernels: 0 us -> 12.2 us
  other arithmetic: 16.2 us -> 5.38 us
  local copies, waits for them, and re-layouts: 7.89 us -> 4.32 us
  matrix products: 2.13 us -> 0.32 us
    ppermute x14 -> x4, starting transfers between devices: 33.6 us -> 7.33 us  [the longest x2 6.04 us: exchange(): lax.ppermute(to_chip, 'gx', by_chip)]
    pallas_call x0 -> x2, Pallas kernels: none -> 12.2 us  [step(): pl.pallas_call(functools.partial(step_kernel, second), out_shape=out, in_...]
    add x5 -> x1, other arithmetic: 6.68 us -> 0.01 us  [placing(): target = dest[:, 0] * capacity + ranks]
    slice x29 -> x2, local copies, waits for them, and re-layouts: 6.69 us -> 0.18 us  [shards(): bottom = jnp.concatenate([kappa[:, -3:], rate[:, -2:], initial[:, -3:]], 1)]
    convert_element_type x2, other arithmetic: 3.58 us -> 0.05 us  [placing(): (jnp.arange(slots, dtype=jnp.int32)[:, None] == target[None, :]).astype(j...]
    mul x12 -> x0, other arithmetic: 3.16 us -> none  [the longest x6 1.62 us: tendency(): flux_y = cond_y * (jnp.roll(centre, -1, 2) - centre)]
    unnamed x18, local copies, waits for them, and re-layouts: 1.19 us -> 4.14 us
    dot_general x4 -> x2, matrix products: 2.13 us -> 0.32 us  [placing(): before = jnp.dot(lower, onehot, preferred_element_type=jnp.float32)]
  transfers between devices with their start and end apart: 15 -> 5, of which waited for: 5 -> 2; matrix products, arithmetic and copies ran while one was open for 12% -> 1% of each run, Pallas kernels for 0% -> 7%
where the time goes in v1:
time: 92.3 us; the launch traced here: 90.5 us
  blocking collectives  34.5 us (37%)
  waiting for transfers between devices  19.9 us (22%)
  starting transfers between devices  13.1 us (14%)
  Pallas kernels  12.2 us (13%)
  other arithmetic  5.38 us (6%)
  local copies, waits for them, and re-layouts  4.32 us (5%)
    all_to_all x1, blocking collectives, route(): return lax.all_to_all(packed, 'gx', split_axis=0, concat_axis=0, tiled=True)  34.5 us
    ppermute x2, waiting for transfers between devices, exchange(): lax.ppermute(to_chip, 'gx', by_chip)  19.9 us
    pallas_call x2, Pallas kernels, step(): pl.pallas_call(functools.partial(step_kernel, second), out_shape=out, in_...  12.2 us
    ppermute x2, starting transfers between devices, exchange(): lax.ppermute(to_chip, 'gx', by_chip)  6.04 us
    all_to_all x1, starting transfers between devices, route(): return lax.all_to_all(packed, 'gx', split_axis=0, concat_axis=0, tiled=True)  5.81 us
    unnamed x18, local copies, waits for them, and re-layouts  4.14 us
    another operation x1, other arithmetic, shards(): return (state, jnp.stack([first, route(packed)]))  2.74 us
  transfers between devices with their start and end apart: 5, of which 2 were waited for; matrix products, arithmetic and copies ran while one was open for 1% of the time, Pallas kernels for 7%

profile of v1, /device:TPU:10, one launch (start us, length us, event | category | flops | bytes accessed | tf_op | source)
XLA Modules:
  0.0 90.5 jit_solution(15948820395377258928)
XLA Ops:
  0.6 0.0 copy-start
  0.6 0.0 copy-start.1
  0.7 1.4 %convert.22 = bf16[4,32,2048]{2,1,0:T(8,128)(2,1)S(1)} convert(f32[4,32,2048]{2,1,0:T(8,128)} %refs_1_.1) | non-fusion elementwise | flops 262144 | bytes 1572864 | tf_op jit(solution)/shard_map/convert.11
  2.1 0.1 copy-done
  2.2 0.0 copy-start.8
  2.2 0.0 copy-start.2
  2.2 0.1 convert.20
  2.2 0.2 copy-done.1
  2.5 0.1 convert.21
  2.6 0.1 fusion.7
  2.6 0.1 fusion.6
  2.7 0.9 %select_bitcast_fusion = (bf16[32,2048]{1,0:T(8,128)(2,1)}, bf16[32,2048]{1,0:T(8,128)(2,1)}) fusion(pred[]{:T(512)S(6)} %eq.29, bf16[4,3,2048]{2,1,0:T(4,128)(2,1)S(1)} %get-tuple-element.13, bf16[4,2,2048]{2,1,0:T(2,128)(2,1)S(1)} %get-tuple-element.15, bf16[4,3,2048]{2,1,0:T(4,128)(2,1)S(1)} %get-tuple-element.26, ...), kind=kLoop, calls=%fused_computation.9 | loop fusion | flops 917504 | bytes 524289 | tf_op jit(solution)/shard_map/jit(_where)/select_n | solution.py:215
  3.7 2.7 %collective-permute-start.1 = (bf16[32,2048]{1,0:T(8,128)(2,1)}, bf16[32,2048]{1,0:T(8,128)(2,1)S(1)}, u32[]{:S(2)}, u32[]{:S(2)}) collective-permute-start(bf16[32,2048]{1,0:T(8,128)(2,1)} %get-tuple-element.18), channel_id=1, source_target_pairs={{1,2},{3,4},{5,6},{7,8},{9,10},{11,12},{13,14},{2,1},{4,3},{6,5},{... | collective-permute-start | bytes 393224 | tf_op jit(solution)/shard_map/ppermute | solution.py:216
  6.4 0.9 collective-permute-start
  7.3 0.0 copy-done.8
  7.3 0.2 fusion.1
  7.5 0.2 fusion
  7.7 0.1 pad_add_fusion.refs_0_
  7.8 3.4 %collective-permute-done.1.refs_5_ = bf16[32,2048]{1,0:T(8,128)(2,1)S(1)} collective-permute-done((bf16[32,2048]{1,0:T(8,128)(2,1)}, bf16[32,2048]{1,0:T(8,128)(2,1)S(1)}, u32[]{:S(2)}, u32[]{:S(2)}) %collective-permute-start.1) | collective-permute-done | bytes 131104 | tf_op jit(solution)/shard_map/ppermute | solution.py:216
  11.2 0.0 collective-permute-done.refs_4_
  11.2 0.0 copy-done.2
  11.2 5.7 %shard_map.59 = (f32[4,32,2048]{2,1,0:T(8,128)S(1)}, bf16[256,2048]{1,0:T(8,128)(2,1)S(1)}, bf16[2,16,2048]{2,1,0:T(8,128)(2,1)S(1)}) custom-call(s32[3]{0:T(128)S(1)} %pad_add_fusion.refs_0_, f32[4,32,2048]{2,1,0:T(8,128)S(1)} %copy-done.2, f32[4,32,2048]{2,1,0:T(8,128)S(1)} %copy-done, f32[4,32,2048]{2,1,0:T(8,128)S(1)} %copy-done.1, ...), custom_call_target="tpu_custom_call" | custom-call | flops 31457280 | bytes 5767168 | tf_op jit(solution)/shard_map/pallas_call | solution.py:179
  16.9 0.0 copy-start.3
  16.9 1.0 %copy-done.3 = bf16[256,2048]{1,0:T(8,128)(2,1)} copy-done((bf16[256,2048]{1,0:T(8,128)(2,1)}, bf16[256,2048]{1,0:T(8,128)(2,1)S(1)}, u32[]{:S(2)}) %copy-start.3) | copy-done | bytes 1048600
  17.9 0.0 copy-start.4
  17.9 1.0 %copy-done.4 = f32[4,32,2048]{2,1,0:T(8,128)} copy-done((f32[4,32,2048]{2,1,0:T(8,128)}, f32[4,32,2048]{2,1,0:T(8,128)S(1)}, u32[]{:S(2)}) %copy-start.4) | copy-done | bytes 1048600
  18.9 0.0 copy-start.6
  18.9 0.6 copy-done.6
  19.5 0.0 copy-start.7
  19.5 5.8 %all-to-all-start = ((bf16[16,16,2048]{2,1,0:T(8,128)(2,1)}), bf16[16,16,2048]{2,1,0:T(8,128)(2,1)}, u32[]{:S(2)}, u32[]{:S(2)}) async-start(bf16[16,16,2048]{2,1,0:T(8,128)(2,1)} %bitcast.23), calls=%async_computation | async-start | bytes 2097152 | tf_op jit(solution)/shard_map/all_to_all | solution.py:225
  25.3 0.0 copy-done.7
  25.3 3.3 %collective-permute-start.3 = (bf16[16,2048]{1,0:T(8,128)(2,1)S(1)}, bf16[16,2048]{1,0:T(8,128)(2,1)S(1)}, u32[]{:S(2)}, u32[]{:S(2)}) collective-permute-start(bf16[16,2048]{1,0:T(8,128)(2,1)S(1)} %get-tuple-element.20), channel_id=1, source_target_pairs={{1,2},{3,4},{5,6},{7,8},{9,10},{11,12},{13,14},{2,1},{4,3},{6,5},{... | collective-permute-start | bytes 196616 | tf_op jit(solution)/shard_map/ppermute | solution.py:216
  28.7 0.4 collective-permute-start.2
  29.1 16.5 %collective-permute-done.3.refs_7_ = bf16[16,2048]{1,0:T(8,128)(2,1)S(1)} collective-permute-done((bf16[16,2048]{1,0:T(8,128)(2,1)S(1)}, bf16[16,2048]{1,0:T(8,128)(2,1)S(1)}, u32[]{:S(2)}, u32[]{:S(2)}) %collective-permute-start.3) | collective-permute-done | bytes 65568 | tf_op jit(solution)/shard_map/ppermute | solution.py:216
  45.6 0.0 collective-permute-done.2.refs_6_
  45.6 0.0 copy-start.5
  45.6 1.2 %copy-done.5 = f32[4,32,2048]{2,1,0:T(8,128)S(1)} copy-done((f32[4,32,2048]{2,1,0:T(8,128)S(1)}, f32[4,32,2048]{2,1,0:T(8,128)}, u32[]{:S(2)}) %copy-start.5) | copy-done | bytes 1048600
  46.9 6.5 %shard_map.60 = (f32[4,32,2048]{2,1,0:T(8,128)}, bf16[256,2048]{1,0:T(8,128)(2,1)S(1)}) custom-call(s32[3]{0:T(128)S(1)} %pad_add_fusion.refs_0_, f32[4,32,2048]{2,1,0:T(8,128)S(1)} %copy-done.5, f32[4,32,2048]{2,1,0:T(8,128)S(1)} %copy-done, f32[4,32,2048]{2,1,0:T(8,128)S(1)} %copy-done.1, bf16[32,2048]{1,0:T(8,128)(2,1)S(1)} %collective-permute-done.refs_4_, ...), custom_call_target="tpu_custom_call" | custom-call | flops 31457280 | bytes 5767168 | tf_op jit(solution)/shard_map/pallas_call | solution.py:179
  53.3 0.0 all-to-all-done
  53.3 34.5 %all_to_all.18 = bf16[16,16,2048]{2,1,0:T(8,128)(2,1)S(1)} all-to-all(bf16[16,16,2048]{2,1,0:T(8,128)(2,1)S(1)} %bitcast.24), channel_id=1, replica_groups=mesh['runs'=2,'gx'=16] {'gx'}, dimensions={0} | all-to-all | bytes 2097152 | tf_op jit(solution)/shard_map/all_to_all | solution.py:225
  87.8 2.7 %pad_maximum_fusion = bf16[2,256,2048]{2,1,0:T(8,128)(2,1)} fusion(bf16[1,256,2048]{2,1,0:T(8,128)(2,1)S(1)} %bitcast.25, bf16[1,256,2048]{2,1,0:T(8,128)(2,1)} %bitcast.10), kind=kLoop, calls=%fused_computation | loop fusion | flops 1048576 | bytes 4194304 | tf_op jit(solution)/shard_map/stack | solution.py:231
  (5 shorter events, 0.1 us)
Async XLA Ops:
  0.6 1.5 %copy-start = (f32[4,32,2048]{2,1,0:T(8,128)S(1)}, f32[4,32,2048]{2,1,0:T(8,128)}, u32[]{:S(2)}) copy-start(f32[4,32,2048]{2,1,0:T(8,128)} %refs_2_.3) | copy-start | bytes 3145732
  0.6 1.8 %copy-start.1 = (f32[4,32,2048]{2,1,0:T(8,128)S(1)}, f32[4,32,2048]{2,1,0:T(8,128)}, u32[]{:S(2)}) copy-start(f32[4,32,2048]{2,1,0:T(8,128)} %refs_3_.3) | copy-start | bytes 3145732
  2.2 5.1 %copy-start.8 = (s32[2,128,1]{1,2,0:T(1,128)S(1)}, s32[2,128,1]{1,2,0:T(1,128)}, u32[]{:S(2)}) copy-start(s32[2,128,1]{1,2,0:T(1,128)} %param.7) | copy-start | bytes 3076
  2.2 9.0 %copy-start.2 = (f32[4,32,2048]{2,1,0:T(8,128)S(1)}, f32[4,32,2048]{2,1,0:T(8,128)}, u32[]{:S(2)}) copy-start(f32[4,32,2048]{2,1,0:T(8,128)} %refs_1_.1) | copy-start | bytes 3145732
  3.7 7.5 %collective-permute-start.1 = (bf16[32,2048]{1,0:T(8,128)(2,1)}, bf16[32,2048]{1,0:T(8,128)(2,1)S(1)}, u32[]{:S(2)}, u32[]{:S(2)}) collective-permute-start(bf16[32,2048]{1,0:T(8,128)(2,1)} %get-tuple-element.18), channel_id=1, source_target_pairs={{1,2},{3,4},{5,6},{7,8},{9,10},{11,12},{13,14},{2,1},{4,3},{6,5},{... | collective-permute-start | bytes 393224 | tf_op jit(solution)/shard_map/ppermute | solution.py:216
  6.4 4.7 %collective-permute-start = (bf16[32,2048]{1,0:T(8,128)(2,1)}, bf16[32,2048]{1,0:T(8,128)(2,1)S(1)}, u32[]{:S(2)}, u32[]{:S(2)}) collective-permute-start(bf16[32,2048]{1,0:T(8,128)(2,1)} %get-tuple-element.19), channel_id=1, source_target_pairs={{0,1},{1,0},{2,3},{3,2},{4,5},{5,4},{6,7},{7,6},{8,9},{9,8},{10,11... | collective-permute-start | bytes 393224 | tf_op jit(solution)/shard_map/ppermute | solution.py:216
  16.9 1.0 %copy-start.3 = (bf16[256,2048]{1,0:T(8,128)(2,1)}, bf16[256,2048]{1,0:T(8,128)(2,1)S(1)}, u32[]{:S(2)}) copy-start(bf16[256,2048]{1,0:T(8,128)(2,1)S(1)} %get-tuple-element.10) | copy-start | bytes 3145732
  17.9 1.0 %copy-start.4 = (f32[4,32,2048]{2,1,0:T(8,128)}, f32[4,32,2048]{2,1,0:T(8,128)S(1)}, u32[]{:S(2)}) copy-start(f32[4,32,2048]{2,1,0:T(8,128)S(1)} %get-tuple-element.7.refs_1_) | copy-start | bytes 3145732
  18.9 0.7 copy-start.6
  19.5 5.8 %copy-start.7 = (bf16[2,16,2048]{2,1,0:T(8,128)(2,1)S(1)}, bf16[2,16,2048]{2,1,0:T(8,128)(2,1)}, u32[]{:S(2)}) copy-start(bf16[2,16,2048]{2,1,0:T(8,128)(2,1)} %copy-done.6) | copy-start | bytes 393220
  19.5 33.8 %all-to-all-start = ((bf16[16,16,2048]{2,1,0:T(8,128)(2,1)}), bf16[16,16,2048]{2,1,0:T(8,128)(2,1)}, u32[]{:S(2)}, u32[]{:S(2)}) async-start(bf16[16,16,2048]{2,1,0:T(8,128)(2,1)} %bitcast.23), calls=%async_computation | async-start | bytes 2097152 | tf_op jit(solution)/shard_map/all_to_all | solution.py:225
  25.3 20.3 %collective-permute-start.3 = (bf16[16,2048]{1,0:T(8,128)(2,1)S(1)}, bf16[16,2048]{1,0:T(8,128)(2,1)S(1)}, u32[]{:S(2)}, u32[]{:S(2)}) collective-permute-start(bf16[16,2048]{1,0:T(8,128)(2,1)S(1)} %get-tuple-element.20), channel_id=1, source_target_pairs={{1,2},{3,4},{5,6},{7,8},{9,10},{11,12},{13,14},{2,1},{4,3},{6,5},{... | collective-permute-start | bytes 196616 | tf_op jit(solution)/shard_map/ppermute | solution.py:216
  28.7 17.0 %collective-permute-start.2 = (bf16[16,2048]{1,0:T(8,128)(2,1)S(1)}, bf16[16,2048]{1,0:T(8,128)(2,1)S(1)}, u32[]{:S(2)}, u32[]{:S(2)}) collective-permute-start(bf16[16,2048]{1,0:T(8,128)(2,1)S(1)} %get-tuple-element.21), channel_id=1, source_target_pairs={{0,1},{1,0},{2,3},{3,2},{4,5},{5,4},{6,7},{7,6},{8,9},{9,8},{10,11... | collective-permute-start | bytes 196616 | tf_op jit(solution)/shard_map/ppermute | solution.py:216
  45.6 1.2 %copy-start.5 = (f32[4,32,2048]{2,1,0:T(8,128)S(1)}, f32[4,32,2048]{2,1,0:T(8,128)}, u32[]{:S(2)}) copy-start(f32[4,32,2048]{2,1,0:T(8,128)} %copy-done.4) | copy-start | bytes 3145732

commit v2 on v1

v2 whole, which is shorter than its diff:
```python
import functools

import jax
import jax.numpy as jnp
from jax import lax
from jax.experimental import pallas as pl
from jax.experimental.pallas import tpu as pltpu
from jax.sharding import PartitionSpec as P

STEPS = 2
DT = 0.15
LANES = 128
TILE = 8
WIDE = 2 * LANES
VMEM = 48 * 1024 * 1024


def roll_rows(v, shift):
    shift = shift % v.shape[0]
    return pltpu.roll(v, shift, 0) if shift else v


def pack_kernel(u_top, k_top, r_top, u_bot, k_bot, r_bot, core_ref, chip_ref):
    levels, _, cells = u_top.shape
    even = lax.axis_index("gx") % 2 == 0
    row = lax.broadcasted_iota(jnp.int32, (TILE, LANES), 0)
    for j in range(0, cells, LANES):
        c = slice(j, j + LANES)
        top, bot = [], []
        last_top = last_bot = jnp.zeros((TILE, LANES), jnp.float32)
        for l in range(levels):
            u, k, r = u_top[l, :, c], k_top[l, :, c], r_top[l, :, c]
            top += [jnp.where(row < 6, u, roll_rows(r, 6)), jnp.where(row < 6, k, roll_rows(r, 4))]
            last_top = jnp.where(row == l, roll_rows(r, l - 4), last_top)
            u, k, r = u_bot[l, :, c], k_bot[l, :, c], r_bot[l, :, c]
            bot += [jnp.where(row >= 2, u, roll_rows(r, 2)), jnp.where(row >= 2, k, roll_rows(r, 4))]
            last_bot = jnp.where(row == l, roll_rows(r, l - 3), last_bot)
        top = jnp.concatenate(top + [last_top], 0).astype(jnp.bfloat16)
        bot = jnp.concatenate(bot + [last_bot], 0).astype(jnp.bfloat16)
        core_ref[:, c] = jnp.where(even, bot, top)
        chip_ref[:, c] = jnp.where(even, top, bot)


def pack_faces(u, k, r):
    levels, rows, cells = u.shape
    top = pl.BlockSpec((levels, TILE, cells), lambda i: (0, 0, 0))
    bot = pl.BlockSpec((levels, TILE, cells), lambda i: (0, rows // TILE - 1, 0))
    shape = ((2 * levels + 1) * TILE, cells)
    out = pl.BlockSpec(shape, lambda i: (0, 0))
    return pl.pallas_call(
        pack_kernel,
        grid=(1,),
        out_shape=[jax.ShapeDtypeStruct(shape, jnp.bfloat16)] * 2,
        in_specs=[top] * 3 + [bot] * 3,
        out_specs=[out] * 2,
        compiler_params=pltpu.CompilerParams(vmem_limit_bytes=16 * 1024 * 1024),
    )(u, k, r, u, k, r)


def step_kernel(first, u_ref, k_ref, r_ref, *refs):
    if first:
        core_ref, chip_ref, place_ref, state_out, pack_out, face_out, face = refs[:7]
        refs = refs[7:]
    else:
        face_ref, place_ref, state_out, pack_out = refs[:4]
        refs = refs[4:]
    u0, u1, u2, xp, xm, yp, ym, zp, lin, quad, new, packed, sems = refs
    levels, rows, cells = u_ref.shape
    ext = u0.shape[1]
    chunks = cells // LANES
    me, n = lax.axis_index("gx"), lax.axis_size("gx")
    even = me % 2 == 0
    row = lax.broadcasted_iota(jnp.int32, (TILE, LANES), 0)
    lane = lax.broadcasted_iota(jnp.int32, (ext, LANES), 1)
    if first:
        side = lax.broadcasted_iota(jnp.int32, (2 * TILE, LANES), 0) < TILE
    else:
        side = row < TILE // 2
    live = jnp.where(side, (me < n - 1).astype(jnp.int32), (me > 0).astype(jnp.int32)) > 0

    def cols(j):
        j = j % chunks
        return slice(j * LANES, (j + 1) * LANES)

    kk = u2
    for j in range(chunks):
        c = cols(j)
        if first:
            core, chip = core_ref[:, c].astype(jnp.float32), chip_ref[:, c].astype(jnp.float32)
            below, above = jnp.where(even, core, chip), jnp.where(even, chip, core)
            last = 2 * levels * TILE
            r_below, r_above = below[last:], above[last:]
        for l in range(levels):
            if first:
                s = 2 * l * TILE
                ub, kb = below[s : s + TILE], below[s + TILE : s + 2 * TILE]
                ua, ka = above[s : s + TILE], above[s + TILE : s + 2 * TILE]
                rb = jnp.where(row < 4, roll_rows(kb, 4), roll_rows(r_below, 4 - l))
                rb = jnp.where(row < 2, roll_rows(ub, 2), rb)
                ra = jnp.where(row >= 4, roll_rows(ka, 4), roll_rows(r_above, 3 - l))
                ra = jnp.where(row >= 6, roll_rows(ua, 6), ra)
                faces = [((rows, ub, kb, rb)), ((rows + TILE, ua, ka, ra))]
                face[1, l, :, c] = jnp.where(row < 4, kb, ka)
                face[2, l, :, c] = jnp.where(row < 4, rb, ra)
            else:
                faces = [(rows, face_ref[0, l, :, c], face_ref[1, l, :, c], face_ref[2, l, :, c])]
            kk[l, :rows, c] = k_ref[l, :, c]
            u0[l, :rows, c] = u_ref[l, :, c]
            quad[l, :rows, c] = DT * r_ref[l, :, c]
            for at, u, k, r in faces:
                u0[l, at : at + TILE, c] = u
                kk[l, at : at + TILE, c] = k
                quad[l, at : at + TILE, c] = DT * r

    def left_right(src, l):
        right, left, here = {}, {}, {}

        def rots(j):
            j = j % chunks
            if j not in here:
                v = src[l, :, cols(j)]
                here[j] = v
                right[j] = pltpu.roll(v, LANES - 1, 1)
                left[j] = pltpu.roll(v, 1, 1)
            return j

        def at(j):
            a, b, d = rots(j - 1), rots(j), rots(j + 1)
            return (
                here[b],
                jnp.where(lane == LANES - 1, right[d], right[b]),
                jnp.where(lane == 0, left[a], left[b]),
            )

        return at

    half = 0.5 * DT
    ats = [left_right(kk, l) for l in range(levels)]
    for j in range(chunks):
        c = cols(j)
        for l in range(levels):
            k, k_right, k_left = ats[l](j)
            a = half * (k + pltpu.roll(k, ext - 1, 0))
            b = pltpu.roll(a, 1, 0)
            d, e = half * (k + k_right), half * (k + k_left)
            xp[l, :, c], xm[l, :, c], yp[l, :, c], ym[l, :, c] = a, b, d, e
            total = a + b + d + e
            if l < levels - 1:
                f = half * (k + kk[l + 1, :, c])
                zp[l, :, c] = f
                total = total + f
            if l > 0:
                total = total + zp[l - 1, :, c]
            lin[l, :, c] = 1.0 + quad[l, :, c] - total

    def euler(src, ats, l, j):
        c = cols(j)
        u, u_right, u_left = ats[l](j)
        out = u * (lin[l, :, c] - quad[l, :, c] * u)
        out = out + xp[l, :, c] * pltpu.roll(u, ext - 1, 0) + xm[l, :, c] * pltpu.roll(u, 1, 0)
        out = out + yp[l, :, c] * u_right + ym[l, :, c] * u_left
        if l < levels - 1:
            out = out + zp[l, :, c] * src[l + 1, :, c]
        if l > 0:
            out = out + zp[l - 1, :, c] * src[l - 1, :, c]
        return out

    def masked(dst, l, c, v):
        dst[l, :rows, c] = v[:rows]
        dst[l, rows:, c] = jnp.where(live, v[rows:], 0.0)

    ats = [left_right(u0, l) for l in range(levels)]
    for j in range(chunks):
        for l in range(levels):
            masked(u1, l, cols(j), euler(u0, ats, l, j))
    ats = [left_right(u1, l) for l in range(levels)]
    for j in range(chunks):
        for l in range(levels):
            c = cols(j)
            masked(u2, l, c, 0.75 * u0[l, :, c] + 0.25 * euler(u1, ats, l, j))
    ats = [left_right(u2, l) for l in range(levels)]
    place = place_ref[...]
    copies = []

    def send(src, dst):
        copy = pltpu.make_async_copy(src, dst, sems.at[len(copies)])
        copy.start()
        copies.append(copy)

    per = WIDE // LANES
    for j in range(chunks):
        for l in range(levels):
            c = cols(j)
            v = (1.0 / 3.0) * u0[l, :, c] + (2.0 / 3.0) * euler(u2, ats, l, j)
            new[l, :, c] = v[:rows]
            if first:
                v = jnp.where(live, v[rows:], 0.0)
                face[0, l, :, c] = jnp.where(
                    row < 3, v[:TILE], jnp.where(row < 5, 0.0, v[TILE:])
                )
        if j % per == per - 1:
            c = slice((j + 1) * LANES - WIDE, (j + 1) * LANES)
            v = new[:, :, c].astype(jnp.bfloat16).reshape(levels * rows, WIDE)
            packed[:, c] = jnp.dot(place, v, preferred_element_type=jnp.float32).astype(
                jnp.bfloat16
            )
            send(packed.at[:, c], pack_out.at[:, c])
            send(new.at[:, :, c], state_out.at[:, :, c])
    if first:
        send(face, face_out)
    for copy in copies:
        copy.wait()


def step(first, state, kappa, rate, faces, place):
    levels, rows, cells = state.shape
    slots = place.shape[0]
    ext = (levels, rows + (2 * TILE if first else TILE), cells)
    out = [
        jax.ShapeDtypeStruct(state.shape, jnp.float32),
        jax.ShapeDtypeStruct((slots, cells), jnp.bfloat16),
    ]
    scratch = [pltpu.VMEM(ext, jnp.float32) for _ in range(10)] + [
        pltpu.VMEM(state.shape, jnp.float32),
        pltpu.VMEM((slots, cells), jnp.bfloat16),
        pltpu.SemaphoreType.DMA((2 * (cells // WIDE) + 1,)),
    ]
    if first:
        face = (3, levels, TILE, cells)
        out.append(jax.ShapeDtypeStruct(face, jnp.float32))
        scratch.insert(0, pltpu.VMEM(face, jnp.float32))
    return pl.pallas_call(
        functools.partial(step_kernel, first),
        out_shape=out,
        in_specs=[pl.BlockSpec(memory_space=pltpu.VMEM)] * (4 + len(faces)),
        out_specs=[pl.BlockSpec(memory_space=pltpu.HBM)] * len(out),
        scratch_shapes=scratch,
        compiler_params=pltpu.CompilerParams(vmem_limit_bytes=VMEM),
        cost_estimate=pl.CostEstimate(
            flops=120 * levels * rows * cells,
            bytes_accessed=22 * levels * rows * cells,
            transcendentals=0,
        ),
    )(state, kappa, rate, *faces, place)


def put_kernel(at, part_ref, *refs):
    out_ref, sem = refs[-2:]
    copy = pltpu.make_async_copy(part_ref, out_ref.at[at], sem)
    copy.start()
    copy.wait()


def put(at, part, whole=None):
    args = (part,) if whole is None else (part, whole)
    return pl.pallas_call(
        functools.partial(put_kernel, at),
        out_shape=jax.ShapeDtypeStruct((STEPS, *part.shape), part.dtype),
        in_specs=[pl.BlockSpec(memory_space=pl.ANY)] * len(args),
        out_specs=pl.BlockSpec(memory_space=pltpu.HBM),
        scratch_shapes=[pltpu.SemaphoreType.DMA],
        input_output_aliases={} if whole is None else {1: 0},
    )(*args)


def placing(dest, writers, per_dev):
    slots = 2 * per_dev
    capacity = slots // writers
    onehot = (dest == jnp.arange(writers, dtype=jnp.int32)[None, :]).astype(jnp.float32)
    row_ids = jnp.arange(per_dev, dtype=jnp.int32)
    lower = (row_ids[:, None] > row_ids[None, :]).astype(jnp.float32)
    before = jnp.dot(lower, onehot, preferred_element_type=jnp.float32)
    ranks = jnp.sum(before * onehot, axis=1).astype(jnp.int32)
    target = dest[:, 0] * capacity + ranks
    return (jnp.arange(slots, dtype=jnp.int32)[:, None] == target[None, :]).astype(jnp.bfloat16)


def shards(initial, kappa, rate, writer):
    n = lax.axis_size("gx")
    levels, rows, cells = initial.shape
    by_core = [(i, i ^ 1) for i in range(n)]
    by_chip = [(i, i + 1) for i in range(1, n - 1, 2)] + [(i + 1, i) for i in range(1, n - 1, 2)]
    to_core, to_chip = pack_faces(initial, kappa, rate)
    faces = (lax.ppermute(to_core, "gx", by_core), lax.ppermute(to_chip, "gx", by_chip))
    places = [placing(writer[s], n, levels * rows) for s in range(STEPS)]

    def route(packed):
        return lax.all_to_all(packed, "gx", split_axis=0, concat_axis=0, tiled=True)

    state, packed, face = step(True, initial, kappa, rate, faces, places[0])
    first = route(packed)
    state, packed = step(False, state, kappa, rate, (face,), places[1])
    second = route(packed)
    return state, put(1, second, put(0, first))


def solution(mesh):
    spec = P("runs", "gx", None)
    return jax.shard_map(
        shards, mesh=mesh, in_specs=(spec,) * 4, out_specs=(spec, spec), check_vma=False
    )
```

time: 92.3 us -> 131 us (1.42)
  Pallas kernels: 12.2 us -> 82.5 us
  blocking collectives: 34.5 us -> 0 us
  other arithmetic: 5.38 us -> 0.06 us
  starting transfers between devices: 13.1 us -> 16.5 us
  waiting for transfers between devices: 19.9 us -> 22.6 us
  local copies, waits for them, and re-layouts: 4.32 us -> 6.65 us
    pallas_call x2 -> x5, Pallas kernels: 12.2 us -> 82.5 us  [the longest x2 65.7 us: put(): pl.pallas_call(functools.partial(put_kernel, at), out_shape=jax.ShapeDtyp...]
    all_to_all x1 -> x0, blocking collectives: 34.5 us -> none  [route(): return lax.all_to_all(packed, 'gx', split_axis=0, concat_axis=0, tiled=True)]
    all_to_all x1 -> x2, waiting for transfers between devices: 0.01 us -> 17.3 us  [route(): return lax.all_to_all(packed, 'gx', split_axis=0, concat_axis=0, tiled=True)]
    ppermute x4 -> x2, waiting for transfers between devices: 19.9 us -> 5.35 us  [the longest x1 5.34 us: shards(): lax.ppermute(to_chip, 'gx', by_chip)]
    all_to_all x1 -> x2, starting transfers between devices: 5.81 us -> 13 us  [route(): return lax.all_to_all(packed, 'gx', split_axis=0, concat_axis=0, tiled=True)]
    another operation x5 -> x0, other arithmetic: 4.36 us -> none  [the longest x1 2.74 us: shards(): return (state, jnp.stack([first, route(packed)]))]
    ppermute x4 -> x2, starting transfers between devices: 7.33 us -> 3.47 us  [the longest x1 3.4 us: shards(): lax.ppermute(to_chip, 'gx', by_chip)]
    unnamed x18 -> x20, local copies, waits for them, and re-layouts: 4.14 us -> 6.65 us
  transfers between devices with their start and end apart: 5 -> 4, of which waited for: 2 -> 2; matrix products, arithmetic and copies ran while one was open for 1% -> 0% of each run, Pallas kernels for 7% -> 30%
where the time goes in v2:
time: 131 us; the launch traced here: 130 us
  Pallas kernels  82.5 us (63%)
  waiting for transfers between devices  22.6 us (17%)
  starting transfers between devices  16.5 us (13%)
  local copies, waits for them, and re-layouts  6.65 us (5%)
    pallas_call x2, Pallas kernels, put(): pl.pallas_call(functools.partial(put_kernel, at), out_shape=jax.ShapeDtyp...  65.7 us
    all_to_all x2, waiting for transfers between devices, route(): return lax.all_to_all(packed, 'gx', split_axis=0, concat_axis=0, tiled=True)  17.3 us
    pallas_call x2, Pallas kernels, step(): pl.pallas_call(functools.partial(step_kernel, first), out_shape=out, in_s...  16.5 us
    all_to_all x2, starting transfers between devices, route(): return lax.all_to_all(packed, 'gx', split_axis=0, concat_axis=0, tiled=True)  13 us
    unnamed x20, local copies, waits for them, and re-layouts  6.65 us
    ppermute x1, waiting for transfers between devices, shards(): lax.ppermute(to_chip, 'gx', by_chip)  5.34 us
    ppermute x1, starting transfers between devices, shards(): lax.ppermute(to_chip, 'gx', by_chip)  3.4 us
  transfers between devices with their start and end apart: 4, of which 2 were waited for; matrix products, arithmetic and copies ran while one was open for 0% of the time, Pallas kernels for 30%

profile of v2, /device:TPU:10, one launch (start us, length us, event | category | flops | bytes accessed | tf_op | source)
XLA Modules:
  0.0 129.6 jit_solution(4063290834481538649)
XLA Ops:
  0.6 0.0 copy-start
  0.6 1.2 copy-done
  1.9 0.0 copy-start.2
  1.9 1.2 copy-done.2
  3.1 0.0 copy-start.4
  3.1 1.2 copy-done.4
  4.3 0.0 copy-start.9
  4.3 0.0 copy-start.1
  4.3 0.0 copy-start.5
  4.3 0.2 shard_map.59
  4.5 0.1 collective-permute-start
  4.6 3.4 %collective-permute-start.1 = (bf16[72,2048]{1,0:T(8,128)(2,1)S(1)}, bf16[72,2048]{1,0:T(8,128)(2,1)S(1)}, u32[]{:S(2)}, u32[]{:S(2)}) collective-permute-start(bf16[72,2048]{1,0:T(8,128)(2,1)S(1)} %get-tuple-element.10), channel_id=1, source_target_pairs={{1,2},{3,4},{5,6},{7,8},{9,10},{11,12},{13,14},{2,1},{4,3},{6,5},{... | collective-permute-start | bytes 884744 | tf_op jit(solution)/shard_map/ppermute | solution.py:284
  8.0 0.0 copy-done.9
  8.0 0.2 fusion.1
  8.2 0.2 fusion
  8.4 0.0 collective-permute-done.refs_0_
  8.4 5.3 %collective-permute-done.1.refs_1_ = bf16[72,2048]{1,0:T(8,128)(2,1)S(1)} collective-permute-done((bf16[72,2048]{1,0:T(8,128)(2,1)S(1)}, bf16[72,2048]{1,0:T(8,128)(2,1)S(1)}, u32[]{:S(2)}, u32[]{:S(2)}) %collective-permute-start.1) | collective-permute-done | bytes 294944 | tf_op jit(solution)/shard_map/ppermute | solution.py:284
  13.8 0.0 copy-done.1
  13.8 0.0 copy-done.5
  13.8 0.0 copy-start.3
  13.8 10.6 %shard_map.60 = (f32[4,32,2048]{2,1,0:T(8,128)S(1)}, bf16[256,2048]{1,0:T(8,128)(2,1)}, f32[3,4,8,2048]{3,2,1,0:T(8,128)S(1)}) custom-call(f32[4,32,2048]{2,1,0:T(8,128)S(1)} %copy-done.5, f32[4,32,2048]{2,1,0:T(8,128)S(1)} %copy-done.1, f32[4,32,2048]{2,1,0:T(8,128)} %r_ref.3, bf16[72,2048]{1,0:T(8,128)(2,1)S(1)} %collective-permute-done.refs_0_, ...), custom_call_target="tpu_custom_call" | custom-call | flops 31457280 | bytes 5767168 | tf_op jit(solution)/shard_map/pallas_call | solution.py:232
  24.4 0.0 copy-start.6
  24.4 0.9 copy-done.6
  25.3 7.5 %all-to-all-start.1 = ((bf16[16,16,2048]{2,1,0:T(8,128)(2,1)}), bf16[16,16,2048]{2,1,0:T(8,128)(2,1)}, u32[]{:S(2)}, u32[]{:S(2)}) async-start(bf16[16,16,2048]{2,1,0:T(8,128)(2,1)} %bitcast.4), calls=%async_computation.1 | async-start | bytes 2097152 | tf_op jit(solution)/shard_map/all_to_all | solution.py:288
  32.8 0.0 copy-done.3
  32.8 0.0 copy-start.7
  32.8 1.1 copy-done.7
  33.9 5.9 %shard_map.61 = (f32[4,32,2048]{2,1,0:T(8,128)}, bf16[256,2048]{1,0:T(8,128)(2,1)}) custom-call(f32[4,32,2048]{2,1,0:T(8,128)S(1)} %get-tuple-element.11.u_ref, f32[4,32,2048]{2,1,0:T(8,128)S(1)} %copy-done.1, f32[4,32,2048]{2,1,0:T(8,128)S(1)} %copy-done.3, f32[3,4,8,2048]{3,2,1,0:T(8,128)S(1)} %copy-done.7, bf16[256,128]{1,0:T(8,128)(2,1)S(1)} %get-tuple-element.21.refs_1_), custom_call_target="tpu_custom_call" | custom-call | flops 31457280 | bytes 5767168 | tf_op jit(solution)/shard_map/pallas_call | solution.py:232
  39.8 17.3 %all-to-all-done.1 = bf16[16,16,2048]{2,1,0:T(8,128)(2,1)} async-done(((bf16[16,16,2048]{2,1,0:T(8,128)(2,1)}), bf16[16,16,2048]{2,1,0:T(8,128)(2,1)}, u32[]{:S(2)}, u32[]{:S(2)}) %all-to-all-start.1) | async-done | bytes 1048608 | tf_op jit(solution)/shard_map/all_to_all | solution.py:288
  57.1 5.6 %all-to-all-start = ((bf16[16,16,2048]{2,1,0:T(8,128)(2,1)}), bf16[16,16,2048]{2,1,0:T(8,128)(2,1)S(1)}, u32[]{:S(2)}, u32[]{:S(2)}) async-start(bf16[16,16,2048]{2,1,0:T(8,128)(2,1)} %bitcast.2), calls=%async_computation | async-start | bytes 2097152 | tf_op jit(solution)/shard_map/all_to_all | solution.py:288
  62.7 32.9 %shard_map.62.refs_0_ = bf16[2,256,2048]{2,1,0:T(8,128)(2,1)} custom-call(bf16[256,2048]{1,0:T(8,128)(2,1)} %bitcast.5.part_ref), custom_call_target="tpu_custom_call" | custom-call | tf_op jit(solution)/shard_map/pallas_call | solution.py:256
  95.6 0.0 all-to-all-done
  95.6 0.0 copy-start.8
  95.6 1.0 copy-done.8
  96.5 32.9 %shard_map.63 = bf16[2,256,2048]{2,1,0:T(8,128)(2,1)} custom-call(bf16[256,2048]{1,0:T(8,128)(2,1)} %bitcast.12, bf16[2,256,2048]{2,1,0:T(8,128)(2,1)} %shard_map.62.refs_0_), custom_call_target="tpu_custom_call", output_to_operand_aliasing={{}: (1, {})} | custom-call | tf_op jit(solution)/shard_map/pallas_call | solution.py:256
  (3 shorter events, 0.1 us)
Async XLA Ops:
  0.6 1.2 copy-start
  1.9 1.2 copy-start.2
  3.1 1.2 copy-start.4
  4.3 3.7 %copy-start.9 = (s32[2,128,1]{1,2,0:T(1,128)S(1)}, s32[2,128,1]{1,2,0:T(1,128)}, u32[]{:S(2)}) copy-start(s32[2,128,1]{1,2,0:T(1,128)} %param.7) | copy-start | bytes 3076
  4.3 9.5 %copy-start.1 = (f32[4,32,2048]{2,1,0:T(8,128)S(1)}, f32[4,32,2048]{2,1,0:T(8,128)}, u32[]{:S(2)}) copy-start(f32[4,32,2048]{2,1,0:T(8,128)} %k_ref.3) | copy-start | bytes 3145732
  4.3 9.5 %copy-start.5 = (f32[4,32,2048]{2,1,0:T(8,128)S(1)}, f32[4,32,2048]{2,1,0:T(8,128)}, u32[]{:S(2)}) copy-start(f32[4,32,2048]{2,1,0:T(8,128)} %u_ref.1) | copy-start | bytes 3145732
  4.5 3.9 %collective-permute-start = (bf16[72,2048]{1,0:T(8,128)(2,1)S(1)}, bf16[72,2048]{1,0:T(8,128)(2,1)S(1)}, u32[]{:S(2)}, u32[]{:S(2)}) collective-permute-start(bf16[72,2048]{1,0:T(8,128)(2,1)S(1)} %get-tuple-element.9), channel_id=1, source_target_pairs={{0,1},{1,0},{2,3},{3,2},{4,5},{5,4},{6,7},{7,6},{8,9},{9,8},{10,11... | collective-permute-start | bytes 884744 | tf_op jit(solution)/shard_map/ppermute | solution.py:284
  4.6 9.2 %collective-permute-start.1 = (bf16[72,2048]{1,0:T(8,128)(2,1)S(1)}, bf16[72,2048]{1,0:T(8,128)(2,1)S(1)}, u32[]{:S(2)}, u32[]{:S(2)}) collective-permute-start(bf16[72,2048]{1,0:T(8,128)(2,1)S(1)} %get-tuple-element.10), channel_id=1, source_target_pairs={{1,2},{3,4},{5,6},{7,8},{9,10},{11,12},{13,14},{2,1},{4,3},{6,5},{... | collective-permute-start | bytes 884744 | tf_op jit(solution)/shard_map/ppermute | solution.py:284
  13.8 19.0 %copy-start.3 = (f32[4,32,2048]{2,1,0:T(8,128)S(1)}, f32[4,32,2048]{2,1,0:T(8,128)}, u32[]{:S(2)}) copy-start(f32[4,32,2048]{2,1,0:T(8,128)} %r_ref.3) | copy-start | bytes 3145732
  24.4 0.9 copy-start.6
  25.3 31.8 %all-to-all-start.1 = ((bf16[16,16,2048]{2,1,0:T(8,128)(2,1)}), bf16[16,16,2048]{2,1,0:T(8,128)(2,1)}, u32[]{:S(2)}, u32[]{:S(2)}) async-start(bf16[16,16,2048]{2,1,0:T(8,128)(2,1)} %bitcast.4), calls=%async_computation.1 | async-start | bytes 2097152 | tf_op jit(solution)/shard_map/all_to_all | solution.py:288
  32.8 1.1 copy-start.7
  57.1 38.5 %all-to-all-start = ((bf16[16,16,2048]{2,1,0:T(8,128)(2,1)}), bf16[16,16,2048]{2,1,0:T(8,128)(2,1)S(1)}, u32[]{:S(2)}, u32[]{:S(2)}) async-start(bf16[16,16,2048]{2,1,0:T(8,128)(2,1)} %bitcast.2), calls=%async_computation | async-start | bytes 2097152 | tf_op jit(solution)/shard_map/all_to_all | solution.py:288
  95.6 1.0 copy-start.8

commit v3 on v2

v3 whole, which is shorter than its diff:
```python
import functools

import jax
import jax.numpy as jnp
from jax import lax
from jax.experimental import pallas as pl
from jax.experimental.pallas import tpu as pltpu
from jax.sharding import PartitionSpec as P

STEPS = 2
DT = 0.15
LANES = 128
TILE = 8
WIDE = 2 * LANES
VMEM = 30 * 1024 * 1024


def roll_rows(v, shift):
    shift = shift % v.shape[0]
    return pltpu.roll(v, shift, 0) if shift else v


def pack_kernel(u_ref, k_ref, r_ref, core_ref, chip_ref, deep_ref, top, bot, sems):
    levels, rows, cells = u_ref.shape
    copies = []
    for i, ref in enumerate((u_ref, k_ref, r_ref)):
        copies.append(pltpu.make_async_copy(ref.at[:, :TILE], top.at[i], sems.at[0, i]))
        copies.append(pltpu.make_async_copy(ref.at[:, rows - TILE :], bot.at[i], sems.at[1, i]))
    for copy in copies:
        copy.start()
    for copy in copies:
        copy.wait()
    even = lax.axis_index("gx") % 2 == 0
    row = lax.broadcasted_iota(jnp.int32, (TILE, LANES), 0)
    near = levels * TILE
    for j in range(0, cells, LANES):
        c = slice(j, j + LANES)
        first, last, deep_first, deep_last = [], [], [], []
        end_first = end_last = zero = jnp.zeros((TILE, LANES), jnp.float32)
        for l in range(levels):
            u, k, r = top[0, l, :, c], top[1, l, :, c], top[2, l, :, c]
            k5 = roll_rows(k, 5)
            first.append(jnp.where(row < 3, u, jnp.where(row < 5, roll_rows(r, 3), k5)))
            v = jnp.where(row < 3, k5, roll_rows(r, 4))
            deep_first.append(jnp.where((row < 3) | (row >= 6), v, u))
            end_first = jnp.where(row == l, roll_rows(r, l - 4), end_first)
            u, k, r = bot[0, l, :, c], bot[1, l, :, c], bot[2, l, :, c]
            k3 = roll_rows(k, 3)
            last.append(jnp.where(row < 5, jnp.where(row < 3, k3, roll_rows(r, 5)), u))
            v = jnp.where(row < 2, roll_rows(r, 4), k3)
            deep_last.append(jnp.where((row < 2) | (row >= 5), v, u))
            end_last = jnp.where(row == l, roll_rows(r, l - 3), end_last)
        a = jnp.concatenate(first + deep_first + [end_first, zero], 0)
        b = jnp.concatenate(last + deep_last + [end_last, zero], 0)
        core_ref[:, c] = jnp.where(even, b, a).astype(jnp.bfloat16)
        chip = jnp.where(even, a, b).astype(jnp.bfloat16)
        chip_ref[:, c] = chip[:near]
        deep_ref[:, c] = chip[near : near + deep_ref.shape[0]]


def pack_faces(u, k, r):
    levels, _, cells = u.shape
    hbm = pl.BlockSpec(memory_space=pltpu.HBM)
    sizes = [(2 * levels + 2) * TILE, levels * TILE, (levels + 2) * TILE]
    return pl.pallas_call(
        pack_kernel,
        out_shape=[jax.ShapeDtypeStruct((size, cells), jnp.bfloat16) for size in sizes],
        in_specs=[hbm] * 3,
        out_specs=[pl.BlockSpec(memory_space=pltpu.VMEM)] * 3,
        scratch_shapes=[pltpu.VMEM((3, levels, TILE, cells), jnp.float32)] * 2
        + [pltpu.SemaphoreType.DMA((2, 3))],
        compiler_params=pltpu.CompilerParams(vmem_limit_bytes=60 * 1024 * 1024),
    )(u, k, r)


def sections(shape, fill, live, done, u0, u1, u2, xp, xm, yp, ym, zp, lin, quad):
    levels, ext, cells = shape
    chunks = cells // LANES
    lane = lax.broadcasted_iota(jnp.int32, (ext, LANES), 1)

    def cols(j):
        j = j % chunks
        return slice(j * LANES, (j + 1) * LANES)

    kk = u2

    def left_right(src, l):
        right, left, here = {}, {}, {}

        def rots(j):
            j = j % chunks
            if j not in here:
                v = src[l, :, cols(j)]
                here[j] = v
                right[j] = pltpu.roll(v, LANES - 1, 1)
                left[j] = pltpu.roll(v, 1, 1)
            return j

        def at(j):
            a, b, d = rots(j - 1), rots(j), rots(j + 1)
            return (
                here[b],
                jnp.where(lane == LANES - 1, right[d], right[b]),
                jnp.where(lane == 0, left[a], left[b]),
            )

        return at

    half = 0.5 * DT
    ats = [left_right(kk, l) for l in range(levels)]
    filled = set()
    for j in range(chunks):
        for i in (j - 1, j, j + 1):
            if i % chunks not in filled:
                filled.add(i % chunks)
                fill(i % chunks, u0, kk, quad)
        c = cols(j)
        for l in range(levels):
            k, k_right, k_left = ats[l](j)
            a = half * (k + pltpu.roll(k, ext - 1, 0))
            b = pltpu.roll(a, 1, 0)
            d, e = half * (k + k_right), half * (k + k_left)
            xp[l, :, c], xm[l, :, c], yp[l, :, c], ym[l, :, c] = a, b, d, e
            total = a + b + d + e
            if l < levels - 1:
                f = half * (k + kk[l + 1, :, c])
                zp[l, :, c] = f
                total = total + f
            if l > 0:
                total = total + zp[l - 1, :, c]
            q = DT * quad[l, :, c]
            quad[l, :, c] = q
            lin[l, :, c] = 1.0 + q - total

    def euler(src, ats, l, j):
        c = cols(j)
        u, u_right, u_left = ats[l](j)
        out = u * (lin[l, :, c] - quad[l, :, c] * u)
        out = out + xp[l, :, c] * pltpu.roll(u, ext - 1, 0) + xm[l, :, c] * pltpu.roll(u, 1, 0)
        out = out + yp[l, :, c] * u_right + ym[l, :, c] * u_left
        if l < levels - 1:
            out = out + zp[l, :, c] * src[l + 1, :, c]
        if l > 0:
            out = out + zp[l - 1, :, c] * src[l - 1, :, c]
        return out

    def masked(dst, l, c, v):
        at = 0
        for start, stop, keep in live:
            if at < start:
                dst[l, at:start, c] = v[at:start]
            dst[l, start:stop, c] = jnp.where(keep, v[start:stop], 0.0)
            at = stop
        if at < ext:
            dst[l, at:, c] = v[at:]

    ats = [left_right(u0, l) for l in range(levels)]
    for j in range(chunks):
        for l in range(levels):
            masked(u1, l, cols(j), euler(u0, ats, l, j))
    ats = [left_right(u1, l) for l in range(levels)]
    for j in range(chunks):
        for l in range(levels):
            c = cols(j)
            masked(u2, l, c, 0.75 * u0[l, :, c] + 0.25 * euler(u1, ats, l, j))
    ats = [left_right(u2, l) for l in range(levels)]
    for j in range(chunks):
        c = cols(j)
        done(
            c,
            [
                (1.0 / 3.0) * u0[l, :, c] + (2.0 / 3.0) * euler(u2, ats, l, j)
                for l in range(levels)
            ],
        )


def grid_ends():
    me, n = lax.axis_index("gx"), lax.axis_size("gx")
    return (me < n - 1).astype(jnp.int32), (me > 0).astype(jnp.int32), me % 2 == 0


def sides(core, chip, even):
    core, chip = core.astype(jnp.float32), chip.astype(jnp.float32)
    return jnp.where(even, core, chip), jnp.where(even, chip, core)


def step_kernel(first, u_ref, k_ref, r_ref, core_ref, chip_ref, *refs):
    face_ref = None if first else refs[0]
    place_ref, state_out, *outs = refs[0 if first else 1 : -14]
    scratch, (new, packed, got, sems) = refs[-14:-4], refs[-4:]
    levels, rows, cells = u_ref.shape
    after, before, even = grid_ends()
    row = lax.broadcasted_iota(jnp.int32, (TILE, LANES), 0)
    side = row < TILE // 2
    per = WIDE // LANES
    groups = cells // WIDE
    u0, kk, quad = scratch[0], scratch[2], scratch[9]
    loads = {}
    for g in (groups - 1, *range(groups - 1)):
        c = slice(g * WIDE, (g + 1) * WIDE)
        loads[g] = [
            pltpu.make_async_copy(ref.at[:, :, c], to.at[:, :rows, c], got.at[i, g])
            for i, (ref, to) in enumerate(((k_ref, kk), (u_ref, u0), (r_ref, quad)))
        ]
        for load in loads[g]:
            load.start()

    def fill(j, u0, kk, quad):
        for load in loads.pop(j // per, ()):
            load.wait()
        c = slice(j * LANES, (j + 1) * LANES)
        near = levels * TILE
        below, above = sides(core_ref[:near, c], chip_ref[:, c], even)
        for l in range(levels):
            b, a = below[l * TILE : (l + 1) * TILE], above[l * TILE : (l + 1) * TILE]
            u0[l, rows:, c] = jnp.where(side, b, a) if first else face_ref[l, :, c]
            kk[l, rows:, c] = jnp.where(side, roll_rows(b, 3), roll_rows(a, 5))
            quad[l, rows:, c] = jnp.where(side, roll_rows(b, 5), roll_rows(a, 3))

    place = place_ref[...]
    copies = []

    def send(src, dst):
        copy = pltpu.make_async_copy(src, dst, sems.at[len(copies)])
        copy.start()
        copies.append(copy)

    def done(c, values):
        for l, v in enumerate(values):
            new[l, :, c] = v[:rows]
        if c.stop % WIDE == 0:
            c = slice(c.stop - WIDE, c.stop)
            send(new.at[:, :, c], state_out.at[:, :, c])
            v = new[:, :, c].astype(jnp.bfloat16).reshape(levels * rows, WIDE)
            v = jnp.dot(place, v, preferred_element_type=jnp.float32).astype(jnp.bfloat16)
            if first:
                packed[:, c] = v
                send(packed.at[:, c], outs[0].at[:, c])
            else:
                at = 0
                for out in outs:
                    out[:, c] = v[at : at + out.shape[0]]
                    at += out.shape[0]

    live = [(rows, rows + TILE, jnp.where(side, after, before) > 0)]
    sections((levels, rows + TILE, cells), fill, live, done, *scratch)
    for copy in copies:
        copy.wait()


def strip_kernel(u_ref, k_ref, r_ref, core_ref, chip_ref, deep_ref, face_ref, *refs):
    scratch, top, bot, sems = refs[:10], refs[10], refs[11], refs[12]
    levels, rows, cells = u_ref.shape
    copies = []
    for i, ref in enumerate((u_ref, k_ref, r_ref)):
        copies.append(pltpu.make_async_copy(ref.at[:, :TILE], top.at[i], sems.at[0, i]))
        copies.append(pltpu.make_async_copy(ref.at[:, rows - TILE :], bot.at[i], sems.at[1, i]))
    for copy in copies:
        copy.start()
    for copy in copies:
        copy.wait()
    after, before, even = grid_ends()
    row = lax.broadcasted_iota(jnp.int32, (TILE, LANES), 0)

    def fill(j, u0, kk, quad):
        c = slice(j * LANES, (j + 1) * LANES)
        near = levels * TILE
        below, above = sides(core_ref[:near, c], chip_ref[:, c], even)
        below2, above2 = sides(core_ref[near:, c], deep_ref[:, c], even)
        r_below, r_above = below2[near : near + TILE], above2[near : near + TILE]
        for l in range(levels):
            t = slice(l * TILE, (l + 1) * TILE)
            b, a, b2, a2 = below[t], above[t], below2[t], above2[t]
            rb = jnp.where(row < 4, roll_rows(b2, 4), roll_rows(r_below, 4 - l))
            ra = jnp.where(row >= 4, roll_rows(a2, 4), roll_rows(r_above, 3 - l))
            for at, u, k, r in (
                (0, bot[0, l, :, c], bot[1, l, :, c], bot[2, l, :, c]),
                (
                    TILE,
                    jnp.where(row < 3, b, b2),
                    roll_rows(jnp.where(row >= 5, b, b2), 3),
                    jnp.where(row < 2, roll_rows(b, 5), rb),
                ),
                (
                    2 * TILE,
                    jnp.where(row >= 5, a, a2),
                    roll_rows(jnp.where(row < 3, a, a2), 5),
                    jnp.where(row >= 6, roll_rows(a, 3), ra),
                ),
                (3 * TILE, top[0, l, :, c], top[1, l, :, c], top[2, l, :, c]),
            ):
                u0[l, at : at + TILE, c] = u
                kk[l, at : at + TILE, c] = k
                quad[l, at : at + TILE, c] = r

    keep_after = jnp.where(row < TILE, after, 0) > 0
    keep_before = jnp.where(row < TILE, before, 0) > 0

    def done(c, values):
        for l, v in enumerate(values):
            b = jnp.where(keep_after, v[TILE : 2 * TILE], 0.0)
            a = jnp.where(keep_before, v[2 * TILE : 3 * TILE], 0.0)
            face_ref[l, :, c] = jnp.where(row < 3, b, jnp.where(row < 5, 0.0, a))

    live = [(TILE, 2 * TILE, keep_after), (2 * TILE, 3 * TILE, keep_before)]
    sections((levels, 4 * TILE, cells), fill, live, done, *scratch)


def strip(u, k, r, packets):
    levels, _, cells = u.shape
    hbm, vmem = pl.BlockSpec(memory_space=pltpu.HBM), pl.BlockSpec(memory_space=pltpu.VMEM)
    return pl.pallas_call(
        strip_kernel,
        out_shape=jax.ShapeDtypeStruct((levels, TILE, cells), jnp.float32),
        in_specs=[hbm] * 3 + [vmem] * 3,
        out_specs=vmem,
        scratch_shapes=[pltpu.VMEM((levels, 4 * TILE, cells), jnp.float32)] * 10
        + [pltpu.VMEM((3, levels, TILE, cells), jnp.float32)] * 2
        + [pltpu.SemaphoreType.DMA((2, 3))],
        compiler_params=pltpu.CompilerParams(vmem_limit_bytes=VMEM),
        cost_estimate=pl.CostEstimate(
            flops=100 * levels * 4 * TILE * cells,
            bytes_accessed=22 * levels * 4 * TILE * cells,
            transcendentals=0,
        ),
    )(u, k, r, *packets)


def step(first, state, kappa, rate, faces, place, parts, limit):
    levels, rows, cells = state.shape
    slots = place.shape[0]
    out = [jax.ShapeDtypeStruct(state.shape, jnp.float32)]
    out += [jax.ShapeDtypeStruct((slots // parts, cells), jnp.bfloat16)] * parts
    vmem, hbm = pl.BlockSpec(memory_space=pltpu.VMEM), pl.BlockSpec(memory_space=pltpu.HBM)
    groups = cells // WIDE
    return pl.pallas_call(
        functools.partial(step_kernel, first),
        out_shape=out,
        in_specs=[hbm] * 3 + [vmem] * (1 + len(faces)),
        out_specs=[hbm] + [hbm if first else vmem] * parts,
        scratch_shapes=[pltpu.VMEM((levels, rows + TILE, cells), jnp.float32)] * 10
        + [
            pltpu.VMEM(state.shape, jnp.float32),
            pltpu.VMEM((slots, cells) if first else (16, LANES), jnp.bfloat16),
            pltpu.SemaphoreType.DMA((3, groups)),
            pltpu.SemaphoreType.DMA((2 * groups,)),
        ],
        compiler_params=pltpu.CompilerParams(vmem_limit_bytes=limit * 1024 * 1024),
        cost_estimate=pl.CostEstimate(
            flops=120 * levels * rows * cells,
            bytes_accessed=22 * levels * rows * cells,
            transcendentals=0,
        ),
    )(state, kappa, rate, *faces, place)


def vmem_call(kernel, args, out, **kw):
    vmem = pl.BlockSpec(memory_space=pltpu.VMEM)
    return pl.pallas_call(
        kernel,
        out_shape=out,
        in_specs=kw.pop("in_specs", [vmem] * len(args)),
        out_specs=kw.pop("out_specs", [vmem] * len(out)),
        compiler_params=pltpu.CompilerParams(vmem_limit_bytes=16 * 1024 * 1024),
        **kw,
    )(*args)


def weave_kernel(mine_ref, theirs_ref, *outs):
    odd = lax.axis_index("gx") % 2 == 1
    size = outs[0].shape[0] // 2
    for p, out in enumerate(outs):
        a, b = mine_ref[p * size : (p + 1) * size], theirs_ref[p * size : (p + 1) * size]
        out[:size] = jnp.where(odd, b, a)
        out[size:] = jnp.where(odd, a, b)


def put_kernel(part_ref, out_ref, sem):
    copy = pltpu.make_async_copy(part_ref, out_ref.at[0], sem)
    copy.start()
    copy.wait()


def put_blocks_kernel(which, *refs):
    blocks, out_ref, sems = refs[: len(which)], refs[-2], refs[-1]
    chip = lax.axis_index("gx") // 2
    copies = []
    for i, (p, ref) in enumerate(zip(which, blocks, strict=True)):
        size = ref.shape[0]
        at = pl.multiple_of((chip ^ p) * size, size)
        copies.append(
            pltpu.make_async_copy(ref, out_ref.at[1, pl.ds(at, size)], sems.at[i])
        )
    for copy in copies:
        copy.start()
    for copy in copies:
        copy.wait()


def placing(dest, block_of, writers, per_dev):
    slots = 2 * per_dev
    capacity = slots // writers
    onehot = (dest == jnp.arange(writers, dtype=jnp.int32)[None, :]).astype(jnp.float32)
    row_ids = jnp.arange(per_dev, dtype=jnp.int32)
    lower = (row_ids[:, None] > row_ids[None, :]).astype(jnp.float32)
    before = jnp.dot(lower, onehot, preferred_element_type=jnp.float32)
    ranks = jnp.sum(before * onehot, axis=1).astype(jnp.int32)
    target = block_of(dest[:, 0]) * capacity + ranks
    return (jnp.arange(slots, dtype=jnp.int32)[:, None] == target[None, :]).astype(jnp.bfloat16)


def shards(initial, kappa, rate, writer):
    n = lax.axis_size("gx")
    levels, rows, cells = initial.shape
    per_dev = levels * rows
    slots = 2 * per_dev
    capacity = slots // n
    by_core = [(i, i ^ 1) for i in range(n)]
    by_chip = [(i, i + 1) for i in range(1, n - 1, 2)] + [(i + 1, i) for i in range(1, n - 1, 2)]

    def route(packed):
        return lax.all_to_all(packed, "gx", split_axis=0, concat_axis=0, tiled=True)

    to_core, to_chip, deep = pack_faces(initial, kappa, rate)
    faces = [lax.ppermute(to_core, "gx", by_core), lax.ppermute(to_chip, "gx", by_chip)]
    deep = lax.ppermute(deep, "gx", by_chip)
    place = placing(writer[0], lambda d: d, n, per_dev)
    state, packed = step(True, initial, kappa, rate, faces, place, 1, 53)
    packed, deep = lax.optimization_barrier((packed, deep))
    first = route(packed)
    faces = faces + [strip(initial, kappa, rate, faces + [deep])]
    if capacity % 16 or n & (n - 1):
        place = placing(writer[1], lambda d: d, n, per_dev)
        state, packed = step(False, state, kappa, rate, faces, place, 1, 30)
        return state, jnp.stack([first, route(packed)])

    chips = n // 2
    me = lax.axis_index("gx")
    place = placing(writer[1], lambda d: ((d ^ me) & 1) * chips + ((d ^ me) >> 1), n, per_dev)
    state, mine, theirs = step(False, state, kappa, rate, faces, place, 2, 30)
    theirs = lax.ppermute(theirs, "gx", by_core)
    block = jax.ShapeDtypeStruct((2 * capacity, cells), jnp.bfloat16)
    frames = jax.ShapeDtypeStruct((STEPS, slots, cells), jnp.bfloat16)
    hbm = pl.BlockSpec(memory_space=pltpu.HBM)
    vmem = pl.BlockSpec(memory_space=pltpu.VMEM)
    blocks = vmem_call(weave_kernel, (mine, theirs), [block] * chips)
    got = [blocks[0]]
    for p in range(1, chips):
        got.append(lax.ppermute(blocks[p], "gx", [(i, i ^ (2 * p)) for i in range(n)]))
    (out,) = vmem_call(
        put_kernel,
        (first,),
        [frames],
        out_specs=[hbm],
        scratch_shapes=[pltpu.SemaphoreType.DMA],
    )
    (out,) = vmem_call(
        functools.partial(put_blocks_kernel, range(chips)),
        (*got, out),
        [frames],
        in_specs=[vmem] * chips + [hbm],
        out_specs=[hbm],
        scratch_shapes=[pltpu.SemaphoreType.DMA((chips,))],
        input_output_aliases={chips: 0},
    )
    return state, out


def solution(mesh):
    spec = P("runs", "gx", None)
    return jax.shard_map(
        shards, mesh=mesh, in_specs=(spec,) * 4, out_specs=(spec, spec), check_vma=False
    )
```

time: 131 us -> 75.8 us (0.58)
  Pallas kernels: 82.5 us -> 25.1 us
  starting transfers between devices: 16.5 us -> 23.5 us
  local copies, waits for them, and re-layouts: 6.65 us -> 2.48 us
    pallas_call x3 -> x5, Pallas kernels: 66 us -> 10.6 us  [the longest x1 4.85 us: strip(): pl.pallas_call(strip_kernel, out_shape=jax.ShapeDtypeStruct((levels, TILE...]
    ppermute x0 -> x9, waiting for transfers between devices: none -> 16.4 us  [the longest x7 14.6 us: shards(): lax.ppermute(blocks[p], 'gx', [(i, i ^ 2 * p) for i in range(n)])]
    ppermute x0 -> x9, starting transfers between devices: none -> 15.2 us  [the longest x7 11.3 us: shards(): lax.ppermute(blocks[p], 'gx', [(i, i ^ 2 * p) for i in range(n)])]
    all_to_all x2 -> x1, waiting for transfers between devices: 17.3 us -> 5.86 us  [route(): return lax.all_to_all(packed, 'gx', split_axis=0, concat_axis=0, tiled=True)]
    all_to_all x2 -> x1, starting transfers between devices: 13 us -> 5.47 us  [route(): return lax.all_to_all(packed, 'gx', split_axis=0, concat_axis=0, tiled=True)]
    ppermute x1, waiting for transfers between devices: 5.34 us -> 0.53 us  [shards(): lax.ppermute(to_chip, 'gx', by_chip)]
    unnamed x20 -> x16, local copies, waits for them, and re-layouts: 6.65 us -> 2.47 us
    pallas_call x2, Pallas kernels: 16.5 us -> 14.5 us  [step(): pl.pallas_call(functools.partial(step_kernel, first), out_shape=out, in_s...]
  transfers between devices with their start and end apart: 4 -> 12, of which waited for: 2 -> 9; matrix products, arithmetic and copies ran while one was open for 0% -> 1% of each run, Pallas kernels for 30% -> 29%
where the time goes in v3:
time: 75.8 us; the launch traced here: 75.5 us
  Pallas kernels  25.1 us (33%)
  starting transfers between devices  23.5 us (31%)
  waiting for transfers between devices  23 us (30%)
  local copies, waits for them, and re-layouts  2.48 us (3%)
  between operations  0.97 us (1%)
    ppermute x7, waiting for transfers between devices, shards(): lax.ppermute(blocks[p], 'gx', [(i, i ^ 2 * p) for i in range(n)])  14.6 us
    pallas_call x2, Pallas kernels, step(): pl.pallas_call(functools.partial(step_kernel, first), out_shape=out, in_s...  14.5 us
    ppermute x7, starting transfers between devices, shards(): lax.ppermute(blocks[p], 'gx', [(i, i ^ 2 * p) for i in range(n)])  11.3 us
    all_to_all x1, waiting for transfers between devices, route(): return lax.all_to_all(packed, 'gx', split_axis=0, concat_axis=0, tiled=True)  5.86 us
    all_to_all x1, starting transfers between devices, route(): return lax.all_to_all(packed, 'gx', split_axis=0, concat_axis=0, tiled=True)  5.47 us
    pallas_call x1, Pallas kernels, strip(): pl.pallas_call(strip_kernel, out_shape=jax.ShapeDtypeStruct((levels, TILE...  4.85 us
    ppermute x1, starting transfers between devices, shards(): deep = lax.ppermute(deep, 'gx', by_chip)  3.71 us
    pallas_call x3, Pallas kernels, vmem_call(): pl.pallas_call(kernel, out_shape=out, in_specs=kw.pop('in_specs', [vmem]...  3.3 us
  transfers between devices with their start and end apart: 12, of which 9 were waited for; matrix products, arithmetic and copies ran while one was open for 1% of the time, Pallas kernels for 29%

profile of v3, /device:TPU:10, one launch (start us, length us, event | category | flops | bytes accessed | tf_op | source)
XLA Modules:
  0.0 75.5 jit_solution(16673771797863743699)
XLA Ops:
  0.6 0.0 copy-start.7
  0.6 2.5 %shard_map.59 = (bf16[80,2048]{1,0:T(8,128)(2,1)}, bf16[32,2048]{1,0:T(8,128)(2,1)}, bf16[48,2048]{1,0:T(8,128)(2,1)}) custom-call(f32[4,32,2048]{2,1,0:T(8,128)} %u_ref.5, f32[4,32,2048]{2,1,0:T(8,128)} %k_ref.7, f32[4,32,2048]{2,1,0:T(8,128)} %r_ref.7), custom_call_target="tpu_custom_call" | custom-call | tf_op jit(solution)/shard_map/pallas_call | solution.py:65
  3.1 2.8 %collective-permute-start.1 = (bf16[32,2048]{1,0:T(8,128)(2,1)}, bf16[32,2048]{1,0:T(8,128)(2,1)S(1)}, u32[]{:S(2)}, u32[]{:S(2)}) collective-permute-start(bf16[32,2048]{1,0:T(8,128)(2,1)} %get-tuple-element.21), channel_id=1, source_target_pairs={{1,2},{3,4},{5,6},{7,8},{9,10},{11,12},{13,14},{2,1},{4,3},{6,5},{... | collective-permute-start | bytes 393224 | tf_op jit(solution)/shard_map/ppermute | solution.py:426
  5.9 3.7 %collective-permute-start.2 = (bf16[48,2048]{1,0:T(8,128)(2,1)}, bf16[48,2048]{1,0:T(8,128)(2,1)}, u32[]{:S(2)}, u32[]{:S(2)}) collective-permute-start(bf16[48,2048]{1,0:T(8,128)(2,1)} %get-tuple-element.24), channel_id=1, source_target_pairs={{1,2},{3,4},{5,6},{7,8},{9,10},{11,12},{13,14},{2,1},{4,3},{6,5},{... | collective-permute-start | bytes 589832 | tf_op jit(solution)/shard_map/ppermute | solution.py:427
  9.6 0.1 collective-permute-start
  9.7 0.0 copy-done.7
  9.7 0.2 fusion.1
  9.8 0.2 fusion
  10.1 0.5 collective-permute-done.1.chip_ref
  10.6 0.0 copy-start.3
  10.6 0.7 copy-done.3
  11.3 0.2 collective-permute-done.core_ref
  11.5 0.0 copy-start.4
  11.5 0.9 %copy-done.4 = bf16[32,2048]{1,0:T(8,128)(2,1)S(1)} copy-done((bf16[32,2048]{1,0:T(8,128)(2,1)S(1)}, bf16[32,2048]{1,0:T(8,128)(2,1)}, u32[]{:S(2)}) %copy-start.4) | copy-done | bytes 131096
  12.4 0.0 copy-start
  12.4 0.0 copy-start.1
  12.4 0.0 copy-start.2
  12.4 7.8 %shard_map.60 = (f32[4,32,2048]{2,1,0:T(8,128)}, bf16[256,2048]{1,0:T(8,128)(2,1)}) custom-call(f32[4,32,2048]{2,1,0:T(8,128)} %u_ref.5, f32[4,32,2048]{2,1,0:T(8,128)} %k_ref.7, f32[4,32,2048]{2,1,0:T(8,128)} %r_ref.7, bf16[80,2048]{1,0:T(8,128)(2,1)S(1)} %collective-permute-done.core_ref, bf16[32,2048]{1,0:T(8,128)(2,1)S(1)} %copy-done.4, ...), custom_call_target="tpu_custom_call" | custom-call | flops 31457280 | bytes 5767168 | tf_op jit(solution)/shard_map/pallas_call | solution.py:337
  20.2 0.0 collective-permute-done.2.deep_ref
  20.2 5.5 %all-to-all-start = ((bf16[16,16,2048]{2,1,0:T(8,128)(2,1)}), bf16[16,16,2048]{2,1,0:T(8,128)(2,1)}, u32[]{:S(2)}, u32[]{:S(2)}) async-start(bf16[16,16,2048]{2,1,0:T(8,128)(2,1)} %bitcast.10), calls=%async_computation | async-start | bytes 2097152 | tf_op jit(solution)/shard_map/all_to_all | solution.py:423
  25.7 0.0 copy-done
  25.7 0.0 copy-done.1
  25.7 0.0 copy-done.2
  25.7 0.0 copy-start.5
  25.7 0.9 %copy-done.5 = bf16[32,2048]{1,0:T(8,128)(2,1)S(1)} copy-done((bf16[32,2048]{1,0:T(8,128)(2,1)S(1)}, bf16[32,2048]{1,0:T(8,128)(2,1)}, u32[]{:S(2)}) %copy-start.5) | copy-done | bytes 131096
  26.6 4.9 %shard_map.61.refs_0_ = f32[4,8,2048]{2,1,0:T(8,128)S(1)} custom-call(f32[4,32,2048]{2,1,0:T(8,128)S(1)} %copy-done.2, f32[4,32,2048]{2,1,0:T(8,128)S(1)} %copy-done, f32[4,32,2048]{2,1,0:T(8,128)S(1)} %copy-done.1, bf16[80,2048]{1,0:T(8,128)(2,1)S(1)} %collective-permute-done.core_ref, bf16[32,2048]{1,0:T(8,128)(2,1)S(1)} %copy-done.5, ...), custom_call_target="tpu_custom_call" | custom-call | flops 26214400 | bytes 5767168 | tf_op jit(solution)/shard_map/pallas_call | solution.py:313
  31.5 0.0 copy-done.6
  31.5 6.8 %shard_map.62 = (f32[4,32,2048]{2,1,0:T(8,128)}, bf16[128,2048]{1,0:T(8,128)(2,1)S(1)}, bf16[128,2048]{1,0:T(8,128)(2,1)S(1)}) custom-call(f32[4,32,2048]{2,1,0:T(8,128)S(1)} %copy-done.6, f32[4,32,2048]{2,1,0:T(8,128)S(1)} %copy-done, f32[4,32,2048]{2,1,0:T(8,128)S(1)} %copy-done.1, bf16[80,2048]{1,0:T(8,128)(2,1)S(1)} %collective-permute-done.core_ref, ...), custom_call_target="tpu_custom_call" | custom-call | flops 31457280 | bytes 5767168 | tf_op jit(solution)/shard_map/pallas_call | solution.py:337
  38.2 0.2 collective-permute-start.3
  38.4 1.8 %collective-permute-done.3.theirs_ref = bf16[128,2048]{1,0:T(8,128)(2,1)S(1)} collective-permute-done((bf16[128,2048]{1,0:T(8,128)(2,1)S(1)}, bf16[128,2048]{1,0:T(8,128)(2,1)S(1)}, u32[]{:S(2)}, u32[]{:S(2)}) %collective-permute-start.3) | collective-permute-done | bytes 524320 | tf_op jit(solution)/shard_map/ppermute | solution.py:442
  40.2 0.1 shard_map.63
  40.3 1.5 %collective-permute-start.4 = (bf16[32,2048]{1,0:T(8,128)(2,1)S(1)}, bf16[32,2048]{1,0:T(8,128)(2,1)S(1)}, u32[]{:S(2)}, u32[]{:S(2)}) collective-permute-start(bf16[32,2048]{1,0:T(8,128)(2,1)S(1)} %get-tuple-element.30), channel_id=1, source_target_pairs={{0,2},{1,3},{2,0},{3,1},{4,6},{5,7},{6,4},{7,5},{8,10},{9,11},{10,... | collective-permute-start | bytes 393224 | tf_op jit(solution)/shard_map/ppermute | solution.py:450
  41.8 0.6 collective-permute-start.5
  42.4 1.5 %collective-permute-start.6 = (bf16[32,2048]{1,0:T(8,128)(2,1)S(1)}, bf16[32,2048]{1,0:T(8,128)(2,1)S(1)}, u32[]{:S(2)}, u32[]{:S(2)}) collective-permute-start(bf16[32,2048]{1,0:T(8,128)(2,1)S(1)} %get-tuple-element.32), channel_id=1, source_target_pairs={{0,6},{1,7},{2,4},{3,5},{4,2},{5,3},{6,0},{7,1},{8,14},{9,15},{10,... | collective-permute-start | bytes 393224 | tf_op jit(solution)/shard_map/ppermute | solution.py:450
  43.9 2.4 %collective-permute-start.7 = (bf16[32,2048]{1,0:T(8,128)(2,1)S(1)}, bf16[32,2048]{1,0:T(8,128)(2,1)S(1)}, u32[]{:S(2)}, u32[]{:S(2)}) collective-permute-start(bf16[32,2048]{1,0:T(8,128)(2,1)S(1)} %get-tuple-element.33), channel_id=1, source_target_pairs={{0,8},{1,9},{2,10},{3,11},{4,12},{5,13},{6,14},{7,15},{8,0},{9,1},... | collective-permute-start | bytes 393224 | tf_op jit(solution)/shard_map/ppermute | solution.py:450
  46.2 1.5 %collective-permute-start.8 = (bf16[32,2048]{1,0:T(8,128)(2,1)S(1)}, bf16[32,2048]{1,0:T(8,128)(2,1)S(1)}, u32[]{:S(2)}, u32[]{:S(2)}) collective-permute-start(bf16[32,2048]{1,0:T(8,128)(2,1)S(1)} %get-tuple-element.34), channel_id=1, source_target_pairs={{0,10},{1,11},{2,8},{3,9},{4,14},{5,15},{6,12},{7,13},{8,2},{9,3},... | collective-permute-start | bytes 393224 | tf_op jit(solution)/shard_map/ppermute | solution.py:450
  47.7 3.2 %collective-permute-done.4.refs_1_ = bf16[32,2048]{1,0:T(8,128)(2,1)S(1)} collective-permute-done((bf16[32,2048]{1,0:T(8,128)(2,1)S(1)}, bf16[32,2048]{1,0:T(8,128)(2,1)S(1)}, u32[]{:S(2)}, u32[]{:S(2)}) %collective-permute-start.4) | collective-permute-done | bytes 131104 | tf_op jit(solution)/shard_map/ppermute | solution.py:450
  50.9 1.1 %collective-permute-start.9 = (bf16[32,2048]{1,0:T(8,128)(2,1)S(1)}, bf16[32,2048]{1,0:T(8,128)(2,1)S(1)}, u32[]{:S(2)}, u32[]{:S(2)}) collective-permute-start(bf16[32,2048]{1,0:T(8,128)(2,1)S(1)} %get-tuple-element.35), channel_id=1, source_target_pairs={{0,12},{1,13},{2,14},{3,15},{4,8},{5,9},{6,10},{7,11},{8,4},{9,5},... | collective-permute-start | bytes 393224 | tf_op jit(solution)/shard_map/ppermute | solution.py:450
  51.9 0.0 collective-permute-done.5.refs_2_
  51.9 2.8 %collective-permute-start.10 = (bf16[32,2048]{1,0:T(8,128)(2,1)S(1)}, bf16[32,2048]{1,0:T(8,128)(2,1)S(1)}, u32[]{:S(2)}, u32[]{:S(2)}) collective-permute-start(bf16[32,2048]{1,0:T(8,128)(2,1)S(1)} %get-tuple-element.36), channel_id=1, source_target_pairs={{0,14},{1,15},{2,12},{3,13},{4,10},{5,11},{6,8},{7,9},{8,6},{9,7},... | collective-permute-start | bytes 393224 | tf_op jit(solution)/shard_map/ppermute | solution.py:450
  54.8 5.9 %all-to-all-done = bf16[16,16,2048]{2,1,0:T(8,128)(2,1)} async-done(((bf16[16,16,2048]{2,1,0:T(8,128)(2,1)}), bf16[16,16,2048]{2,1,0:T(8,128)(2,1)}, u32[]{:S(2)}, u32[]{:S(2)}) %all-to-all-start) | async-done | bytes 1048608 | tf_op jit(solution)/shard_map/all_to_all | solution.py:423
  60.6 2.2 %shard_map.64.refs_8_ = bf16[2,256,2048]{2,1,0:T(8,128)(2,1)} custom-call(bf16[256,2048]{1,0:T(8,128)(2,1)} %bitcast.3.part_ref), custom_call_target="tpu_custom_call" | custom-call | tf_op jit(solution)/shard_map/pallas_call | solution.py:360
  62.9 0.0 collective-permute-done.6.refs_3_
  62.9 0.6 collective-permute-done.7.refs_4_
  63.5 2.8 %collective-permute-done.8.refs_5_ = bf16[32,2048]{1,0:T(8,128)(2,1)S(1)} collective-permute-done((bf16[32,2048]{1,0:T(8,128)(2,1)S(1)}, bf16[32,2048]{1,0:T(8,128)(2,1)S(1)}, u32[]{:S(2)}, u32[]{:S(2)}) %collective-permute-start.8) | collective-permute-done | bytes 131104 | tf_op jit(solution)/shard_map/ppermute | solution.py:450
  66.3 4.7 %collective-permute-done.9.refs_6_ = bf16[32,2048]{1,0:T(8,128)(2,1)S(1)} collective-permute-done((bf16[32,2048]{1,0:T(8,128)(2,1)S(1)}, bf16[32,2048]{1,0:T(8,128)(2,1)S(1)}, u32[]{:S(2)}, u32[]{:S(2)}) %collective-permute-start.9) | collective-permute-done | bytes 131104 | tf_op jit(solution)/shard_map/ppermute | solution.py:450
  71.0 3.3 %collective-permute-done.10.refs_7_ = bf16[32,2048]{1,0:T(8,128)(2,1)S(1)} collective-permute-done((bf16[32,2048]{1,0:T(8,128)(2,1)S(1)}, bf16[32,2048]{1,0:T(8,128)(2,1)S(1)}, u32[]{:S(2)}, u32[]{:S(2)}) %collective-permute-start.10) | collective-permute-done | bytes 131104 | tf_op jit(solution)/shard_map/ppermute | solution.py:450
  74.3 1.0 %shard_map.65 = bf16[2,256,2048]{2,1,0:T(8,128)(2,1)} custom-call(bf16[32,2048]{1,0:T(8,128)(2,1)S(1)} %get-tuple-element.29.refs_0_, bf16[32,2048]{1,0:T(8,128)(2,1)S(1)} %collective-permute-done.4.refs_1_, bf16[32,2048]{1,0:T(8,128)(2,1)S(1)} %collective-permute-done.5.refs_2_, ...), custom_call_target="tpu_custom_call", output_to_operand_aliasing={{}: (8, {})} | custom-call | tf_op jit(solution)/shard_map/pallas_call | solution.py:360
  (4 shorter events, 0.1 us)
Async XLA Ops:
  0.6 9.0 %copy-start.7 = (s32[2,128,1]{1,2,0:T(1,128)S(1)}, s32[2,128,1]{1,2,0:T(1,128)}, u32[]{:S(2)}) copy-start(s32[2,128,1]{1,2,0:T(1,128)} %param.7) | copy-start | bytes 3076
  3.1 7.5 %collective-permute-start.1 = (bf16[32,2048]{1,0:T(8,128)(2,1)}, bf16[32,2048]{1,0:T(8,128)(2,1)S(1)}, u32[]{:S(2)}, u32[]{:S(2)}) collective-permute-start(bf16[32,2048]{1,0:T(8,128)(2,1)} %get-tuple-element.21), channel_id=1, source_target_pairs={{1,2},{3,4},{5,6},{7,8},{9,10},{11,12},{13,14},{2,1},{4,3},{6,5},{... | collective-permute-start | bytes 393224 | tf_op jit(solution)/shard_map/ppermute | solution.py:426
  5.9 14.3 %collective-permute-start.2 = (bf16[48,2048]{1,0:T(8,128)(2,1)}, bf16[48,2048]{1,0:T(8,128)(2,1)}, u32[]{:S(2)}, u32[]{:S(2)}) collective-permute-start(bf16[48,2048]{1,0:T(8,128)(2,1)} %get-tuple-element.24), channel_id=1, source_target_pairs={{1,2},{3,4},{5,6},{7,8},{9,10},{11,12},{13,14},{2,1},{4,3},{6,5},{... | collective-permute-start | bytes 589832 | tf_op jit(solution)/shard_map/ppermute | solution.py:427
  9.6 1.9 %collective-permute-start = (bf16[80,2048]{1,0:T(8,128)(2,1)}, bf16[80,2048]{1,0:T(8,128)(2,1)S(1)}, u32[]{:S(2)}, u32[]{:S(2)}) collective-permute-start(bf16[80,2048]{1,0:T(8,128)(2,1)} %get-tuple-element.20), channel_id=1, source_target_pairs={{0,1},{1,0},{2,3},{3,2},{4,5},{5,4},{6,7},{7,6},{8,9},{9,8},{10,11... | collective-permute-start | bytes 983048 | tf_op jit(solution)/shard_map/ppermute | solution.py:426
  10.6 0.7 copy-start.3
  11.5 0.9 %copy-start.4 = (bf16[32,2048]{1,0:T(8,128)(2,1)S(1)}, bf16[32,2048]{1,0:T(8,128)(2,1)}, u32[]{:S(2)}) copy-start(bf16[32,2048]{1,0:T(8,128)(2,1)} %copy-done.3) | copy-start | bytes 393220
  12.4 13.3 %copy-start = (f32[4,32,2048]{2,1,0:T(8,128)S(1)}, f32[4,32,2048]{2,1,0:T(8,128)}, u32[]{:S(2)}) copy-start(f32[4,32,2048]{2,1,0:T(8,128)} %k_ref.7) | copy-start | bytes 3145732
  12.4 13.3 %copy-start.1 = (f32[4,32,2048]{2,1,0:T(8,128)S(1)}, f32[4,32,2048]{2,1,0:T(8,128)}, u32[]{:S(2)}) copy-start(f32[4,32,2048]{2,1,0:T(8,128)} %r_ref.7) | copy-start | bytes 3145732
  12.4 13.3 %copy-start.2 = (f32[4,32,2048]{2,1,0:T(8,128)S(1)}, f32[4,32,2048]{2,1,0:T(8,128)}, u32[]{:S(2)}) copy-start(f32[4,32,2048]{2,1,0:T(8,128)} %u_ref.5) | copy-start | bytes 3145732
  20.2 40.4 %all-to-all-start = ((bf16[16,16,2048]{2,1,0:T(8,128)(2,1)}), bf16[16,16,2048]{2,1,0:T(8,128)(2,1)}, u32[]{:S(2)}, u32[]{:S(2)}) async-start(bf16[16,16,2048]{2,1,0:T(8,128)(2,1)} %bitcast.10), calls=%async_computation | async-start | bytes 2097152 | tf_op jit(solution)/shard_map/all_to_all | solution.py:423
  25.7 0.9 %copy-start.5 = (bf16[32,2048]{1,0:T(8,128)(2,1)S(1)}, bf16[32,2048]{1,0:T(8,128)(2,1)}, u32[]{:S(2)}) copy-start(bf16[32,2048]{1,0:T(8,128)(2,1)} %copy-done.3) | copy-start | bytes 393220
  26.6 4.9 %copy-start.6 = (f32[4,32,2048]{2,1,0:T(8,128)S(1)}, f32[4,32,2048]{2,1,0:T(8,128)}, u32[]{:S(2)}) copy-start(f32[4,32,2048]{2,1,0:T(8,128)} %get-tuple-element.22.u_ref) | copy-start | bytes 3145732
  38.2 2.0 %collective-permute-start.3 = (bf16[128,2048]{1,0:T(8,128)(2,1)S(1)}, bf16[128,2048]{1,0:T(8,128)(2,1)S(1)}, u32[]{:S(2)}, u32[]{:S(2)}) collective-permute-start(bf16[128,2048]{1,0:T(8,128)(2,1)S(1)} %get-tuple-element.28), channel_id=1, source_target_pairs={{0,1},{1,0},{2,3},{3,2},{4,5},{5,4},{6,7},{7,6},{8,9},{9,8},{10,11... | collective-permute-start | bytes 1572872 | tf_op jit(solution)/shard_map/ppermute | solution.py:442
  40.3 10.6 %collective-permute-start.4 = (bf16[32,2048]{1,0:T(8,128)(2,1)S(1)}, bf16[32,2048]{1,0:T(8,128)(2,1)S(1)}, u32[]{:S(2)}, u32[]{:S(2)}) collective-permute-start(bf16[32,2048]{1,0:T(8,128)(2,1)S(1)} %get-tuple-element.30), channel_id=1, source_target_pairs={{0,2},{1,3},{2,0},{3,1},{4,6},{5,7},{6,4},{7,5},{8,10},{9,11},{10,... | collective-permute-start | bytes 393224 | tf_op jit(solution)/shard_map/ppermute | solution.py:450
  41.8 10.1 %collective-permute-start.5 = (bf16[32,2048]{1,0:T(8,128)(2,1)S(1)}, bf16[32,2048]{1,0:T(8,128)(2,1)S(1)}, u32[]{:S(2)}, u32[]{:S(2)}) collective-permute-start(bf16[32,2048]{1,0:T(8,128)(2,1)S(1)} %get-tuple-element.31), channel_id=1, source_target_pairs={{0,4},{1,5},{2,6},{3,7},{4,0},{5,1},{6,2},{7,3},{8,12},{9,13},{10,... | collective-permute-start | bytes 393224 | tf_op jit(solution)/shard_map/ppermute | solution.py:450
  42.4 20.5 %collective-permute-start.6 = (bf16[32,2048]{1,0:T(8,128)(2,1)S(1)}, bf16[32,2048]{1,0:T(8,128)(2,1)S(1)}, u32[]{:S(2)}, u32[]{:S(2)}) collective-permute-start(bf16[32,2048]{1,0:T(8,128)(2,1)S(1)} %get-tuple-element.32), channel_id=1, source_target_pairs={{0,6},{1,7},{2,4},{3,5},{4,2},{5,3},{6,0},{7,1},{8,14},{9,15},{10,... | collective-permute-start | bytes 393224 | tf_op jit(solution)/shard_map/ppermute | solution.py:450
  43.9 19.6 %collective-permute-start.7 = (bf16[32,2048]{1,0:T(8,128)(2,1)S(1)}, bf16[32,2048]{1,0:T(8,128)(2,1)S(1)}, u32[]{:S(2)}, u32[]{:S(2)}) collective-permute-start(bf16[32,2048]{1,0:T(8,128)(2,1)S(1)} %get-tuple-element.33), channel_id=1, source_target_pairs={{0,8},{1,9},{2,10},{3,11},{4,12},{5,13},{6,14},{7,15},{8,0},{9,1},... | collective-permute-start | bytes 393224 | tf_op jit(solution)/shard_map/ppermute | solution.py:450
  46.2 20.1 %collective-permute-start.8 = (bf16[32,2048]{1,0:T(8,128)(2,1)S(1)}, bf16[32,2048]{1,0:T(8,128)(2,1)S(1)}, u32[]{:S(2)}, u32[]{:S(2)}) collective-permute-start(bf16[32,2048]{1,0:T(8,128)(2,1)S(1)} %get-tuple-element.34), channel_id=1, source_target_pairs={{0,10},{1,11},{2,8},{3,9},{4,14},{5,15},{6,12},{7,13},{8,2},{9,3},... | collective-permute-start | bytes 393224 | tf_op jit(solution)/shard_map/ppermute | solution.py:450
  50.9 20.2 %collective-permute-start.9 = (bf16[32,2048]{1,0:T(8,128)(2,1)S(1)}, bf16[32,2048]{1,0:T(8,128)(2,1)S(1)}, u32[]{:S(2)}, u32[]{:S(2)}) collective-permute-start(bf16[32,2048]{1,0:T(8,128)(2,1)S(1)} %get-tuple-element.35), channel_id=1, source_target_pairs={{0,12},{1,13},{2,14},{3,15},{4,8},{5,9},{6,10},{7,11},{8,4},{9,5},... | collective-permute-start | bytes 393224 | tf_op jit(solution)/shard_map/ppermute | solution.py:450
  51.9 22.4 %collective-permute-start.10 = (bf16[32,2048]{1,0:T(8,128)(2,1)S(1)}, bf16[32,2048]{1,0:T(8,128)(2,1)S(1)}, u32[]{:S(2)}, u32[]{:S(2)}) collective-permute-start(bf16[32,2048]{1,0:T(8,128)(2,1)S(1)} %get-tuple-element.36), channel_id=1, source_target_pairs={{0,14},{1,15},{2,12},{3,13},{4,10},{5,11},{6,8},{7,9},{8,6},{9,7},... | collective-permute-start | bytes 393224 | tf_op jit(solution)/shard_map/ppermute | solution.py:450

commit v4 on v3

--- a/solution.py
+++ b/solution.py
@@ -73,7 +73,7 @@
     )(u, k, r)
 
 
-def sections(shape, fill, live, done, u0, u1, u2, xp, xm, yp, ym, zp, lin, quad):
+def sections(steps, shape, fill, live, done, u0, u1, u2, xp, xm, yp, ym, zp, lin, quad):
     levels, ext, cells = shape
     chunks = cells // LANES
     lane = lax.broadcasted_iota(jnp.int32, (ext, LANES), 1)
@@ -154,25 +154,28 @@
         if at < ext:
             dst[l, at:, c] = v[at:]
 
-    ats = [left_right(u0, l) for l in range(levels)]
-    for j in range(chunks):
-        for l in range(levels):
-            masked(u1, l, cols(j), euler(u0, ats, l, j))
-    ats = [left_right(u1, l) for l in range(levels)]
-    for j in range(chunks):
-        for l in range(levels):
+    for step in range(steps):
+        ats = [left_right(u0, l) for l in range(levels)]
+        for j in range(chunks):
+            for l in range(levels):
+                masked(u1, l, cols(j), euler(u0, ats, l, j))
+        ats = [left_right(u1, l) for l in range(levels)]
+        for j in range(chunks):
+            for l in range(levels):
+                c = cols(j)
+                masked(u2, l, c, 0.75 * u0[l, :, c] + 0.25 * euler(u1, ats, l, j))
+        ats = [left_right(u2, l) for l in range(levels)]
+        for j in range(chunks):
             c = cols(j)
-            masked(u2, l, c, 0.75 * u0[l, :, c] + 0.25 * euler(u1, ats, l, j))
-    ats = [left_right(u2, l) for l in range(levels)]
-    for j in range(chunks):
-        c = cols(j)
-        done(
-            c,
-            [
+            values = [
                 (1.0 / 3.0) * u0[l, :, c] + (2.0 / 3.0) * euler(u2, ats, l, j)
                 for l in range(levels)
-            ],
-        )
+            ]
+            if step == steps - 1:
+                done(c, values)
+            else:
+                for l in range(levels):
+                    masked(u0, l, c, values[l])
 
 
 def grid_ends():
@@ -185,170 +188,106 @@
     return jnp.where(even, core, chip), jnp.where(even, chip, core)
 
 
-def step_kernel(first, u_ref, k_ref, r_ref, core_ref, chip_ref, *refs):
-    face_ref = None if first else refs[0]
-    place_ref, state_out, *outs = refs[0 if first else 1 : -14]
-    scratch, (new, packed, got, sems) = refs[-14:-4], refs[-4:]
+def steps_kernel(steps, u_ref, k_ref, r_ref, core_ref, chip_ref, *refs):
+    scratch, refs = refs[-10:], refs[:-10]
+    if steps == 1:
+        place_ref, *outs, new = refs
+    else:
+        deep_ref, place_ref, new, *outs = refs
     levels, rows, cells = u_ref.shape
+    near = levels * TILE
     after, before, even = grid_ends()
     row = lax.broadcasted_iota(jnp.int32, (TILE, LANES), 0)
     side = row < TILE // 2
-    per = WIDE // LANES
-    groups = cells // WIDE
-    u0, kk, quad = scratch[0], scratch[2], scratch[9]
-    loads = {}
-    for g in (groups - 1, *range(groups - 1)):
-        c = slice(g * WIDE, (g + 1) * WIDE)
-        loads[g] = [
-            pltpu.make_async_copy(ref.at[:, :, c], to.at[:, :rows, c], got.at[i, g])
-            for i, (ref, to) in enumerate(((k_ref, kk), (u_ref, u0), (r_ref, quad)))
-        ]
-        for load in loads[g]:
-            load.start()
+
+    def faces(c):
+        below, above = sides(core_ref[:near, c], chip_ref[:, c], even)
+        tiles = [slice(l * TILE, (l + 1) * TILE) for l in range(levels)]
+        if steps == 1:
+            for t in tiles:
+                b, a = below[t], above[t]
+                yield [
+                    (
+                        jnp.where(side, b, a),
+                        jnp.where(side, roll_rows(b, 3), roll_rows(a, 5)),
+                        jnp.where(side, roll_rows(b, 5), roll_rows(a, 3)),
+                    )
+                ]
+            return
+        below2, above2 = sides(core_ref[near:, c], deep_ref[:, c], even)
+        r_below, r_above = below2[near : near + TILE], above2[near : near + TILE]
+        for l, t in enumerate(tiles):
+            b, a, b2, a2 = below[t], above[t], below2[t], above2[t]
+            rb = jnp.where(row < 4, roll_rows(b2, 4), roll_rows(r_below, 4 - l))
+            ra = jnp.where(row >= 4, roll_rows(a2, 4), roll_rows(r_above, 3 - l))
+            b_tiles = (
+                jnp.where(row < 3, b, b2),
+                roll_rows(jnp.where(row >= 5, b, b2), 3),
+                jnp.where(row < 2, roll_rows(b, 5), rb),
+            )
+            a_tiles = (
+                jnp.where(row >= 5, a, a2),
+                roll_rows(jnp.where(row < 3, a, a2), 5),
+                jnp.where(row >= 6, roll_rows(a, 3), ra),
+            )
+            yield [
+                [jnp.where(row < 6, v, 0.0) for v in b_tiles],
+                [jnp.where(row >= 2, v, 0.0) for v in a_tiles],
+            ]
 
     def fill(j, u0, kk, quad):
-        for load in loads.pop(j // per, ()):
-            load.wait()
         c = slice(j * LANES, (j + 1) * LANES)
-        near = levels * TILE
-        below, above = sides(core_ref[:near, c], chip_ref[:, c], even)
-        for l in range(levels):
-            b, a = below[l * TILE : (l + 1) * TILE], above[l * TILE : (l + 1) * TILE]
-            u0[l, rows:, c] = jnp.where(side, b, a) if first else face_ref[l, :, c]
-            kk[l, rows:, c] = jnp.where(side, roll_rows(b, 3), roll_rows(a, 5))
-            quad[l, rows:, c] = jnp.where(side, roll_rows(b, 5), roll_rows(a, 3))
+        for l, tiles in enumerate(faces(c)):
+            u0[l, :rows, c] = u_ref[l, :, c]
+            kk[l, :rows, c] = k_ref[l, :, c]
+            quad[l, :rows, c] = r_ref[l, :, c]
+            for i, (u, k, r) in enumerate(tiles):
+                at = slice(rows + i * TILE, rows + (i + 1) * TILE)
+                u0[l, at, c] = u
+                kk[l, at, c] = k
+                quad[l, at, c] = r
 
     place = place_ref[...]
-    copies = []
-
-    def send(src, dst):
-        copy = pltpu.make_async_copy(src, dst, sems.at[len(copies)])
-        copy.start()
-        copies.append(copy)
 
     def done(c, values):
         for l, v in enumerate(values):
             new[l, :, c] = v[:rows]
         if c.stop % WIDE == 0:
             c = slice(c.stop - WIDE, c.stop)
-            send(new.at[:, :, c], state_out.at[:, :, c])
             v = new[:, :, c].astype(jnp.bfloat16).reshape(levels * rows, WIDE)
             v = jnp.dot(place, v, preferred_element_type=jnp.float32).astype(jnp.bfloat16)
-            if first:
-                packed[:, c] = v
-                send(packed.at[:, c], outs[0].at[:, c])
-            else:
-                at = 0
-                for out in outs:
-                    out[:, c] = v[at : at + out.shape[0]]
-                    at += out.shape[0]
-
-    live = [(rows, rows + TILE, jnp.where(side, after, before) > 0)]
-    sections((levels, rows + TILE, cells), fill, live, done, *scratch)
-    for copy in copies:
-        copy.wait()
-
-
-def strip_kernel(u_ref, k_ref, r_ref, core_ref, chip_ref, deep_ref, face_ref, *refs):
-    scratch, top, bot, sems = refs[:10], refs[10], refs[11], refs[12]
-    levels, rows, cells = u_ref.shape
-    copies = []
-    for i, ref in enumerate((u_ref, k_ref, r_ref)):
-        copies.append(pltpu.make_async_copy(ref.at[:, :TILE], top.at[i], sems.at[0, i]))
-        copies.append(pltpu.make_async_copy(ref.at[:, rows - TILE :], bot.at[i], sems.at[1, i]))
-    for copy in copies:
-        copy.start()
-    for copy in copies:
-        copy.wait()
-    after, before, even = grid_ends()
-    row = lax.broadcasted_iota(jnp.int32, (TILE, LANES), 0)
-
-    def fill(j, u0, kk, quad):
-        c = slice(j * LANES, (j + 1) * LANES)
-        near = levels * TILE
-        below, above = sides(core_ref[:near, c], chip_ref[:, c], even)
-        below2, above2 = sides(core_ref[near:, c], deep_ref[:, c], even)
-        r_below, r_above = below2[near : near + TILE], above2[near : near + TILE]
-        for l in range(levels):
-            t = slice(l * TILE, (l + 1) * TILE)
-            b, a, b2, a2 = below[t], above[t], below2[t], above2[t]
-            rb = jnp.where(row < 4, roll_rows(b2, 4), roll_rows(r_below, 4 - l))
-            ra = jnp.where(row >= 4, roll_rows(a2, 4), roll_rows(r_above, 3 - l))
-            for at, u, k, r in (
-                (0, bot[0, l, :, c], bot[1, l, :, c], bot[2, l, :, c]),
-                (
-                    TILE,
-                    jnp.where(row < 3, b, b2),
-                    roll_rows(jnp.where(row >= 5, b, b2), 3),
-                    jnp.where(row < 2, roll_rows(b, 5), rb),
-                ),
-                (
-                    2 * TILE,
-                    jnp.where(row >= 5, a, a2),
-                    roll_rows(jnp.where(row < 3, a, a2), 5),
-                    jnp.where(row >= 6, roll_rows(a, 3), ra),
-                ),
-                (3 * TILE, top[0, l, :, c], top[1, l, :, c], top[2, l, :, c]),
-            ):
-                u0[l, at : at + TILE, c] = u
-                kk[l, at : at + TILE, c] = k
-                quad[l, at : at + TILE, c] = r
-
-    keep_after = jnp.where(row < TILE, after, 0) > 0
-    keep_before = jnp.where(row < TILE, before, 0) > 0
-
-    def done(c, values):
-        for l, v in enumerate(values):
-            b = jnp.where(keep_after, v[TILE : 2 * TILE], 0.0)
-            a = jnp.where(keep_before, v[2 * TILE : 3 * TILE], 0.0)
-            face_ref[l, :, c] = jnp.where(row < 3, b, jnp.where(row < 5, 0.0, a))
-
-    live = [(TILE, 2 * TILE, keep_after), (2 * TILE, 3 * TILE, keep_before)]
-    sections((levels, 4 * TILE, cells), fill, live, done, *scratch)
-
-
-def strip(u, k, r, packets):
-    levels, _, cells = u.shape
-    hbm, vmem = pl.BlockSpec(memory_space=pltpu.HBM), pl.BlockSpec(memory_space=pltpu.VMEM)
+            at = 0
+            for out in outs:
+                out[:, c] = v[at : at + out.shape[0]]
+                at += out.shape[0]
+
+    if steps == 1:
+        live = [(rows, rows + TILE, jnp.where(side, after, before) > 0)]
+    else:
+        live = [
+            (rows, rows + TILE, jnp.where(row < TILE, after, 0) > 0),
+            (rows + TILE, rows + 2 * TILE, jnp.where(row < TILE, before, 0) > 0),
+        ]
+    sections(steps, (levels, rows + steps * TILE, cells), fill, live, done, *scratch)
+
+
+def advance(steps, state, kappa, rate, faces, place, parts):
+    levels, rows, cells = state.shape
+    slots = place.shape[0]
+    out = [jax.ShapeDtypeStruct(state.shape, jnp.float32)] if steps > 1 else []
+    out += [jax.ShapeDtypeStruct((slots // parts, cells), jnp.bfloat16)] * parts
+    scratch = [] if steps > 1 else [pltpu.VMEM(state.shape, jnp.float32)]
+    vmem = pl.BlockSpec(memory_space=pltpu.VMEM)
     return pl.pallas_call(
-        strip_kernel,
-        out_shape=jax.ShapeDtypeStruct((levels, TILE, cells), jnp.float32),
-        in_specs=[hbm] * 3 + [vmem] * 3,
-        out_specs=vmem,
-        scratch_shapes=[pltpu.VMEM((levels, 4 * TILE, cells), jnp.float32)] * 10
-        + [pltpu.VMEM((3, levels, TILE, cells), jnp.float32)] * 2
-        + [pltpu.SemaphoreType.DMA((2, 3))],
+        functools.partial(steps_kernel, steps),
+        out_shape=out,
+        in_specs=[vmem] * (4 + len(faces)),
+        out_specs=[vmem] * len(out),
+        scratch_shapes=scratch
+        + [pltpu.VMEM((levels, rows + steps * TILE, cells), jnp.float32)] * 10,
         compiler_params=pltpu.CompilerParams(vmem_limit_bytes=VMEM),
         cost_estimate=pl.CostEstimate(
-            flops=100 * levels * 4 * TILE * cells,
-            bytes_accessed=22 * levels * 4 * TILE * cells,
-            transcendentals=0,
-        ),
-    )(u, k, r, *packets)
-
-
-def step(first, state, kappa, rate, faces, place, parts, limit):
-    levels, rows, cells = state.shape
-    slots = place.shape[0]
-    out = [jax.ShapeDtypeStruct(state.shape, jnp.float32)]
-    out += [jax.ShapeDtypeStruct((slots // parts, cells), jnp.bfloat16)] * parts
-    vmem, hbm = pl.BlockSpec(memory_space=pltpu.VMEM), pl.BlockSpec(memory_space=pltpu.HBM)
-    groups = cells // WIDE
-    return pl.pallas_call(
-        functools.partial(step_kernel, first),
-        out_shape=out,
-        in_specs=[hbm] * 3 + [vmem] * (1 + len(faces)),
-        out_specs=[hbm] + [hbm if first else vmem] * parts,
-        scratch_shapes=[pltpu.VMEM((levels, rows + TILE, cells), jnp.float32)] * 10
-        + [
-            pltpu.VMEM(state.shape, jnp.float32),
-            pltpu.VMEM((slots, cells) if first else (16, LANES), jnp.bfloat16),
-            pltpu.SemaphoreType.DMA((3, groups)),
-            pltpu.SemaphoreType.DMA((2 * groups,)),
-        ],
-        compiler_params=pltpu.CompilerParams(vmem_limit_bytes=limit * 1024 * 1024),
-        cost_estimate=pl.CostEstimate(
-            flops=120 * levels * rows * cells,
+            flops=120 * steps * levels * rows * cells,
             bytes_accessed=22 * levels * rows * cells,
             transcendentals=0,
         ),
@@ -426,19 +365,19 @@
     faces = [lax.ppermute(to_core, "gx", by_core), lax.ppermute(to_chip, "gx", by_chip)]
     deep = lax.ppermute(deep, "gx", by_chip)
     place = placing(writer[0], lambda d: d, n, per_dev)
-    state, packed = step(True, initial, kappa, rate, faces, place, 1, 53)
+    (packed,) = advance(1, initial, kappa, rate, faces, place, 1)
     packed, deep = lax.optimization_barrier((packed, deep))
     first = route(packed)
-    faces = faces + [strip(initial, kappa, rate, faces + [deep])]
+    faces = faces + [deep]
     if capacity % 16 or n & (n - 1):
         place = placing(writer[1], lambda d: d, n, per_dev)
-        state, packed = step(False, state, kappa, rate, faces, place, 1, 30)
+        state, packed = advance(2, initial, kappa, rate, faces, place, 1)
         return state, jnp.stack([first, route(packed)])
 
     chips = n // 2
     me = lax.axis_index("gx")
     place = placing(writer[1], lambda d: ((d ^ me) & 1) * chips + ((d ^ me) >> 1), n, per_dev)
-    state, mine, theirs = step(False, state, kappa, rate, faces, place, 2, 30)
+    state, mine, theirs = advance(2, initial, kappa, rate, faces, place, 2)
     theirs = lax.ppermute(theirs, "gx", by_core)
     block = jax.ShapeDtypeStruct((2 * capacity, cells), jnp.bfloat16)
     frames = jax.ShapeDtypeStruct((STEPS, slots, cells), jnp.bfloat16)

time: 75.8 us -> 74.2 us (0.979)
  local copies, waits for them, and re-layouts: 2.48 us -> 0.98 us
  waiting for transfers between devices: 23 us -> 24 us
  Pallas kernels: 25.1 us -> 24.3 us
    unnamed x16 -> x10, local copies, waits for them, and re-layouts: 2.47 us -> 0.98 us
    pallas_call x3 -> x2, Pallas kernels: 19.4 us -> 18.4 us  [advance(): pl.pallas_call(functools.partial(steps_kernel, steps), out_shape=out, in_...]
  transfers between devices with their start and end apart: 12 -> 12, of which waited for: 9 -> 9; matrix products, arithmetic and copies ran while one was open for 1% -> 1% of each run, Pallas kernels for 29% -> 28%
where the time goes in v4:
time: 74.2 us; the launch traced here: 73.9 us
  Pallas kernels  24.3 us (33%)
  waiting for transfers between devices  24 us (32%)
  starting transfers between devices  23.4 us (32%)
  local copies, waits for them, and re-layouts  0.98 us (1%)
  between operations  0.95 us (1%)
    pallas_call x2, Pallas kernels, advance(): pl.pallas_call(functools.partial(steps_kernel, steps), out_shape=out, in_...  18.4 us
    ppermute x7, waiting for transfers between devices, shards(): lax.ppermute(blocks[p], 'gx', [(i, i ^ 2 * p) for i in range(n)])  14.9 us
    ppermute x7, starting transfers between devices, shards(): lax.ppermute(blocks[p], 'gx', [(i, i ^ 2 * p) for i in range(n)])  11.3 us
    all_to_all x1, waiting for transfers between devices, route(): return lax.all_to_all(packed, 'gx', split_axis=0, concat_axis=0, tiled=True)  5.87 us
    all_to_all x1, starting transfers between devices, route(): return lax.all_to_all(packed, 'gx', split_axis=0, concat_axis=0, tiled=True)  5.4 us
    ppermute x1, starting transfers between devices, shards(): deep = lax.ppermute(deep, 'gx', by_chip)  3.71 us
    pallas_call x3, Pallas kernels, vmem_call(): pl.pallas_call(kernel, out_shape=out, in_specs=kw.pop('in_specs', [vmem]...  3.3 us
    ppermute x1, starting transfers between devices, shards(): lax.ppermute(to_chip, 'gx', by_chip)  2.75 us
  transfers between devices with their start and end apart: 12, of which 9 were waited for; matrix products, arithmetic and copies ran while one was open for 1% of the time, Pallas kernels for 28%

profile of v4, /device:TPU:10, one launch (start us, length us, event | category | flops | bytes accessed | tf_op | source)
XLA Modules:
  0.0 73.9 jit_solution(365017522501129188)
XLA Ops:
  0.6 0.0 copy-start.2
  0.6 0.0 copy-start.1
  0.7 0.0 copy-start
  0.7 0.0 copy-start.4
  0.7 2.6 %shard_map.59 = (bf16[80,2048]{1,0:T(8,128)(2,1)}, bf16[32,2048]{1,0:T(8,128)(2,1)}, bf16[48,2048]{1,0:T(8,128)(2,1)}) custom-call(f32[4,32,2048]{2,1,0:T(8,128)} %u_ref.5, f32[4,32,2048]{2,1,0:T(8,128)} %k_ref.5, f32[4,32,2048]{2,1,0:T(8,128)} %r_ref.5), custom_call_target="tpu_custom_call" | custom-call | tf_op jit(solution)/shard_map/pallas_call | solution.py:65
  3.3 2.8 %collective-permute-start.1 = (bf16[32,2048]{1,0:T(8,128)(2,1)}, bf16[32,2048]{1,0:T(8,128)(2,1)}, u32[]{:S(2)}, u32[]{:S(2)}) collective-permute-start(bf16[32,2048]{1,0:T(8,128)(2,1)} %get-tuple-element.19), channel_id=1, source_target_pairs={{1,2},{3,4},{5,6},{7,8},{9,10},{11,12},{13,14},{2,1},{4,3},{6,5},{... | collective-permute-start | bytes 393224 | tf_op jit(solution)/shard_map/ppermute | solution.py:365
  6.0 3.7 %collective-permute-start.2 = (bf16[48,2048]{1,0:T(8,128)(2,1)}, bf16[48,2048]{1,0:T(8,128)(2,1)}, u32[]{:S(2)}, u32[]{:S(2)}) collective-permute-start(bf16[48,2048]{1,0:T(8,128)(2,1)} %get-tuple-element.20), channel_id=1, source_target_pairs={{1,2},{3,4},{5,6},{7,8},{9,10},{11,12},{13,14},{2,1},{4,3},{6,5},{... | collective-permute-start | bytes 589832 | tf_op jit(solution)/shard_map/ppermute | solution.py:366
  9.8 0.1 collective-permute-start
  9.8 0.0 copy-done.4
  9.9 0.2 fusion.1
  10.0 0.2 fusion
  10.2 0.6 collective-permute-done.1.chip_ref
  10.9 0.8 %collective-permute-done.core_ref = bf16[80,2048]{1,0:T(8,128)(2,1)S(1)} collective-permute-done((bf16[80,2048]{1,0:T(8,128)(2,1)}, bf16[80,2048]{1,0:T(8,128)(2,1)S(1)}, u32[]{:S(2)}, u32[]{:S(2)}) %collective-permute-start) | collective-permute-done | bytes 327712 | tf_op jit(solution)/shard_map/ppermute | solution.py:365
  11.7 0.0 copy-done.2
  11.7 0.0 copy-done.1
  11.7 0.0 copy-done
  11.7 6.1 %shard_map.60 = bf16[256,2048]{1,0:T(8,128)(2,1)S(1)} custom-call(f32[4,32,2048]{2,1,0:T(8,128)S(1)} %copy-done, f32[4,32,2048]{2,1,0:T(8,128)S(1)} %copy-done.1, f32[4,32,2048]{2,1,0:T(8,128)S(1)} %copy-done.2, bf16[80,2048]{1,0:T(8,128)(2,1)S(1)} %collective-permute-done.core_ref, bf16[32,2048]{1,0:T(8,128)(2,1)} %collective-permute-done.1.chip_ref, ...), custom_call_target="tpu_custom_call" | custom-call | flops 31457280 | bytes 5767168 | tf_op jit(solution)/shard_map/pallas_call | solution.py:281
  17.7 0.0 copy-start.3
  17.8 1.0 %copy-done.3 = bf16[256,2048]{1,0:T(8,128)(2,1)} copy-done((bf16[256,2048]{1,0:T(8,128)(2,1)}, bf16[256,2048]{1,0:T(8,128)(2,1)S(1)}, u32[]{:S(2)}) %copy-start.3) | copy-done | bytes 1048600
  18.7 0.0 collective-permute-done.2.refs_0_
  18.7 5.4 %all-to-all-start = ((bf16[16,16,2048]{2,1,0:T(8,128)(2,1)}), bf16[16,16,2048]{2,1,0:T(8,128)(2,1)}, u32[]{:S(2)}, u32[]{:S(2)}) async-start(bf16[16,16,2048]{2,1,0:T(8,128)(2,1)} %bitcast.10), calls=%async_computation | async-start | bytes 2097152 | tf_op jit(solution)/shard_map/all_to_all | solution.py:362
  24.1 12.3 %shard_map.61 = (f32[4,32,2048]{2,1,0:T(8,128)}, bf16[128,2048]{1,0:T(8,128)(2,1)S(1)}, bf16[128,2048]{1,0:T(8,128)(2,1)S(1)}) custom-call(f32[4,32,2048]{2,1,0:T(8,128)S(1)} %copy-done, f32[4,32,2048]{2,1,0:T(8,128)S(1)} %copy-done.1, f32[4,32,2048]{2,1,0:T(8,128)S(1)} %copy-done.2, bf16[80,2048]{1,0:T(8,128)(2,1)S(1)} %collective-permute-done.core_ref, ...), custom_call_target="tpu_custom_call" | custom-call | flops 62914560 | bytes 5767168 | tf_op jit(solution)/shard_map/pallas_call | solution.py:281
  36.4 0.1 collective-permute-start.3
  36.6 1.8 %collective-permute-done.3.theirs_ref = bf16[128,2048]{1,0:T(8,128)(2,1)S(1)} collective-permute-done((bf16[128,2048]{1,0:T(8,128)(2,1)S(1)}, bf16[128,2048]{1,0:T(8,128)(2,1)S(1)}, u32[]{:S(2)}, u32[]{:S(2)}) %collective-permute-start.3) | collective-permute-done | bytes 524320 | tf_op jit(solution)/shard_map/ppermute | solution.py:381
  38.3 0.1 shard_map.62
  38.4 1.5 %collective-permute-start.4 = (bf16[32,2048]{1,0:T(8,128)(2,1)S(1)}, bf16[32,2048]{1,0:T(8,128)(2,1)S(1)}, u32[]{:S(2)}, u32[]{:S(2)}) collective-permute-start(bf16[32,2048]{1,0:T(8,128)(2,1)S(1)} %get-tuple-element.26), channel_id=1, source_target_pairs={{0,2},{1,3},{2,0},{3,1},{4,6},{5,7},{6,4},{7,5},{8,10},{9,11},{10,... | collective-permute-start | bytes 393224 | tf_op jit(solution)/shard_map/ppermute | solution.py:389
  40.0 0.6 collective-permute-start.5
  40.5 1.5 %collective-permute-start.6 = (bf16[32,2048]{1,0:T(8,128)(2,1)S(1)}, bf16[32,2048]{1,0:T(8,128)(2,1)S(1)}, u32[]{:S(2)}, u32[]{:S(2)}) collective-permute-start(bf16[32,2048]{1,0:T(8,128)(2,1)S(1)} %get-tuple-element.28), channel_id=1, source_target_pairs={{0,6},{1,7},{2,4},{3,5},{4,2},{5,3},{6,0},{7,1},{8,14},{9,15},{10,... | collective-permute-start | bytes 393224 | tf_op jit(solution)/shard_map/ppermute | solution.py:389
  42.0 2.4 %collective-permute-start.7 = (bf16[32,2048]{1,0:T(8,128)(2,1)S(1)}, bf16[32,2048]{1,0:T(8,128)(2,1)S(1)}, u32[]{:S(2)}, u32[]{:S(2)}) collective-permute-start(bf16[32,2048]{1,0:T(8,128)(2,1)S(1)} %get-tuple-element.29), channel_id=1, source_target_pairs={{0,8},{1,9},{2,10},{3,11},{4,12},{5,13},{6,14},{7,15},{8,0},{9,1},... | collective-permute-start | bytes 393224 | tf_op jit(solution)/shard_map/ppermute | solution.py:389
  44.4 1.5 %collective-permute-start.8 = (bf16[32,2048]{1,0:T(8,128)(2,1)S(1)}, bf16[32,2048]{1,0:T(8,128)(2,1)S(1)}, u32[]{:S(2)}, u32[]{:S(2)}) collective-permute-start(bf16[32,2048]{1,0:T(8,128)(2,1)S(1)} %get-tuple-element.30), channel_id=1, source_target_pairs={{0,10},{1,11},{2,8},{3,9},{4,14},{5,15},{6,12},{7,13},{8,2},{9,3},... | collective-permute-start | bytes 393224 | tf_op jit(solution)/shard_map/ppermute | solution.py:389
  45.8 3.5 %collective-permute-done.4.refs_1_ = bf16[32,2048]{1,0:T(8,128)(2,1)S(1)} collective-permute-done((bf16[32,2048]{1,0:T(8,128)(2,1)S(1)}, bf16[32,2048]{1,0:T(8,128)(2,1)S(1)}, u32[]{:S(2)}, u32[]{:S(2)}) %collective-permute-start.4) | collective-permute-done | bytes 131104 | tf_op jit(solution)/shard_map/ppermute | solution.py:389
  49.3 0.5 collective-permute-start.9
  49.8 0.0 collective-permute-done.5.refs_2_
  49.8 3.5 %collective-permute-start.10 = (bf16[32,2048]{1,0:T(8,128)(2,1)S(1)}, bf16[32,2048]{1,0:T(8,128)(2,1)S(1)}, u32[]{:S(2)}, u32[]{:S(2)}) collective-permute-start(bf16[32,2048]{1,0:T(8,128)(2,1)S(1)} %get-tuple-element.32), channel_id=1, source_target_pairs={{0,14},{1,15},{2,12},{3,13},{4,10},{5,11},{6,8},{7,9},{8,6},{9,7},... | collective-permute-start | bytes 393224 | tf_op jit(solution)/shard_map/ppermute | solution.py:389
  53.2 5.9 %all-to-all-done = bf16[16,16,2048]{2,1,0:T(8,128)(2,1)} async-done(((bf16[16,16,2048]{2,1,0:T(8,128)(2,1)}), bf16[16,16,2048]{2,1,0:T(8,128)(2,1)}, u32[]{:S(2)}, u32[]{:S(2)}) %all-to-all-start) | async-done | bytes 1048608 | tf_op jit(solution)/shard_map/all_to_all | solution.py:362
  59.1 2.2 %shard_map.63.refs_8_ = bf16[2,256,2048]{2,1,0:T(8,128)(2,1)} custom-call(bf16[256,2048]{1,0:T(8,128)(2,1)} %bitcast.3.part_ref), custom_call_target="tpu_custom_call" | custom-call | tf_op jit(solution)/shard_map/pallas_call | solution.py:299
  61.3 0.0 collective-permute-done.6.refs_3_
  61.3 0.6 collective-permute-done.7.refs_4_
  61.9 2.8 %collective-permute-done.8.refs_5_ = bf16[32,2048]{1,0:T(8,128)(2,1)S(1)} collective-permute-done((bf16[32,2048]{1,0:T(8,128)(2,1)S(1)}, bf16[32,2048]{1,0:T(8,128)(2,1)S(1)}, u32[]{:S(2)}, u32[]{:S(2)}) %collective-permute-start.8) | collective-permute-done | bytes 131104 | tf_op jit(solution)/shard_map/ppermute | solution.py:389
  64.7 4.7 %collective-permute-done.9.refs_6_ = bf16[32,2048]{1,0:T(8,128)(2,1)S(1)} collective-permute-done((bf16[32,2048]{1,0:T(8,128)(2,1)S(1)}, bf16[32,2048]{1,0:T(8,128)(2,1)S(1)}, u32[]{:S(2)}, u32[]{:S(2)}) %collective-permute-start.9) | collective-permute-done | bytes 131104 | tf_op jit(solution)/shard_map/ppermute | solution.py:389
  69.5 3.3 %collective-permute-done.10.refs_7_ = bf16[32,2048]{1,0:T(8,128)(2,1)S(1)} collective-permute-done((bf16[32,2048]{1,0:T(8,128)(2,1)S(1)}, bf16[32,2048]{1,0:T(8,128)(2,1)S(1)}, u32[]{:S(2)}, u32[]{:S(2)}) %collective-permute-start.10) | collective-permute-done | bytes 131104 | tf_op jit(solution)/shard_map/ppermute | solution.py:389
  72.7 1.0 %shard_map.64 = bf16[2,256,2048]{2,1,0:T(8,128)(2,1)} custom-call(bf16[32,2048]{1,0:T(8,128)(2,1)S(1)} %get-tuple-element.25.refs_0_, bf16[32,2048]{1,0:T(8,128)(2,1)S(1)} %collective-permute-done.4.refs_1_, bf16[32,2048]{1,0:T(8,128)(2,1)S(1)} %collective-permute-done.5.refs_2_, ...), custom_call_target="tpu_custom_call", output_to_operand_aliasing={{}: (8, {})} | custom-call | tf_op jit(solution)/shard_map/pallas_call | solution.py:299
  (4 shorter events, 0.1 us)
Async XLA Ops:
  0.6 11.0 %copy-start.2 = (f32[4,32,2048]{2,1,0:T(8,128)S(1)}, f32[4,32,2048]{2,1,0:T(8,128)}, u32[]{:S(2)}) copy-start(f32[4,32,2048]{2,1,0:T(8,128)} %r_ref.5) | copy-start | bytes 3145732
  0.6 11.0 %copy-start.1 = (f32[4,32,2048]{2,1,0:T(8,128)S(1)}, f32[4,32,2048]{2,1,0:T(8,128)}, u32[]{:S(2)}) copy-start(f32[4,32,2048]{2,1,0:T(8,128)} %k_ref.5) | copy-start | bytes 3145732
  0.7 11.0 %copy-start = (f32[4,32,2048]{2,1,0:T(8,128)S(1)}, f32[4,32,2048]{2,1,0:T(8,128)}, u32[]{:S(2)}) copy-start(f32[4,32,2048]{2,1,0:T(8,128)} %u_ref.5) | copy-start | bytes 3145732
  0.7 9.2 %copy-start.4 = (s32[2,128,1]{1,2,0:T(1,128)S(1)}, s32[2,128,1]{1,2,0:T(1,128)}, u32[]{:S(2)}) copy-start(s32[2,128,1]{1,2,0:T(1,128)} %param.7) | copy-start | bytes 3076
  3.3 7.6 %collective-permute-start.1 = (bf16[32,2048]{1,0:T(8,128)(2,1)}, bf16[32,2048]{1,0:T(8,128)(2,1)}, u32[]{:S(2)}, u32[]{:S(2)}) collective-permute-start(bf16[32,2048]{1,0:T(8,128)(2,1)} %get-tuple-element.19), channel_id=1, source_target_pairs={{1,2},{3,4},{5,6},{7,8},{9,10},{11,12},{13,14},{2,1},{4,3},{6,5},{... | collective-permute-start | bytes 393224 | tf_op jit(solution)/shard_map/ppermute | solution.py:365
  6.0 12.7 %collective-permute-start.2 = (bf16[48,2048]{1,0:T(8,128)(2,1)}, bf16[48,2048]{1,0:T(8,128)(2,1)}, u32[]{:S(2)}, u32[]{:S(2)}) collective-permute-start(bf16[48,2048]{1,0:T(8,128)(2,1)} %get-tuple-element.20), channel_id=1, source_target_pairs={{1,2},{3,4},{5,6},{7,8},{9,10},{11,12},{13,14},{2,1},{4,3},{6,5},{... | collective-permute-start | bytes 589832 | tf_op jit(solution)/shard_map/ppermute | solution.py:366
  9.8 1.9 %collective-permute-start = (bf16[80,2048]{1,0:T(8,128)(2,1)}, bf16[80,2048]{1,0:T(8,128)(2,1)S(1)}, u32[]{:S(2)}, u32[]{:S(2)}) collective-permute-start(bf16[80,2048]{1,0:T(8,128)(2,1)} %get-tuple-element.18), channel_id=1, source_target_pairs={{0,1},{1,0},{2,3},{3,2},{4,5},{5,4},{6,7},{7,6},{8,9},{9,8},{10,11... | collective-permute-start | bytes 983048 | tf_op jit(solution)/shard_map/ppermute | solution.py:365
  17.7 1.0 %copy-start.3 = (bf16[256,2048]{1,0:T(8,128)(2,1)}, bf16[256,2048]{1,0:T(8,128)(2,1)S(1)}, u32[]{:S(2)}) copy-start(bf16[256,2048]{1,0:T(8,128)(2,1)S(1)} %shard_map.60) | copy-start | bytes 3145732
  18.7 40.4 %all-to-all-start = ((bf16[16,16,2048]{2,1,0:T(8,128)(2,1)}), bf16[16,16,2048]{2,1,0:T(8,128)(2,1)}, u32[]{:S(2)}, u32[]{:S(2)}) async-start(bf16[16,16,2048]{2,1,0:T(8,128)(2,1)} %bitcast.10), calls=%async_computation | async-start | bytes 2097152 | tf_op jit(solution)/shard_map/all_to_all | solution.py:362
  36.4 1.9 %collective-permute-start.3 = (bf16[128,2048]{1,0:T(8,128)(2,1)S(1)}, bf16[128,2048]{1,0:T(8,128)(2,1)S(1)}, u32[]{:S(2)}, u32[]{:S(2)}) collective-permute-start(bf16[128,2048]{1,0:T(8,128)(2,1)S(1)} %get-tuple-element.24), channel_id=1, source_target_pairs={{0,1},{1,0},{2,3},{3,2},{4,5},{5,4},{6,7},{7,6},{8,9},{9,8},{10,11... | collective-permute-start | bytes 1572872 | tf_op jit(solution)/shard_map/ppermute | solution.py:381
  38.4 10.9 %collective-permute-start.4 = (bf16[32,2048]{1,0:T(8,128)(2,1)S(1)}, bf16[32,2048]{1,0:T(8,128)(2,1)S(1)}, u32[]{:S(2)}, u32[]{:S(2)}) collective-permute-start(bf16[32,2048]{1,0:T(8,128)(2,1)S(1)} %get-tuple-element.26), channel_id=1, source_target_pairs={{0,2},{1,3},{2,0},{3,1},{4,6},{5,7},{6,4},{7,5},{8,10},{9,11},{10,... | collective-permute-start | bytes 393224 | tf_op jit(solution)/shard_map/ppermute | solution.py:389
  40.0 9.8 %collective-permute-start.5 = (bf16[32,2048]{1,0:T(8,128)(2,1)S(1)}, bf16[32,2048]{1,0:T(8,128)(2,1)S(1)}, u32[]{:S(2)}, u32[]{:S(2)}) collective-permute-start(bf16[32,2048]{1,0:T(8,128)(2,1)S(1)} %get-tuple-element.27), channel_id=1, source_target_pairs={{0,4},{1,5},{2,6},{3,7},{4,0},{5,1},{6,2},{7,3},{8,12},{9,13},{10,... | collective-permute-start | bytes 393224 | tf_op jit(solution)/shard_map/ppermute | solution.py:389
  40.5 20.8 %collective-permute-start.6 = (bf16[32,2048]{1,0:T(8,128)(2,1)S(1)}, bf16[32,2048]{1,0:T(8,128)(2,1)S(1)}, u32[]{:S(2)}, u32[]{:S(2)}) collective-permute-start(bf16[32,2048]{1,0:T(8,128)(2,1)S(1)} %get-tuple-element.28), channel_id=1, source_target_pairs={{0,6},{1,7},{2,4},{3,5},{4,2},{5,3},{6,0},{7,1},{8,14},{9,15},{10,... | collective-permute-start | bytes 393224 | tf_op jit(solution)/shard_map/ppermute | solution.py:389
  42.0 19.9 %collective-permute-start.7 = (bf16[32,2048]{1,0:T(8,128)(2,1)S(1)}, bf16[32,2048]{1,0:T(8,128)(2,1)S(1)}, u32[]{:S(2)}, u32[]{:S(2)}) collective-permute-start(bf16[32,2048]{1,0:T(8,128)(2,1)S(1)} %get-tuple-element.29), channel_id=1, source_target_pairs={{0,8},{1,9},{2,10},{3,11},{4,12},{5,13},{6,14},{7,15},{8,0},{9,1},... | collective-permute-start | bytes 393224 | tf_op jit(solution)/shard_map/ppermute | solution.py:389
  44.4 20.4 %collective-permute-start.8 = (bf16[32,2048]{1,0:T(8,128)(2,1)S(1)}, bf16[32,2048]{1,0:T(8,128)(2,1)S(1)}, u32[]{:S(2)}, u32[]{:S(2)}) collective-permute-start(bf16[32,2048]{1,0:T(8,128)(2,1)S(1)} %get-tuple-element.30), channel_id=1, source_target_pairs={{0,10},{1,11},{2,8},{3,9},{4,14},{5,15},{6,12},{7,13},{8,2},{9,3},... | collective-permute-start | bytes 393224 | tf_op jit(solution)/shard_map/ppermute | solution.py:389
  49.3 20.2 %collective-permute-start.9 = (bf16[32,2048]{1,0:T(8,128)(2,1)S(1)}, bf16[32,2048]{1,0:T(8,128)(2,1)S(1)}, u32[]{:S(2)}, u32[]{:S(2)}) collective-permute-start(bf16[32,2048]{1,0:T(8,128)(2,1)S(1)} %get-tuple-element.31), channel_id=1, source_target_pairs={{0,12},{1,13},{2,14},{3,15},{4,8},{5,9},{6,10},{7,11},{8,4},{9,5},... | collective-permute-start | bytes 393224 | tf_op jit(solution)/shard_map/ppermute | solution.py:389
  49.8 23.0 %collective-permute-start.10 = (bf16[32,2048]{1,0:T(8,128)(2,1)S(1)}, bf16[32,2048]{1,0:T(8,128)(2,1)S(1)}, u32[]{:S(2)}, u32[]{:S(2)}) collective-permute-start(bf16[32,2048]{1,0:T(8,128)(2,1)S(1)} %get-tuple-element.32), channel_id=1, source_target_pairs={{0,14},{1,15},{2,12},{3,13},{4,10},{5,11},{6,8},{7,9},{8,6},{9,7},... | collective-permute-start | bytes 393224 | tf_op jit(solution)/shard_map/ppermute | solution.py:389

commit v5 on v4

--- a/solution.py
+++ b/solution.py
@@ -108,12 +108,9 @@
 
     half = 0.5 * DT
     ats = [left_right(kk, l) for l in range(levels)]
-    filled = set()
     for j in range(chunks):
-        for i in (j - 1, j, j + 1):
-            if i % chunks not in filled:
-                filled.add(i % chunks)
-                fill(i % chunks, u0, kk, quad)
+        fill(j, u0, kk, quad)
+    for j in range(chunks):
         c = cols(j)
         for l in range(levels):
             k, k_right, k_left = ats[l](j)
@@ -128,9 +125,7 @@
                 total = total + f
             if l > 0:
                 total = total + zp[l - 1, :, c]
-            q = DT * quad[l, :, c]
-            quad[l, :, c] = q
-            lin[l, :, c] = 1.0 + q - total
+            lin[l, :, c] = 1.0 + quad[l, :, c] - total
 
     def euler(src, ats, l, j):
         c = cols(j)
@@ -240,12 +235,12 @@
         for l, tiles in enumerate(faces(c)):
             u0[l, :rows, c] = u_ref[l, :, c]
             kk[l, :rows, c] = k_ref[l, :, c]
-            quad[l, :rows, c] = r_ref[l, :, c]
+            quad[l, :rows, c] = DT * r_ref[l, :, c]
             for i, (u, k, r) in enumerate(tiles):
                 at = slice(rows + i * TILE, rows + (i + 1) * TILE)
                 u0[l, at, c] = u
                 kk[l, at, c] = k
-                quad[l, at, c] = r
+                quad[l, at, c] = DT * r
 
     place = place_ref[...]
 
@@ -394,15 +389,16 @@
         out_specs=[hbm],
         scratch_shapes=[pltpu.SemaphoreType.DMA],
     )
-    (out,) = vmem_call(
-        functools.partial(put_blocks_kernel, range(chips)),
-        (*got, out),
-        [frames],
-        in_specs=[vmem] * chips + [hbm],
-        out_specs=[hbm],
-        scratch_shapes=[pltpu.SemaphoreType.DMA((chips,))],
-        input_output_aliases={chips: 0},
-    )
+    for which in (range(chips - 2), range(chips - 2, chips)):
+        (out,) = vmem_call(
+            functools.partial(put_blocks_kernel, which),
+            (*[got[p] for p in which], out),
+            [frames],
+            in_specs=[vmem] * len(which) + [hbm],
+            out_specs=[hbm],
+            scratch_shapes=[pltpu.SemaphoreType.DMA((chips,))],
+            input_output_aliases={len(which): 0},
+        )
     return state, out
 
 

time: 74.2 us -> 74 us (level)
  waiting for transfers between devices: 24 us -> 23.1 us
    ppermute x7, waiting for transfers between devices: 14.9 us -> 14 us  [shards(): lax.ppermute(blocks[p], 'gx', [(i, i ^ 2 * p) for i in range(n)])]
    pallas_call x3 -> x4, Pallas kernels: 3.3 us -> 3.98 us  [vmem_call(): pl.pallas_call(kernel, out_shape=out, in_specs=kw.pop('in_specs', [vmem]...]
  transfers between devices with their start and end apart: 12 -> 12, of which waited for: 9 -> 9; matrix products, arithmetic and copies ran while one was open for 1% -> 1% of each run, Pallas kernels for 28% -> 29%
where the time goes in v5:
time: 74 us; the launch traced here: 73.7 us
  Pallas kernels  24.9 us (34%)
  starting transfers between devices  23.4 us (32%)
  waiting for transfers between devices  23.1 us (31%)
  local copies, waits for them, and re-layouts  0.98 us (1%)
  between operations  0.96 us (1%)
    pallas_call x2, Pallas kernels, advance(): pl.pallas_call(functools.partial(steps_kernel, steps), out_shape=out, in_...  18.3 us
    ppermute x7, waiting for transfers between devices, shards(): lax.ppermute(blocks[p], 'gx', [(i, i ^ 2 * p) for i in range(n)])  14 us
    ppermute x7, starting transfers between devices, shards(): lax.ppermute(blocks[p], 'gx', [(i, i ^ 2 * p) for i in range(n)])  11.3 us
    all_to_all x1, waiting for transfers between devices, route(): return lax.all_to_all(packed, 'gx', split_axis=0, concat_axis=0, tiled=True)  5.87 us
    all_to_all x1, starting transfers between devices, route(): return lax.all_to_all(packed, 'gx', split_axis=0, concat_axis=0, tiled=True)  5.4 us
    pallas_call x4, Pallas kernels, vmem_call(): pl.pallas_call(kernel, out_shape=out, in_specs=kw.pop('in_specs', [vmem]...  3.98 us
    ppermute x1, starting transfers between devices, shards(): deep = lax.ppermute(deep, 'gx', by_chip)  3.71 us
    ppermute x1, starting transfers between devices, shards(): lax.ppermute(to_chip, 'gx', by_chip)  2.75 us
  transfers between devices with their start and end apart: 12, of which 9 were waited for; matrix products, arithmetic and copies ran while one was open for 1% of the time, Pallas kernels for 29%

profile of v5, /device:TPU:10, one launch (start us, length us, event | category | flops | bytes accessed | tf_op | source)
XLA Modules:
  0.0 73.7 jit_solution(2629291105310902186)
XLA Ops:
  0.6 0.0 copy-start.2
  0.6 0.0 copy-start.1
  0.7 0.0 copy-start
  0.7 0.0 copy-start.4
  0.7 2.6 %shard_map.59 = (bf16[80,2048]{1,0:T(8,128)(2,1)}, bf16[32,2048]{1,0:T(8,128)(2,1)}, bf16[48,2048]{1,0:T(8,128)(2,1)}) custom-call(f32[4,32,2048]{2,1,0:T(8,128)} %u_ref.5, f32[4,32,2048]{2,1,0:T(8,128)} %k_ref.5, f32[4,32,2048]{2,1,0:T(8,128)} %r_ref.5), custom_call_target="tpu_custom_call" | custom-call | tf_op jit(solution)/shard_map/pallas_call | solution.py:65
  3.3 2.8 %collective-permute-start.1 = (bf16[32,2048]{1,0:T(8,128)(2,1)}, bf16[32,2048]{1,0:T(8,128)(2,1)}, u32[]{:S(2)}, u32[]{:S(2)}) collective-permute-start(bf16[32,2048]{1,0:T(8,128)(2,1)} %get-tuple-element.19), channel_id=1, source_target_pairs={{1,2},{3,4},{5,6},{7,8},{9,10},{11,12},{13,14},{2,1},{4,3},{6,5},{... | collective-permute-start | bytes 393224 | tf_op jit(solution)/shard_map/ppermute | solution.py:360
  6.0 3.7 %collective-permute-start.2 = (bf16[48,2048]{1,0:T(8,128)(2,1)}, bf16[48,2048]{1,0:T(8,128)(2,1)}, u32[]{:S(2)}, u32[]{:S(2)}) collective-permute-start(bf16[48,2048]{1,0:T(8,128)(2,1)} %get-tuple-element.20), channel_id=1, source_target_pairs={{1,2},{3,4},{5,6},{7,8},{9,10},{11,12},{13,14},{2,1},{4,3},{6,5},{... | collective-permute-start | bytes 589832 | tf_op jit(solution)/shard_map/ppermute | solution.py:361
  9.8 0.1 collective-permute-start
  9.8 0.0 copy-done.4
  9.9 0.2 fusion.1
  10.0 0.2 fusion
  10.2 0.6 collective-permute-done.1.chip_ref
  10.9 0.8 %collective-permute-done.core_ref = bf16[80,2048]{1,0:T(8,128)(2,1)S(1)} collective-permute-done((bf16[80,2048]{1,0:T(8,128)(2,1)}, bf16[80,2048]{1,0:T(8,128)(2,1)S(1)}, u32[]{:S(2)}, u32[]{:S(2)}) %collective-permute-start) | collective-permute-done | bytes 327712 | tf_op jit(solution)/shard_map/ppermute | solution.py:360
  11.7 0.0 copy-done.2
  11.7 0.0 copy-done.1
  11.7 0.0 copy-done
  11.7 6.1 %shard_map.60 = bf16[256,2048]{1,0:T(8,128)(2,1)S(1)} custom-call(f32[4,32,2048]{2,1,0:T(8,128)S(1)} %copy-done, f32[4,32,2048]{2,1,0:T(8,128)S(1)} %copy-done.1, f32[4,32,2048]{2,1,0:T(8,128)S(1)} %copy-done.2, bf16[80,2048]{1,0:T(8,128)(2,1)S(1)} %collective-permute-done.core_ref, bf16[32,2048]{1,0:T(8,128)(2,1)} %collective-permute-done.1.chip_ref, ...), custom_call_target="tpu_custom_call" | custom-call | flops 31457280 | bytes 5767168 | tf_op jit(solution)/shard_map/pallas_call | solution.py:276
  17.8 0.0 copy-start.3
  17.8 1.0 %copy-done.3 = bf16[256,2048]{1,0:T(8,128)(2,1)} copy-done((bf16[256,2048]{1,0:T(8,128)(2,1)}, bf16[256,2048]{1,0:T(8,128)(2,1)S(1)}, u32[]{:S(2)}) %copy-start.3) | copy-done | bytes 1048600
  18.7 0.0 collective-permute-done.2.refs_0_
  18.7 5.4 %all-to-all-start = ((bf16[16,16,2048]{2,1,0:T(8,128)(2,1)}), bf16[16,16,2048]{2,1,0:T(8,128)(2,1)}, u32[]{:S(2)}, u32[]{:S(2)}) async-start(bf16[16,16,2048]{2,1,0:T(8,128)(2,1)} %bitcast.10), calls=%async_computation | async-start | bytes 2097152 | tf_op jit(solution)/shard_map/all_to_all | solution.py:357
  24.2 12.3 %shard_map.61 = (f32[4,32,2048]{2,1,0:T(8,128)}, bf16[128,2048]{1,0:T(8,128)(2,1)S(1)}, bf16[128,2048]{1,0:T(8,128)(2,1)S(1)}) custom-call(f32[4,32,2048]{2,1,0:T(8,128)S(1)} %copy-done, f32[4,32,2048]{2,1,0:T(8,128)S(1)} %copy-done.1, f32[4,32,2048]{2,1,0:T(8,128)S(1)} %copy-done.2, bf16[80,2048]{1,0:T(8,128)(2,1)S(1)} %collective-permute-done.core_ref, ...), custom_call_target="tpu_custom_call" | custom-call | flops 62914560 | bytes 5767168 | tf_op jit(solution)/shard_map/pallas_call | solution.py:276
  36.4 0.1 collective-permute-start.3
  36.6 1.8 %collective-permute-done.3.theirs_ref = bf16[128,2048]{1,0:T(8,128)(2,1)S(1)} collective-permute-done((bf16[128,2048]{1,0:T(8,128)(2,1)S(1)}, bf16[128,2048]{1,0:T(8,128)(2,1)S(1)}, u32[]{:S(2)}, u32[]{:S(2)}) %collective-permute-start.3) | collective-permute-done | bytes 524320 | tf_op jit(solution)/shard_map/ppermute | solution.py:376
  38.3 0.1 shard_map.62
  38.4 1.5 %collective-permute-start.6 = (bf16[32,2048]{1,0:T(8,128)(2,1)S(1)}, bf16[32,2048]{1,0:T(8,128)(2,1)S(1)}, u32[]{:S(2)}, u32[]{:S(2)}) collective-permute-start(bf16[32,2048]{1,0:T(8,128)(2,1)S(1)} %get-tuple-element.28), channel_id=1, source_target_pairs={{0,2},{1,3},{2,0},{3,1},{4,6},{5,7},{6,4},{7,5},{8,10},{9,11},{10,... | collective-permute-start | bytes 393224 | tf_op jit(solution)/shard_map/ppermute | solution.py:384
  39.9 0.6 collective-permute-start.7
  40.5 1.5 %collective-permute-start.8 = (bf16[32,2048]{1,0:T(8,128)(2,1)S(1)}, bf16[32,2048]{1,0:T(8,128)(2,1)S(1)}, u32[]{:S(2)}, u32[]{:S(2)}) collective-permute-start(bf16[32,2048]{1,0:T(8,128)(2,1)S(1)} %get-tuple-element.30), channel_id=1, source_target_pairs={{0,6},{1,7},{2,4},{3,5},{4,2},{5,3},{6,0},{7,1},{8,14},{9,15},{10,... | collective-permute-start | bytes 393224 | tf_op jit(solution)/shard_map/ppermute | solution.py:384
  42.0 2.4 %collective-permute-start.9 = (bf16[32,2048]{1,0:T(8,128)(2,1)S(1)}, bf16[32,2048]{1,0:T(8,128)(2,1)S(1)}, u32[]{:S(2)}, u32[]{:S(2)}) collective-permute-start(bf16[32,2048]{1,0:T(8,128)(2,1)S(1)} %get-tuple-element.31), channel_id=1, source_target_pairs={{0,8},{1,9},{2,10},{3,11},{4,12},{5,13},{6,14},{7,15},{8,0},{9,1},... | collective-permute-start | bytes 393224 | tf_op jit(solution)/shard_map/ppermute | solution.py:384
  44.3 1.5 %collective-permute-start.10 = (bf16[32,2048]{1,0:T(8,128)(2,1)S(1)}, bf16[32,2048]{1,0:T(8,128)(2,1)S(1)}, u32[]{:S(2)}, u32[]{:S(2)}) collective-permute-start(bf16[32,2048]{1,0:T(8,128)(2,1)S(1)} %get-tuple-element.32), channel_id=1, source_target_pairs={{0,10},{1,11},{2,8},{3,9},{4,14},{5,15},{6,12},{7,13},{8,2},{9,3},... | collective-permute-start | bytes 393224 | tf_op jit(solution)/shard_map/ppermute | solution.py:384
  45.8 3.5 %collective-permute-done.6.refs_1_ = bf16[32,2048]{1,0:T(8,128)(2,1)S(1)} collective-permute-done((bf16[32,2048]{1,0:T(8,128)(2,1)S(1)}, bf16[32,2048]{1,0:T(8,128)(2,1)S(1)}, u32[]{:S(2)}, u32[]{:S(2)}) %collective-permute-start.6) | collective-permute-done | bytes 131104 | tf_op jit(solution)/shard_map/ppermute | solution.py:384
  49.3 0.4 collective-permute-start.4
  49.7 0.0 collective-permute-done.7.refs_2_
  49.7 3.5 %collective-permute-start.5 = (bf16[32,2048]{1,0:T(8,128)(2,1)S(1)}, bf16[32,2048]{1,0:T(8,128)(2,1)S(1)}, u32[]{:S(2)}, u32[]{:S(2)}) collective-permute-start(bf16[32,2048]{1,0:T(8,128)(2,1)S(1)} %get-tuple-element.26), channel_id=1, source_target_pairs={{0,14},{1,15},{2,12},{3,13},{4,10},{5,11},{6,8},{7,9},{8,6},{9,7},... | collective-permute-start | bytes 393224 | tf_op jit(solution)/shard_map/ppermute | solution.py:384
  53.2 5.9 %all-to-all-done = bf16[16,16,2048]{2,1,0:T(8,128)(2,1)} async-done(((bf16[16,16,2048]{2,1,0:T(8,128)(2,1)}), bf16[16,16,2048]{2,1,0:T(8,128)(2,1)}, u32[]{:S(2)}, u32[]{:S(2)}) %all-to-all-start) | async-done | bytes 1048608 | tf_op jit(solution)/shard_map/all_to_all | solution.py:357
  59.1 2.2 %shard_map.63.refs_6_ = bf16[2,256,2048]{2,1,0:T(8,128)(2,1)} custom-call(bf16[256,2048]{1,0:T(8,128)(2,1)} %bitcast.3.part_ref), custom_call_target="tpu_custom_call" | custom-call | tf_op jit(solution)/shard_map/pallas_call | solution.py:294
  61.3 0.0 collective-permute-done.8.refs_3_
  61.3 0.6 collective-permute-done.9.refs_4_
  61.9 2.8 %collective-permute-done.10.refs_5_ = bf16[32,2048]{1,0:T(8,128)(2,1)S(1)} collective-permute-done((bf16[32,2048]{1,0:T(8,128)(2,1)S(1)}, bf16[32,2048]{1,0:T(8,128)(2,1)S(1)}, u32[]{:S(2)}, u32[]{:S(2)}) %collective-permute-start.10) | collective-permute-done | bytes 131104 | tf_op jit(solution)/shard_map/ppermute | solution.py:384
  64.8 0.9 %shard_map.64.refs_2_ = bf16[2,256,2048]{2,1,0:T(8,128)(2,1)} custom-call(bf16[32,2048]{1,0:T(8,128)(2,1)S(1)} %get-tuple-element.27.refs_0_, bf16[32,2048]{1,0:T(8,128)(2,1)S(1)} %collective-permute-done.6.refs_1_, bf16[32,2048]{1,0:T(8,128)(2,1)S(1)} %collective-permute-done.7.refs_2_, ...), custom_call_target="tpu_custom_call", output_to_operand_aliasing={{}: (6, {})} | custom-call | tf_op jit(solution)/shard_map/pallas_call | solution.py:294
  65.7 3.8 %collective-permute-done.4.refs_0_ = bf16[32,2048]{1,0:T(8,128)(2,1)S(1)} collective-permute-done((bf16[32,2048]{1,0:T(8,128)(2,1)S(1)}, bf16[32,2048]{1,0:T(8,128)(2,1)S(1)}, u32[]{:S(2)}, u32[]{:S(2)}) %collective-permute-start.4) | collective-permute-done | bytes 131104 | tf_op jit(solution)/shard_map/ppermute | solution.py:384
  69.5 3.3 %collective-permute-done.5.refs_1_ = bf16[32,2048]{1,0:T(8,128)(2,1)S(1)} collective-permute-done((bf16[32,2048]{1,0:T(8,128)(2,1)S(1)}, bf16[32,2048]{1,0:T(8,128)(2,1)S(1)}, u32[]{:S(2)}, u32[]{:S(2)}) %collective-permute-start.5) | collective-permute-done | bytes 131104 | tf_op jit(solution)/shard_map/ppermute | solution.py:384
  72.8 0.8 %shard_map.65 = bf16[2,256,2048]{2,1,0:T(8,128)(2,1)} custom-call(bf16[32,2048]{1,0:T(8,128)(2,1)S(1)} %collective-permute-done.4.refs_0_, bf16[32,2048]{1,0:T(8,128)(2,1)S(1)} %collective-permute-done.5.refs_1_, bf16[2,256,2048]{2,1,0:T(8,128)(2,1)} %shard_map.64.refs_2_), custom_call_target="tpu_custom_call", output_to_operand_aliasing={{}: (2, {})} | custom-call | tf_op jit(solution)/shard_map/pallas_call | solution.py:294
  (4 shorter events, 0.1 us)
Async XLA Ops:
  0.6 11.0 %copy-start.2 = (f32[4,32,2048]{2,1,0:T(8,128)S(1)}, f32[4,32,2048]{2,1,0:T(8,128)}, u32[]{:S(2)}) copy-start(f32[4,32,2048]{2,1,0:T(8,128)} %r_ref.5) | copy-start | bytes 3145732
  0.6 11.0 %copy-start.1 = (f32[4,32,2048]{2,1,0:T(8,128)S(1)}, f32[4,32,2048]{2,1,0:T(8,128)}, u32[]{:S(2)}) copy-start(f32[4,32,2048]{2,1,0:T(8,128)} %k_ref.5) | copy-start | bytes 3145732
  0.7 11.0 %copy-start = (f32[4,32,2048]{2,1,0:T(8,128)S(1)}, f32[4,32,2048]{2,1,0:T(8,128)}, u32[]{:S(2)}) copy-start(f32[4,32,2048]{2,1,0:T(8,128)} %u_ref.5) | copy-start | bytes 3145732
  0.7 9.2 %copy-start.4 = (s32[2,128,1]{1,2,0:T(1,128)S(1)}, s32[2,128,1]{1,2,0:T(1,128)}, u32[]{:S(2)}) copy-start(s32[2,128,1]{1,2,0:T(1,128)} %param.7) | copy-start | bytes 3076
  3.3 7.6 %collective-permute-start.1 = (bf16[32,2048]{1,0:T(8,128)(2,1)}, bf16[32,2048]{1,0:T(8,128)(2,1)}, u32[]{:S(2)}, u32[]{:S(2)}) collective-permute-start(bf16[32,2048]{1,0:T(8,128)(2,1)} %get-tuple-element.19), channel_id=1, source_target_pairs={{1,2},{3,4},{5,6},{7,8},{9,10},{11,12},{13,14},{2,1},{4,3},{6,5},{... | collective-permute-start | bytes 393224 | tf_op jit(solution)/shard_map/ppermute | solution.py:360
  6.0 12.7 %collective-permute-start.2 = (bf16[48,2048]{1,0:T(8,128)(2,1)}, bf16[48,2048]{1,0:T(8,128)(2,1)}, u32[]{:S(2)}, u32[]{:S(2)}) collective-permute-start(bf16[48,2048]{1,0:T(8,128)(2,1)} %get-tuple-element.20), channel_id=1, source_target_pairs={{1,2},{3,4},{5,6},{7,8},{9,10},{11,12},{13,14},{2,1},{4,3},{6,5},{... | collective-permute-start | bytes 589832 | tf_op jit(solution)/shard_map/ppermute | solution.py:361
  9.8 1.9 %collective-permute-start = (bf16[80,2048]{1,0:T(8,128)(2,1)}, bf16[80,2048]{1,0:T(8,128)(2,1)S(1)}, u32[]{:S(2)}, u32[]{:S(2)}) collective-permute-start(bf16[80,2048]{1,0:T(8,128)(2,1)} %get-tuple-element.18), channel_id=1, source_target_pairs={{0,1},{1,0},{2,3},{3,2},{4,5},{5,4},{6,7},{7,6},{8,9},{9,8},{10,11... | collective-permute-start | bytes 983048 | tf_op jit(solution)/shard_map/ppermute | solution.py:360
  17.8 1.0 %copy-start.3 = (bf16[256,2048]{1,0:T(8,128)(2,1)}, bf16[256,2048]{1,0:T(8,128)(2,1)S(1)}, u32[]{:S(2)}) copy-start(bf16[256,2048]{1,0:T(8,128)(2,1)S(1)} %shard_map.60) | copy-start | bytes 3145732
  18.7 40.4 %all-to-all-start = ((bf16[16,16,2048]{2,1,0:T(8,128)(2,1)}), bf16[16,16,2048]{2,1,0:T(8,128)(2,1)}, u32[]{:S(2)}, u32[]{:S(2)}) async-start(bf16[16,16,2048]{2,1,0:T(8,128)(2,1)} %bitcast.10), calls=%async_computation | async-start | bytes 2097152 | tf_op jit(solution)/shard_map/all_to_all | solution.py:357
  36.4 1.9 %collective-permute-start.3 = (bf16[128,2048]{1,0:T(8,128)(2,1)S(1)}, bf16[128,2048]{1,0:T(8,128)(2,1)S(1)}, u32[]{:S(2)}, u32[]{:S(2)}) collective-permute-start(bf16[128,2048]{1,0:T(8,128)(2,1)S(1)} %get-tuple-element.24), channel_id=1, source_target_pairs={{0,1},{1,0},{2,3},{3,2},{4,5},{5,4},{6,7},{7,6},{8,9},{9,8},{10,11... | collective-permute-start | bytes 1572872 | tf_op jit(solution)/shard_map/ppermute | solution.py:376
  38.4 10.9 %collective-permute-start.6 = (bf16[32,2048]{1,0:T(8,128)(2,1)S(1)}, bf16[32,2048]{1,0:T(8,128)(2,1)S(1)}, u32[]{:S(2)}, u32[]{:S(2)}) collective-permute-start(bf16[32,2048]{1,0:T(8,128)(2,1)S(1)} %get-tuple-element.28), channel_id=1, source_target_pairs={{0,2},{1,3},{2,0},{3,1},{4,6},{5,7},{6,4},{7,5},{8,10},{9,11},{10,... | collective-permute-start | bytes 393224 | tf_op jit(solution)/shard_map/ppermute | solution.py:384
  39.9 9.8 %collective-permute-start.7 = (bf16[32,2048]{1,0:T(8,128)(2,1)S(1)}, bf16[32,2048]{1,0:T(8,128)(2,1)S(1)}, u32[]{:S(2)}, u32[]{:S(2)}) collective-permute-start(bf16[32,2048]{1,0:T(8,128)(2,1)S(1)} %get-tuple-element.29), channel_id=1, source_target_pairs={{0,4},{1,5},{2,6},{3,7},{4,0},{5,1},{6,2},{7,3},{8,12},{9,13},{10,... | collective-permute-start | bytes 393224 | tf_op jit(solution)/shard_map/ppermute | solution.py:384
  40.5 20.8 %collective-permute-start.8 = (bf16[32,2048]{1,0:T(8,128)(2,1)S(1)}, bf16[32,2048]{1,0:T(8,128)(2,1)S(1)}, u32[]{:S(2)}, u32[]{:S(2)}) collective-permute-start(bf16[32,2048]{1,0:T(8,128)(2,1)S(1)} %get-tuple-element.30), channel_id=1, source_target_pairs={{0,6},{1,7},{2,4},{3,5},{4,2},{5,3},{6,0},{7,1},{8,14},{9,15},{10,... | collective-permute-start | bytes 393224 | tf_op jit(solution)/shard_map/ppermute | solution.py:384
  42.0 20.0 %collective-permute-start.9 = (bf16[32,2048]{1,0:T(8,128)(2,1)S(1)}, bf16[32,2048]{1,0:T(8,128)(2,1)S(1)}, u32[]{:S(2)}, u32[]{:S(2)}) collective-permute-start(bf16[32,2048]{1,0:T(8,128)(2,1)S(1)} %get-tuple-element.31), channel_id=1, source_target_pairs={{0,8},{1,9},{2,10},{3,11},{4,12},{5,13},{6,14},{7,15},{8,0},{9,1},... | collective-permute-start | bytes 393224 | tf_op jit(solution)/shard_map/ppermute | solution.py:384
  44.3 20.4 %collective-permute-start.10 = (bf16[32,2048]{1,0:T(8,128)(2,1)S(1)}, bf16[32,2048]{1,0:T(8,128)(2,1)S(1)}, u32[]{:S(2)}, u32[]{:S(2)}) collective-permute-start(bf16[32,2048]{1,0:T(8,128)(2,1)S(1)} %get-tuple-element.32), channel_id=1, source_target_pairs={{0,10},{1,11},{2,8},{3,9},{4,14},{5,15},{6,12},{7,13},{8,2},{9,3},... | collective-permute-start | bytes 393224 | tf_op jit(solution)/shard_map/ppermute | solution.py:384
  49.3 20.2 %collective-permute-start.4 = (bf16[32,2048]{1,0:T(8,128)(2,1)S(1)}, bf16[32,2048]{1,0:T(8,128)(2,1)S(1)}, u32[]{:S(2)}, u32[]{:S(2)}) collective-permute-start(bf16[32,2048]{1,0:T(8,128)(2,1)S(1)} %get-tuple-element.25), channel_id=1, source_target_pairs={{0,12},{1,13},{2,14},{3,15},{4,8},{5,9},{6,10},{7,11},{8,4},{9,5},... | collective-permute-start | bytes 393224 | tf_op jit(solution)/shard_map/ppermute | solution.py:384
  49.7 23.0 %collective-permute-start.5 = (bf16[32,2048]{1,0:T(8,128)(2,1)S(1)}, bf16[32,2048]{1,0:T(8,128)(2,1)S(1)}, u32[]{:S(2)}, u32[]{:S(2)}) collective-permute-start(bf16[32,2048]{1,0:T(8,128)(2,1)S(1)} %get-tuple-element.26), channel_id=1, source_target_pairs={{0,14},{1,15},{2,12},{3,13},{4,10},{5,11},{6,8},{7,9},{8,6},{9,7},... | collective-permute-start | bytes 393224 | tf_op jit(solution)/shard_map/ppermute | solution.py:384

commit v6 on v5

--- a/solution.py
+++ b/solution.py
@@ -61,7 +61,7 @@
 def pack_faces(u, k, r):
     levels, _, cells = u.shape
     hbm = pl.BlockSpec(memory_space=pltpu.HBM)
-    sizes = [(2 * levels + 2) * TILE, levels * TILE, (levels + 2) * TILE]
+    sizes = [(2 * levels + 2) * TILE, levels * TILE, (levels + 1) * TILE]
     return pl.pallas_call(
         pack_kernel,
         out_shape=[jax.ShapeDtypeStruct((size, cells), jnp.bfloat16) for size in sizes],
@@ -179,7 +179,7 @@
 
 
 def sides(core, chip, even):
-    core, chip = core.astype(jnp.float32), chip.astype(jnp.float32)
+    core, chip = core.astype(jnp.float32)[: chip.shape[0]], chip.astype(jnp.float32)
     return jnp.where(even, core, chip), jnp.where(even, chip, core)
 
 

time: 74 us -> 74 us (level)
  no operation moved by 1% of the time
where the time goes in v6:
time: 74 us; the launch traced here: 73.7 us
  Pallas kernels  24.9 us (34%)
  starting transfers between devices  23.4 us (32%)
  waiting for transfers between devices  23.1 us (31%)
  local copies, waits for them, and re-layouts  0.98 us (1%)
  between operations  0.96 us (1%)
    pallas_call x2, Pallas kernels, advance(): pl.pallas_call(functools.partial(steps_kernel, steps), out_shape=out, in_...  18.3 us
    ppermute x7, waiting for transfers between devices, shards(): lax.ppermute(blocks[p], 'gx', [(i, i ^ 2 * p) for i in range(n)])  14 us
    ppermute x7, starting transfers between devices, shards(): lax.ppermute(blocks[p], 'gx', [(i, i ^ 2 * p) for i in range(n)])  11.3 us
    all_to_all x1, waiting for transfers between devices, route(): return lax.all_to_all(packed, 'gx', split_axis=0, concat_axis=0, tiled=True)  5.87 us
    all_to_all x1, starting transfers between devices, route(): return lax.all_to_all(packed, 'gx', split_axis=0, concat_axis=0, tiled=True)  5.4 us
    pallas_call x4, Pallas kernels, vmem_call(): pl.pallas_call(kernel, out_shape=out, in_specs=kw.pop('in_specs', [vmem]...  3.98 us
    ppermute x1, starting transfers between devices, shards(): deep = lax.ppermute(deep, 'gx', by_chip)  3.71 us
    ppermute x1, starting transfers between devices, shards(): lax.ppermute(to_chip, 'gx', by_chip)  2.75 us
  transfers between devices with their start and end apart: 12, of which 9 were waited for; matrix products, arithmetic and copies ran while one was open for 1% of the time, Pallas kernels for 29%

profile of v6, /device:TPU:10, one launch (start us, length us, event | category | flops | bytes accessed | tf_op | source)
XLA Modules:
  0.0 73.7 jit_solution(17209709678824772780)
XLA Ops:
  0.6 0.0 copy-start.2
  0.6 0.0 copy-start.1
  0.7 0.0 copy-start
  0.7 0.0 copy-start.4
  0.7 2.6 %shard_map.59 = (bf16[80,2048]{1,0:T(8,128)(2,1)}, bf16[32,2048]{1,0:T(8,128)(2,1)}, bf16[40,2048]{1,0:T(8,128)(2,1)}) custom-call(f32[4,32,2048]{2,1,0:T(8,128)} %u_ref.5, f32[4,32,2048]{2,1,0:T(8,128)} %k_ref.5, f32[4,32,2048]{2,1,0:T(8,128)} %r_ref.5), custom_call_target="tpu_custom_call" | custom-call | tf_op jit(solution)/shard_map/pallas_call | solution.py:65
  3.3 2.8 %collective-permute-start.1 = (bf16[32,2048]{1,0:T(8,128)(2,1)}, bf16[32,2048]{1,0:T(8,128)(2,1)}, u32[]{:S(2)}, u32[]{:S(2)}) collective-permute-start(bf16[32,2048]{1,0:T(8,128)(2,1)} %get-tuple-element.19), channel_id=1, source_target_pairs={{1,2},{3,4},{5,6},{7,8},{9,10},{11,12},{13,14},{2,1},{4,3},{6,5},{... | collective-permute-start | bytes 393224 | tf_op jit(solution)/shard_map/ppermute | solution.py:360
  6.0 3.7 %collective-permute-start.2 = (bf16[40,2048]{1,0:T(8,128)(2,1)}, bf16[40,2048]{1,0:T(8,128)(2,1)}, u32[]{:S(2)}, u32[]{:S(2)}) collective-permute-start(bf16[40,2048]{1,0:T(8,128)(2,1)} %get-tuple-element.20), channel_id=1, source_target_pairs={{1,2},{3,4},{5,6},{7,8},{9,10},{11,12},{13,14},{2,1},{4,3},{6,5},{... | collective-permute-start | bytes 491528 | tf_op jit(solution)/shard_map/ppermute | solution.py:361
  9.8 0.1 collective-permute-start
  9.8 0.0 copy-done.4
  9.9 0.2 fusion.1
  10.0 0.2 fusion
  10.2 0.6 collective-permute-done.1.chip_ref
  10.9 0.8 %collective-permute-done.core_ref = bf16[80,2048]{1,0:T(8,128)(2,1)S(1)} collective-permute-done((bf16[80,2048]{1,0:T(8,128)(2,1)}, bf16[80,2048]{1,0:T(8,128)(2,1)S(1)}, u32[]{:S(2)}, u32[]{:S(2)}) %collective-permute-start) | collective-permute-done | bytes 327712 | tf_op jit(solution)/shard_map/ppermute | solution.py:360
  11.7 0.0 copy-done.2
  11.7 0.0 copy-done.1
  11.7 0.0 copy-done
  11.7 6.1 %shard_map.60 = bf16[256,2048]{1,0:T(8,128)(2,1)S(1)} custom-call(f32[4,32,2048]{2,1,0:T(8,128)S(1)} %copy-done, f32[4,32,2048]{2,1,0:T(8,128)S(1)} %copy-done.1, f32[4,32,2048]{2,1,0:T(8,128)S(1)} %copy-done.2, bf16[80,2048]{1,0:T(8,128)(2,1)S(1)} %collective-permute-done.core_ref, bf16[32,2048]{1,0:T(8,128)(2,1)} %collective-permute-done.1.chip_ref, ...), custom_call_target="tpu_custom_call" | custom-call | flops 31457280 | bytes 5767168 | tf_op jit(solution)/shard_map/pallas_call | solution.py:276
  17.7 0.0 copy-start.3
  17.8 1.0 %copy-done.3 = bf16[256,2048]{1,0:T(8,128)(2,1)} copy-done((bf16[256,2048]{1,0:T(8,128)(2,1)}, bf16[256,2048]{1,0:T(8,128)(2,1)S(1)}, u32[]{:S(2)}) %copy-start.3) | copy-done | bytes 1048600
  18.7 0.0 collective-permute-done.2.refs_0_
  18.7 5.4 %all-to-all-start = ((bf16[16,16,2048]{2,1,0:T(8,128)(2,1)}), bf16[16,16,2048]{2,1,0:T(8,128)(2,1)}, u32[]{:S(2)}, u32[]{:S(2)}) async-start(bf16[16,16,2048]{2,1,0:T(8,128)(2,1)} %bitcast.10), calls=%async_computation | async-start | bytes 2097152 | tf_op jit(solution)/shard_map/all_to_all | solution.py:357
  24.1 12.3 %shard_map.61 = (f32[4,32,2048]{2,1,0:T(8,128)}, bf16[128,2048]{1,0:T(8,128)(2,1)S(1)}, bf16[128,2048]{1,0:T(8,128)(2,1)S(1)}) custom-call(f32[4,32,2048]{2,1,0:T(8,128)S(1)} %copy-done, f32[4,32,2048]{2,1,0:T(8,128)S(1)} %copy-done.1, f32[4,32,2048]{2,1,0:T(8,128)S(1)} %copy-done.2, bf16[80,2048]{1,0:T(8,128)(2,1)S(1)} %collective-permute-done.core_ref, ...), custom_call_target="tpu_custom_call" | custom-call | flops 62914560 | bytes 5767168 | tf_op jit(solution)/shard_map/pallas_call | solution.py:276
  36.4 0.2 collective-permute-start.3
  36.5 1.8 %collective-permute-done.3.theirs_ref = bf16[128,2048]{1,0:T(8,128)(2,1)S(1)} collective-permute-done((bf16[128,2048]{1,0:T(8,128)(2,1)S(1)}, bf16[128,2048]{1,0:T(8,128)(2,1)S(1)}, u32[]{:S(2)}, u32[]{:S(2)}) %collective-permute-start.3) | collective-permute-done | bytes 524320 | tf_op jit(solution)/shard_map/ppermute | solution.py:376
  38.3 0.1 shard_map.62
  38.4 1.5 %collective-permute-start.6 = (bf16[32,2048]{1,0:T(8,128)(2,1)S(1)}, bf16[32,2048]{1,0:T(8,128)(2,1)S(1)}, u32[]{:S(2)}, u32[]{:S(2)}) collective-permute-start(bf16[32,2048]{1,0:T(8,128)(2,1)S(1)} %get-tuple-element.28), channel_id=1, source_target_pairs={{0,2},{1,3},{2,0},{3,1},{4,6},{5,7},{6,4},{7,5},{8,10},{9,11},{10,... | collective-permute-start | bytes 393224 | tf_op jit(solution)/shard_map/ppermute | solution.py:384
  39.9 0.6 collective-permute-start.7
  40.5 1.5 %collective-permute-start.8 = (bf16[32,2048]{1,0:T(8,128)(2,1)S(1)}, bf16[32,2048]{1,0:T(8,128)(2,1)S(1)}, u32[]{:S(2)}, u32[]{:S(2)}) collective-permute-start(bf16[32,2048]{1,0:T(8,128)(2,1)S(1)} %get-tuple-element.30), channel_id=1, source_target_pairs={{0,6},{1,7},{2,4},{3,5},{4,2},{5,3},{6,0},{7,1},{8,14},{9,15},{10,... | collective-permute-start | bytes 393224 | tf_op jit(solution)/shard_map/ppermute | solution.py:384
  41.9 2.4 %collective-permute-start.9 = (bf16[32,2048]{1,0:T(8,128)(2,1)S(1)}, bf16[32,2048]{1,0:T(8,128)(2,1)S(1)}, u32[]{:S(2)}, u32[]{:S(2)}) collective-permute-start(bf16[32,2048]{1,0:T(8,128)(2,1)S(1)} %get-tuple-element.31), channel_id=1, source_target_pairs={{0,8},{1,9},{2,10},{3,11},{4,12},{5,13},{6,14},{7,15},{8,0},{9,1},... | collective-permute-start | bytes 393224 | tf_op jit(solution)/shard_map/ppermute | solution.py:384
  44.3 1.5 %collective-permute-start.10 = (bf16[32,2048]{1,0:T(8,128)(2,1)S(1)}, bf16[32,2048]{1,0:T(8,128)(2,1)S(1)}, u32[]{:S(2)}, u32[]{:S(2)}) collective-permute-start(bf16[32,2048]{1,0:T(8,128)(2,1)S(1)} %get-tuple-element.32), channel_id=1, source_target_pairs={{0,10},{1,11},{2,8},{3,9},{4,14},{5,15},{6,12},{7,13},{8,2},{9,3},... | collective-permute-start | bytes 393224 | tf_op jit(solution)/shard_map/ppermute | solution.py:384
  45.8 3.5 %collective-permute-done.6.refs_1_ = bf16[32,2048]{1,0:T(8,128)(2,1)S(1)} collective-permute-done((bf16[32,2048]{1,0:T(8,128)(2,1)S(1)}, bf16[32,2048]{1,0:T(8,128)(2,1)S(1)}, u32[]{:S(2)}, u32[]{:S(2)}) %collective-permute-start.6) | collective-permute-done | bytes 131104 | tf_op jit(solution)/shard_map/ppermute | solution.py:384
  49.3 0.3 collective-permute-start.4
  49.6 0.0 collective-permute-done.7.refs_2_
  49.6 3.6 %collective-permute-start.5 = (bf16[32,2048]{1,0:T(8,128)(2,1)S(1)}, bf16[32,2048]{1,0:T(8,128)(2,1)S(1)}, u32[]{:S(2)}, u32[]{:S(2)}) collective-permute-start(bf16[32,2048]{1,0:T(8,128)(2,1)S(1)} %get-tuple-element.26), channel_id=1, source_target_pairs={{0,14},{1,15},{2,12},{3,13},{4,10},{5,11},{6,8},{7,9},{8,6},{9,7},... | collective-permute-start | bytes 393224 | tf_op jit(solution)/shard_map/ppermute | solution.py:384
  53.2 5.9 %all-to-all-done = bf16[16,16,2048]{2,1,0:T(8,128)(2,1)} async-done(((bf16[16,16,2048]{2,1,0:T(8,128)(2,1)}), bf16[16,16,2048]{2,1,0:T(8,128)(2,1)}, u32[]{:S(2)}, u32[]{:S(2)}) %all-to-all-start) | async-done | bytes 1048608 | tf_op jit(solution)/shard_map/all_to_all | solution.py:357
  59.1 2.2 %shard_map.63.refs_6_ = bf16[2,256,2048]{2,1,0:T(8,128)(2,1)} custom-call(bf16[256,2048]{1,0:T(8,128)(2,1)} %bitcast.3.part_ref), custom_call_target="tpu_custom_call" | custom-call | tf_op jit(solution)/shard_map/pallas_call | solution.py:294
  61.3 0.0 collective-permute-done.8.refs_3_
  61.3 0.6 collective-permute-done.9.refs_4_
  61.9 2.8 %collective-permute-done.10.refs_5_ = bf16[32,2048]{1,0:T(8,128)(2,1)S(1)} collective-permute-done((bf16[32,2048]{1,0:T(8,128)(2,1)S(1)}, bf16[32,2048]{1,0:T(8,128)(2,1)S(1)}, u32[]{:S(2)}, u32[]{:S(2)}) %collective-permute-start.10) | collective-permute-done | bytes 131104 | tf_op jit(solution)/shard_map/ppermute | solution.py:384
  64.8 0.9 %shard_map.64.refs_2_ = bf16[2,256,2048]{2,1,0:T(8,128)(2,1)} custom-call(bf16[32,2048]{1,0:T(8,128)(2,1)S(1)} %get-tuple-element.27.refs_0_, bf16[32,2048]{1,0:T(8,128)(2,1)S(1)} %collective-permute-done.6.refs_1_, bf16[32,2048]{1,0:T(8,128)(2,1)S(1)} %collective-permute-done.7.refs_2_, ...), custom_call_target="tpu_custom_call", output_to_operand_aliasing={{}: (6, {})} | custom-call | tf_op jit(solution)/shard_map/pallas_call | solution.py:294
  65.7 3.8 %collective-permute-done.4.refs_0_ = bf16[32,2048]{1,0:T(8,128)(2,1)S(1)} collective-permute-done((bf16[32,2048]{1,0:T(8,128)(2,1)S(1)}, bf16[32,2048]{1,0:T(8,128)(2,1)S(1)}, u32[]{:S(2)}, u32[]{:S(2)}) %collective-permute-start.4) | collective-permute-done | bytes 131104 | tf_op jit(solution)/shard_map/ppermute | solution.py:384
  69.5 3.3 %collective-permute-done.5.refs_1_ = bf16[32,2048]{1,0:T(8,128)(2,1)S(1)} collective-permute-done((bf16[32,2048]{1,0:T(8,128)(2,1)S(1)}, bf16[32,2048]{1,0:T(8,128)(2,1)S(1)}, u32[]{:S(2)}, u32[]{:S(2)}) %collective-permute-start.5) | collective-permute-done | bytes 131104 | tf_op jit(solution)/shard_map/ppermute | solution.py:384
  72.7 0.8 %shard_map.65 = bf16[2,256,2048]{2,1,0:T(8,128)(2,1)} custom-call(bf16[32,2048]{1,0:T(8,128)(2,1)S(1)} %collective-permute-done.4.refs_0_, bf16[32,2048]{1,0:T(8,128)(2,1)S(1)} %collective-permute-done.5.refs_1_, bf16[2,256,2048]{2,1,0:T(8,128)(2,1)} %shard_map.64.refs_2_), custom_call_target="tpu_custom_call", output_to_operand_aliasing={{}: (2, {})} | custom-call | tf_op jit(solution)/shard_map/pallas_call | solution.py:294
  (4 shorter events, 0.1 us)
Async XLA Ops:
  0.6 11.0 %copy-start.2 = (f32[4,32,2048]{2,1,0:T(8,128)S(1)}, f32[4,32,2048]{2,1,0:T(8,128)}, u32[]{:S(2)}) copy-start(f32[4,32,2048]{2,1,0:T(8,128)} %r_ref.5) | copy-start | bytes 3145732
  0.6 11.0 %copy-start.1 = (f32[4,32,2048]{2,1,0:T(8,128)S(1)}, f32[4,32,2048]{2,1,0:T(8,128)}, u32[]{:S(2)}) copy-start(f32[4,32,2048]{2,1,0:T(8,128)} %k_ref.5) | copy-start | bytes 3145732
  0.7 11.0 %copy-start = (f32[4,32,2048]{2,1,0:T(8,128)S(1)}, f32[4,32,2048]{2,1,0:T(8,128)}, u32[]{:S(2)}) copy-start(f32[4,32,2048]{2,1,0:T(8,128)} %u_ref.5) | copy-start | bytes 3145732
  0.7 9.2 %copy-start.4 = (s32[2,128,1]{1,2,0:T(1,128)S(1)}, s32[2,128,1]{1,2,0:T(1,128)}, u32[]{:S(2)}) copy-start(s32[2,128,1]{1,2,0:T(1,128)} %param.7) | copy-start | bytes 3076
  3.3 7.6 %collective-permute-start.1 = (bf16[32,2048]{1,0:T(8,128)(2,1)}, bf16[32,2048]{1,0:T(8,128)(2,1)}, u32[]{:S(2)}, u32[]{:S(2)}) collective-permute-start(bf16[32,2048]{1,0:T(8,128)(2,1)} %get-tuple-element.19), channel_id=1, source_target_pairs={{1,2},{3,4},{5,6},{7,8},{9,10},{11,12},{13,14},{2,1},{4,3},{6,5},{... | collective-permute-start | bytes 393224 | tf_op jit(solution)/shard_map/ppermute | solution.py:360
  6.0 12.7 %collective-permute-start.2 = (bf16[40,2048]{1,0:T(8,128)(2,1)}, bf16[40,2048]{1,0:T(8,128)(2,1)}, u32[]{:S(2)}, u32[]{:S(2)}) collective-permute-start(bf16[40,2048]{1,0:T(8,128)(2,1)} %get-tuple-element.20), channel_id=1, source_target_pairs={{1,2},{3,4},{5,6},{7,8},{9,10},{11,12},{13,14},{2,1},{4,3},{6,5},{... | collective-permute-start | bytes 491528 | tf_op jit(solution)/shard_map/ppermute | solution.py:361
  9.8 1.9 %collective-permute-start = (bf16[80,2048]{1,0:T(8,128)(2,1)}, bf16[80,2048]{1,0:T(8,128)(2,1)S(1)}, u32[]{:S(2)}, u32[]{:S(2)}) collective-permute-start(bf16[80,2048]{1,0:T(8,128)(2,1)} %get-tuple-element.18), channel_id=1, source_target_pairs={{0,1},{1,0},{2,3},{3,2},{4,5},{5,4},{6,7},{7,6},{8,9},{9,8},{10,11... | collective-permute-start | bytes 983048 | tf_op jit(solution)/shard_map/ppermute | solution.py:360
  17.7 1.0 %copy-start.3 = (bf16[256,2048]{1,0:T(8,128)(2,1)}, bf16[256,2048]{1,0:T(8,128)(2,1)S(1)}, u32[]{:S(2)}) copy-start(bf16[256,2048]{1,0:T(8,128)(2,1)S(1)} %shard_map.60) | copy-start | bytes 3145732
  18.7 40.4 %all-to-all-start = ((bf16[16,16,2048]{2,1,0:T(8,128)(2,1)}), bf16[16,16,2048]{2,1,0:T(8,128)(2,1)}, u32[]{:S(2)}, u32[]{:S(2)}) async-start(bf16[16,16,2048]{2,1,0:T(8,128)(2,1)} %bitcast.10), calls=%async_computation | async-start | bytes 2097152 | tf_op jit(solution)/shard_map/all_to_all | solution.py:357
  36.4 1.9 %collective-permute-start.3 = (bf16[128,2048]{1,0:T(8,128)(2,1)S(1)}, bf16[128,2048]{1,0:T(8,128)(2,1)S(1)}, u32[]{:S(2)}, u32[]{:S(2)}) collective-permute-start(bf16[128,2048]{1,0:T(8,128)(2,1)S(1)} %get-tuple-element.24), channel_id=1, source_target_pairs={{0,1},{1,0},{2,3},{3,2},{4,5},{5,4},{6,7},{7,6},{8,9},{9,8},{10,11... | collective-permute-start | bytes 1572872 | tf_op jit(solution)/shard_map/ppermute | solution.py:376
  38.4 10.9 %collective-permute-start.6 = (bf16[32,2048]{1,0:T(8,128)(2,1)S(1)}, bf16[32,2048]{1,0:T(8,128)(2,1)S(1)}, u32[]{:S(2)}, u32[]{:S(2)}) collective-permute-start(bf16[32,2048]{1,0:T(8,128)(2,1)S(1)} %get-tuple-element.28), channel_id=1, source_target_pairs={{0,2},{1,3},{2,0},{3,1},{4,6},{5,7},{6,4},{7,5},{8,10},{9,11},{10,... | collective-permute-start | bytes 393224 | tf_op jit(solution)/shard_map/ppermute | solution.py:384
  39.9 9.7 %collective-permute-start.7 = (bf16[32,2048]{1,0:T(8,128)(2,1)S(1)}, bf16[32,2048]{1,0:T(8,128)(2,1)S(1)}, u32[]{:S(2)}, u32[]{:S(2)}) collective-permute-start(bf16[32,2048]{1,0:T(8,128)(2,1)S(1)} %get-tuple-element.29), channel_id=1, source_target_pairs={{0,4},{1,5},{2,6},{3,7},{4,0},{5,1},{6,2},{7,3},{8,12},{9,13},{10,... | collective-permute-start | bytes 393224 | tf_op jit(solution)/shard_map/ppermute | solution.py:384
  40.5 20.8 %collective-permute-start.8 = (bf16[32,2048]{1,0:T(8,128)(2,1)S(1)}, bf16[32,2048]{1,0:T(8,128)(2,1)S(1)}, u32[]{:S(2)}, u32[]{:S(2)}) collective-permute-start(bf16[32,2048]{1,0:T(8,128)(2,1)S(1)} %get-tuple-element.30), channel_id=1, source_target_pairs={{0,6},{1,7},{2,4},{3,5},{4,2},{5,3},{6,0},{7,1},{8,14},{9,15},{10,... | collective-permute-start | bytes 393224 | tf_op jit(solution)/shard_map/ppermute | solution.py:384
  41.9 20.0 %collective-permute-start.9 = (bf16[32,2048]{1,0:T(8,128)(2,1)S(1)}, bf16[32,2048]{1,0:T(8,128)(2,1)S(1)}, u32[]{:S(2)}, u32[]{:S(2)}) collective-permute-start(bf16[32,2048]{1,0:T(8,128)(2,1)S(1)} %get-tuple-element.31), channel_id=1, source_target_pairs={{0,8},{1,9},{2,10},{3,11},{4,12},{5,13},{6,14},{7,15},{8,0},{9,1},... | collective-permute-start | bytes 393224 | tf_op jit(solution)/shard_map/ppermute | solution.py:384
  44.3 20.4 %collective-permute-start.10 = (bf16[32,2048]{1,0:T(8,128)(2,1)S(1)}, bf16[32,2048]{1,0:T(8,128)(2,1)S(1)}, u32[]{:S(2)}, u32[]{:S(2)}) collective-permute-start(bf16[32,2048]{1,0:T(8,128)(2,1)S(1)} %get-tuple-element.32), channel_id=1, source_target_pairs={{0,10},{1,11},{2,8},{3,9},{4,14},{5,15},{6,12},{7,13},{8,2},{9,3},... | collective-permute-start | bytes 393224 | tf_op jit(solution)/shard_map/ppermute | solution.py:384
  49.3 20.2 %collective-permute-start.4 = (bf16[32,2048]{1,0:T(8,128)(2,1)S(1)}, bf16[32,2048]{1,0:T(8,128)(2,1)S(1)}, u32[]{:S(2)}, u32[]{:S(2)}) collective-permute-start(bf16[32,2048]{1,0:T(8,128)(2,1)S(1)} %get-tuple-element.25), channel_id=1, source_target_pairs={{0,12},{1,13},{2,14},{3,15},{4,8},{5,9},{6,10},{7,11},{8,4},{9,5},... | collective-permute-start | bytes 393224 | tf_op jit(solution)/shard_map/ppermute | solution.py:384
  49.6 23.1 %collective-permute-start.5 = (bf16[32,2048]{1,0:T(8,128)(2,1)S(1)}, bf16[32,2048]{1,0:T(8,128)(2,1)S(1)}, u32[]{:S(2)}, u32[]{:S(2)}) collective-permute-start(bf16[32,2048]{1,0:T(8,128)(2,1)S(1)} %get-tuple-element.26), channel_id=1, source_target_pairs={{0,14},{1,15},{2,12},{3,13},{4,10},{5,11},{6,8},{7,9},{8,6},{9,7},... | collective-permute-start | bytes 393224 | tf_op jit(solution)/shard_map/ppermute | solution.py:384
